TPU v7x, 128 devices: a whole 4x4x4 slice. The times are simulated.
128 devices in a mesh: inst: 16 (over y, x_lo, core), tp: 8 (over x_hi, z).
Axes of the slice: x: 4 (x_hi: 2, x_lo: 2; x = x_hi * 2 + x_lo), y: 4, z: 4, core: 2. Of those that a mesh axis runs over, the one named last changes fastest.
Arguments:
- old_cache: bfloat16 [16384, 64, 256], P(('inst', 'tp')), may hold values from -6 to 6
- old_weight: bfloat16 [8192, 4096], P('tp'), may hold values from -4 to 4
- plan_src: int32 [128, 128], P(('inst', 'tp')), may hold values from 0 to 127, as said below
- plan_page: int32 [128, 128], P(('inst', 'tp')), may hold values from 0 to 127
- lengths: int32 [16, 2, 1], P('inst'), may hold values from 512 to 4096
- queries: bfloat16 [128, 4, 2048], P(('inst', 'tp')), may hold values from -100 to 100
- new_kv: bfloat16 [128, 4, 512], P(('inst', 'tp')), may hold values from -100 to 100
Outputs:
- layer_out: bfloat16 [128, 4, 4096], P(('inst', 'tp'))
- moved_cache: bfloat16 [16384, 64, 256], P(('inst', 'tp'))
Inputs may be any that keep to these rules, and one draw needn't show every extreme that they name: `plan_src`: in every row at most 2 slots name the same source device, and some source is named by exactly 2 slots of that row.
All inputs are finite; a program needn't handle non-finite values.
Results may differ from a plain program's by a relative error of at most 0.011.
Values may be sent and summed in bfloat16 or wider, within the bound.
No kernel may reach another device: no remote copies, remote signals or barrier semaphores. Data moves between devices by JAX's collectives and lax.ppermute only.
A program may use at most 128 MiB of HBM per device.

v0:
```python
import jax
import jax.numpy as jnp
from jax import lax
from jax.sharding import PartitionSpec as P


def swapped(value, axis, distance):
    return lax.ppermute(value, axis, [(i, i ^ 1 << distance) for i in range(lax.axis_size(axis))])


def attend(cache, queries, new_kv, lengths_own):
    requests, steps, q_width = queries.shape
    kv_local = cache.shape[1]
    head = cache.shape[3] // 2
    groups = q_width // (kv_local * head)
    query_rows = queries.reshape(requests, steps, kv_local, groups, head)
    key_rows = cache[..., :head]
    value_rows = cache[..., head:]
    fresh_rows = new_kv.reshape(requests, steps, kv_local, 2 * head)
    fresh_keys = fresh_rows[..., :head]
    fresh_values = fresh_rows[..., head:]
    score_scale = head ** (-0.5)
    cache_scores = (
        jnp.einsum("rtkgd,rkld->rkgtl", query_rows, key_rows, preferred_element_type=jnp.float32)
        * score_scale
    )
    positions = jnp.arange(cache.shape[2], dtype=jnp.int32)
    visible = positions[None, :] < lengths_own[:, None]
    cache_scores = jnp.where(visible[:, None, None, None, :], cache_scores, jnp.float32(-1e30))
    fresh_scores = (
        jnp.einsum("rtkgd,rukd->rkgtu", query_rows, fresh_keys, preferred_element_type=jnp.float32)
        * score_scale
    )
    causal = jnp.arange(steps)[:, None] >= jnp.arange(steps)[None, :]
    fresh_scores = jnp.where(causal, fresh_scores, jnp.float32(-1e30))
    highest = jnp.maximum(jnp.max(cache_scores, axis=-1), jnp.max(fresh_scores, axis=-1))
    cache_exp = jnp.exp(cache_scores - highest[..., None])
    fresh_exp = jnp.exp(fresh_scores - highest[..., None])
    summed = jnp.sum(cache_exp, axis=-1) + jnp.sum(fresh_exp, axis=-1)
    cache_prob = (cache_exp / summed[..., None]).astype(jnp.bfloat16)
    fresh_prob = (fresh_exp / summed[..., None]).astype(jnp.bfloat16)
    mixed = jnp.einsum(
        "rkgtl,rkld->rtkgd", cache_prob, value_rows, preferred_element_type=jnp.float32
    )
    mixed = mixed + jnp.einsum(
        "rkgtu,rukd->rtkgd", fresh_prob, fresh_values, preferred_element_type=jnp.float32
    )
    return mixed.reshape(requests * steps, q_width).astype(jnp.bfloat16)


def on_device(old_cache, old_weight, plan_src, plan_page, lengths, queries, new_kv):
    count_all = lax.axis_size("inst") * lax.axis_size("tp")
    myself = lax.axis_index("inst") * lax.axis_size("tp") + lax.axis_index("tp")
    all_sources, all_pages = (
        lax.all_gather(plan_src, ("inst", "tp"), axis=0, tiled=True),
        lax.all_gather(plan_page, ("inst", "tp"), axis=0, tiled=True),
    )
    page_count = plan_src.shape[1]
    capacity = 2 * page_count // count_all
    chosen = (all_sources == myself).astype(jnp.int32)
    ranking = jnp.cumsum(chosen, axis=1) - 1
    onehot = chosen[:, :, None] * (
        ranking[:, :, None] == jnp.arange(capacity, dtype=jnp.int32)[None, None, :]
    ).astype(jnp.int32)
    picked = jnp.sum(onehot * all_pages[:, :, None], axis=1)
    filled = jnp.sum(onehot, axis=1)
    outgoing = old_cache[picked] * filled[:, :, None, None].astype(old_cache.dtype)
    arrived = lax.all_to_all(outgoing, ("inst", "tp"), split_axis=0, concat_axis=0, tiled=True)
    arrived = arrived.reshape((count_all * capacity,) + old_cache.shape[1:])
    own_sources = plan_src[0]
    matches = own_sources[:, None] == own_sources[None, :]
    earlier = jnp.arange(page_count)[None, :] < jnp.arange(page_count)[:, None]
    slot_rank = jnp.sum((matches & earlier).astype(jnp.int32), axis=1)
    moved_pages = arrived[own_sources * capacity + slot_rank]
    requests, steps, q_width = queries.shape
    kv_local = new_kv.shape[2] // old_cache.shape[2]
    cache = moved_pages.reshape(
        requests,
        kv_local,
        page_count * old_cache.shape[1] // (requests * kv_local),
        old_cache.shape[2],
    )
    group_index = lax.axis_index("tp") % 2
    even_side = group_index == 0
    lengths_own = lax.dynamic_index_in_dim(lengths[0], group_index, 0, keepdims=False)
    mixed = attend(cache, queries, new_kv, lengths_own)
    half_width = q_width // 2
    partner = swapped(old_weight, "tp", 0)
    first_rows = jnp.where(even_side, old_weight, partner)
    second_rows = jnp.where(even_side, partner, old_weight)
    partial_value = jnp.dot(mixed[:, :half_width], first_rows, preferred_element_type=jnp.float32)
    partial_value = partial_value + jnp.dot(
        mixed[:, half_width:], second_rows, preferred_element_type=jnp.float32
    )
    holder = partial_value[None]
    first_bit = 1
    slot_pick = 0
    summed = holder
    for bit_index in range(first_bit, lax.axis_size("tp").bit_length() - 1):
        summed = summed + swapped(summed.astype(jnp.bfloat16), "tp", bit_index).astype(summed.dtype)
    result = lax.dynamic_index_in_dim(summed, slot_pick, 0, keepdims=False)
    layer_out = result.reshape(requests, steps, -1).astype(jnp.bfloat16)
    return (layer_out, moved_pages)


def solution(mesh):
    placed = (
        P(("inst", "tp"), None, None),
        P("tp", None),
        P(("inst", "tp"), None),
        P(("inst", "tp"), None),
        P("inst", None, None),
        P(("inst", "tp"), None, None),
        P(("inst", "tp"), None, None),
    )
    return jax.shard_map(
        on_device,
        mesh=mesh,
        in_specs=placed,
        out_specs=(P(("inst", "tp"), None, None), P(("inst", "tp"), None, None)),
        check_vma=False,
    )
```

profile of v0, /device:TPU:24, one launch (start us, length us, event | category | flops | bytes accessed | tf_op | source)
XLA Modules:
  0.0 950.1 jit_solution(1786047523505354544)
XLA Ops:
  0.6 277.8 %all-gather = s32[128,1,128]{2,1,0:T(1,128)S(1)} all-gather(s32[1,1,128]{2,1,0:T(1,128)} %bitcast.110), channel_id=1, replica_groups=mesh['inst'=16,'tp'=8] {'inst','tp'}, dimensions={0}, use_global_device_ids=true | all-gather | bytes 66048 | tf_op jit(solution)/shard_map/all_gather | solution.py:55
  278.6 0.2 reduce_window_sum.11
  278.9 278.3 %all-gather.1 = s32[128,1,128]{2,1,0:T(1,128)S(1)} all-gather(s32[1,1,128]{2,1,0:T(1,128)} %bitcast.109), channel_id=1, replica_groups=mesh['inst'=16,'tp'=8] {'inst','tp'}, dimensions={0}, use_global_device_ids=true | all-gather | bytes 66048 | tf_op jit(solution)/shard_map/all_gather | solution.py:56
  557.8 10.7 %gather_fusion = bf16[256,64,256]{2,1,0:T(8,128)(2,1)} fusion(bf16[128,64,256]{2,1,0:T(8,128)(2,1)} %param.7, s32[1024]{0:T(1024)S(1)} %pad_clamp_fusion.1), kind=kCustom, calls=%fused_computation | custom fusion | bytes 16778240 | tf_op jit(solution)/shard_map/gather | solution.py:67
  568.4 7.2 broadcast_multiply_fusion
  575.7 74.3 %all-to-all-start = ((bf16[128,2,64,256]{3,2,1,0:T(8,128)(2,1)}), bf16[128,2,64,256]{3,2,1,0:T(8,128)(2,1)}, u32[]{:S(2)}, u32[]{:S(2)}) async-start(bf16[128,2,64,256]{3,2,1,0:T(8,128)(2,1)} %broadcast_multiply_fusion), calls=%async_computation | async-start | bytes 16777216 | tf_op jit(solution)/shard_map/all_to_all | solution.py:68
  650.0 1.8 collective-permute-start
  651.8 0.6 constant_dynamic-slice_fusion
  652.4 0.7 iota_compare_fusion.2
  653.3 0.2 fusion.33
  653.5 102.3 %all-to-all-done = bf16[128,2,64,256]{3,2,1,0:T(8,128)(2,1)} async-done(((bf16[128,2,64,256]{3,2,1,0:T(8,128)(2,1)}), bf16[128,2,64,256]{3,2,1,0:T(8,128)(2,1)}, u32[]{:S(2)}, u32[]{:S(2)}) %all-to-all-start) | async-done | bytes 8388640 | tf_op jit(solution)/shard_map/all_to_all | solution.py:68
  755.8 6.2 gather_fusion.1
  762.0 2.5 fusion.32
  764.5 0.3 fusion.18
  764.9 2.1 fusion.12
  766.9 0.2 fusion.15
  767.2 161.9 %collective-permute-done = bf16[1024,4096]{1,0:T(8,128)(2,1)} collective-permute-done((bf16[1024,4096]{1,0:T(8,128)(2,1)}, bf16[1024,4096]{1,0:T(8,128)(2,1)}, u32[]{:S(2)}, u32[]{:S(2)}) %collective-permute-start) | collective-permute-done | bytes 8388640 | tf_op jit(solution)/shard_map/ppermute | solution.py:8
  929.1 4.8 fusion
  933.8 4.6 fusion.9
  938.5 1.7 collective-permute-start.1
  940.1 3.8 collective-permute-done.1
  944.0 1.7 collective-permute-start.2
  945.7 3.8 collective-permute-done.2
  949.5 0.6 add_convert_fusion
  (30 shorter events, 1.1 us)
Async XLA Ops:
  0.6 651.2 %copy-start = (s32[1,2,1]{1,2,0:T(1,128)S(1)}, s32[1,2,1]{1,2,0:T(1,128)}, u32[]{:S(2)}) copy-start(s32[1,2,1]{1,2,0:T(1,128)} %param.11) | copy-start | bytes 28
  575.7 77.4 %copy-start.2 = (s32[1,128]{1,0:T(1,128)S(1)}, s32[1,128]{1,0:T(1,128)}, u32[]{:S(2)}) copy-start(s32[1,128]{1,0:T(1,128)} %param.9) | copy-start | bytes 1540
  575.7 77.6 %copy-start.1 = (bf16[1,4,2048]{2,1,0:T(4,128)(2,1)S(1)}, bf16[1,4,2048]{2,1,0:T(4,128)(2,1)}, u32[]{:S(2)}) copy-start(bf16[1,4,2048]{2,1,0:T(4,128)(2,1)} %param.12) | copy-start | bytes 49156
  575.7 77.6 %copy-start.3 = (bf16[1,4,512]{2,1,0:T(4,128)(2,1)S(1)}, bf16[1,4,512]{2,1,0:T(4,128)(2,1)}, u32[]{:S(2)}) copy-start(bf16[1,4,512]{2,1,0:T(4,128)(2,1)} %param.13) | copy-start | bytes 12292
  575.7 180.1 %all-to-all-start = ((bf16[128,2,64,256]{3,2,1,0:T(8,128)(2,1)}), bf16[128,2,64,256]{3,2,1,0:T(8,128)(2,1)}, u32[]{:S(2)}, u32[]{:S(2)}) async-start(bf16[128,2,64,256]{3,2,1,0:T(8,128)(2,1)} %broadcast_multiply_fusion), calls=%async_computation | async-start | bytes 16777216 | tf_op jit(solution)/shard_map/all_to_all | solution.py:68
  650.0 279.0 %collective-permute-start = (bf16[1024,4096]{1,0:T(8,128)(2,1)}, bf16[1024,4096]{1,0:T(8,128)(2,1)}, u32[]{:S(2)}, u32[]{:S(2)}) collective-permute-start(bf16[1024,4096]{1,0:T(8,128)(2,1)} %param.8), channel_id=1, source_target_pairs={{0,1},{1,0},{2,3},{3,2},{4,5},{5,4},{6,7},{7,6},{8,9},{9,8},{10,11... | collective-permute-start | bytes 25165832 | tf_op jit(solution)/shard_map/ppermute | solution.py:8
  938.5 5.5 collective-permute-start.1
  944.0 5.5 collective-permute-start.2
where the time goes:
time: 955 us; the launch traced here: 950 us
  blocking collectives  556 us (58%)
  waiting for transfers between devices  272 us (28%)
  starting transfers between devices  79.6 us (8%)
  local copies, waits for them, and re-layouts  18.1 us (2%)
  matrix products  14.4 us (2%)
    all_gather x1, blocking collectives, on_device(): lax.all_gather(plan_page, ('inst', 'tp'), axis=0, tiled=True)  278 us
    all_gather x1, blocking collectives, on_device(): lax.all_gather(plan_src, ('inst', 'tp'), axis=0, tiled=True)  278 us
    ppermute x3, waiting for transfers between devices, swapped(): lax.ppermute(value, axis, [(i, i ^ 1 << distance) for i in range(lax.axis...  169 us
    all_to_all x1, waiting for transfers between devices, on_device(): lax.all_to_all(outgoing, ('inst', 'tp'), split_axis=0, concat_axis=0, til...  102 us
    all_to_all x1, starting transfers between devices, on_device(): lax.all_to_all(outgoing, ('inst', 'tp'), split_axis=0, concat_axis=0, til...  74.3 us
  transfers between devices with their start and end apart: 4, of which 4 were waited for; matrix products, arithmetic and copies ran while one was open for 1% of the time, Pallas kernels for 0%

commit v1 on v0

v1 whole, which is shorter than its diff:
```python
import functools

import jax
import jax.numpy as jnp
from jax import lax
from jax.experimental import pallas as pl
from jax.experimental.pallas import tpu as pltpu
from jax.sharding import PartitionSpec as P

BOTH = ("inst", "tp")
ANY = pl.BlockSpec(memory_space=pl.ANY)
VMEM = pl.BlockSpec(memory_space=pltpu.VMEM)
SMEM = pl.BlockSpec(memory_space=pltpu.SMEM)
LIMIT = 48 * 1024 * 1024


def flipped(value, bits):
    size = lax.axis_size("tp")
    return lax.ppermute(value, "tp", [(i, i ^ bits) for i in range(size)])


def plan_kernel(src_ref, page_ref, wanted_ref, place_ref):
    slots = src_ref.shape[1]
    sources = wanted_ref.shape[0]
    src = src_ref[...]
    order = lax.broadcasted_iota(jnp.int32, (1, slots), 1)
    coded = order * 65536 + page_ref[...]
    named = lax.broadcasted_iota(jnp.int32, (sources, slots), 0) == src
    first = jnp.min(jnp.where(named, coded, slots * 65536), axis=1, keepdims=True)
    last = jnp.max(jnp.where(named, coded, 0), axis=1, keepdims=True)
    found = first < slots * 65536
    wanted_ref[:, 0:1] = jnp.where(found, first & 65535, 0)
    wanted_ref[:, 1:2] = jnp.where(found, last & 65535, 0)
    rows = lax.broadcasted_iota(jnp.int32, (slots, slots), 0)
    columns = lax.broadcasted_iota(jnp.int32, (slots, slots), 1)
    src_column = jnp.max(jnp.where(rows == columns, src, 0), axis=1, keepdims=True)
    again = jnp.max(jnp.where((src_column == src) & (rows < columns), 1, 0), axis=0, keepdims=True)
    place_ref[...] = src * 2 + again


def make_plan(plan_src, plan_page, sources):
    slots = plan_src.shape[1]
    return pl.pallas_call(
        plan_kernel,
        out_shape=(
            jax.ShapeDtypeStruct((sources, 2), jnp.int32),
            jax.ShapeDtypeStruct((1, slots), jnp.int32),
        ),
        in_specs=[VMEM, VMEM],
        out_specs=(VMEM, VMEM),
        name="make_plan",
    )(plan_src, plan_page)


def take_kernel(at_ref, from_ref, to_ref, sem):
    columns = at_ref.shape[1]

    @pl.loop(0, at_ref.shape[0])
    def _(row):
        for column in range(columns):
            pltpu.make_async_copy(
                from_ref.at[at_ref[row, column]], to_ref.at[row * columns + column], sem
            ).start()

    pltpu.make_async_copy(to_ref, to_ref, sem).wait()


def take(pages, at, name):
    count = at.shape[0] * at.shape[1]
    shape = (count,) + pages.shape[1:]
    return pl.pallas_call(
        take_kernel,
        out_shape=jax.ShapeDtypeStruct(shape, pages.dtype),
        in_specs=[SMEM, ANY],
        out_specs=ANY,
        scratch_shapes=[pltpu.SemaphoreType.DMA],
        cost_estimate=pl.CostEstimate(
            flops=0, bytes_accessed=2 * count * pages.shape[1] * pages.shape[2] * 2, transcendentals=0
        ),
        name=name,
    )(at, pages)


def attend_kernel(info_ref, place_ref, pages_ref, query_ref, fresh_ref, out_ref, cache, sem):
    half, page, width = cache.shape
    head = width // 2
    which = info_ref[0]
    length = info_ref[1]

    @pl.loop(0, half)
    def _(slot):
        pltpu.make_async_copy(
            pages_ref.at[place_ref[0, which * half + slot]], cache.at[slot], sem
        ).start()

    query = query_ref[which]
    steps = fresh_ref.shape[1]
    rows = query.shape[0]
    scale = head ** (-0.5)
    contract_last = (((1,), (1,)), ((), ()))
    fresh = fresh_ref[which]
    fresh_scores = (
        lax.dot_general(query, fresh[:, :head], contract_last, preferred_element_type=jnp.float32) * scale
    )
    step_of = lax.broadcasted_iota(jnp.int32, (rows, steps), 0) // (rows // steps)
    key_step = lax.broadcasted_iota(jnp.int32, (rows, steps), 1)
    fresh_scores = jnp.where(step_of >= key_step, fresh_scores, jnp.float32(-1e30))
    pltpu.make_async_copy(cache, cache, sem).wait()
    keys = cache[:, :, :head].reshape(half * page, head)
    scores = lax.dot_general(query, keys, contract_last, preferred_element_type=jnp.float32) * scale
    position = lax.broadcasted_iota(jnp.int32, scores.shape, 1)
    scores = jnp.where(position < length, scores, jnp.float32(-1e30))
    highest = jnp.maximum(
        jnp.max(scores, axis=1, keepdims=True), jnp.max(fresh_scores, axis=1, keepdims=True)
    )
    weights = jnp.exp(scores - highest)
    fresh_weights = jnp.exp(fresh_scores - highest)
    total = jnp.sum(weights, axis=1, keepdims=True) + jnp.sum(fresh_weights, axis=1, keepdims=True)
    values = cache[:, :, head:].reshape(half * page, head)
    mixed = jnp.dot((weights / total).astype(jnp.bfloat16), values, preferred_element_type=jnp.float32)
    fresh_prob = (fresh_weights / total).astype(jnp.bfloat16).astype(jnp.float32)
    fresh_values = fresh[:, head:].astype(jnp.float32)
    for step in range(steps):
        mixed = mixed + fresh_prob[:, step : step + 1] * fresh_values[step : step + 1, :]
    out_ref[...] = mixed.astype(jnp.bfloat16)


def attend(which, length, place, arrived, queries, fresh, name):
    half = place.shape[1] // 2
    rows, head = queries.shape[1:]
    info = jnp.stack([which, length]).astype(jnp.int32)
    return pl.pallas_call(
        attend_kernel,
        out_shape=jax.ShapeDtypeStruct((rows, head), jnp.bfloat16),
        in_specs=[SMEM, SMEM, ANY, VMEM, VMEM],
        out_specs=VMEM,
        scratch_shapes=[
            pltpu.VMEM((half,) + arrived.shape[1:], arrived.dtype),
            pltpu.SemaphoreType.DMA,
        ],
        compiler_params=pltpu.CompilerParams(vmem_limit_bytes=LIMIT),
        cost_estimate=pl.CostEstimate(
            flops=4 * rows * half * arrived.shape[1] * head,
            bytes_accessed=half * arrived.shape[1] * arrived.shape[2] * 2,
            transcendentals=rows * half * arrived.shape[1],
        ),
        name=name,
    )(info, place, arrived, queries, fresh)


def on_device(old_cache, old_weight, plan_src, plan_page, lengths, queries, new_kv):
    devices = lax.axis_size("inst") * lax.axis_size("tp")
    steps = queries.shape[1]
    width = old_cache.shape[2]
    heads = new_kv.shape[2] // width
    head = width // 2
    groups = queries.shape[2] // (heads * head)
    side = lax.axis_index("tp") % 2

    wanted, place = make_plan(plan_src, plan_page, devices)
    asked = lax.all_to_all(wanted, BOTH, split_axis=0, concat_axis=0, tiled=True)
    outgoing = take(old_cache, asked, "take_outgoing")
    outgoing = outgoing.reshape((devices, 2) + old_cache.shape[1:])
    arrived = lax.all_to_all(outgoing, BOTH, split_axis=0, concat_axis=0, tiled=True)
    arrived = arrived.reshape((devices * 2,) + old_cache.shape[1:])

    rows = queries.reshape(steps, heads, groups, head).transpose(1, 0, 2, 3)
    rows = rows.reshape(heads, steps * groups, head)
    fresh = new_kv.reshape(steps, heads, width).transpose(1, 0, 2)
    length = lax.dynamic_index_in_dim(lengths[0, :, 0], side, 0, keepdims=False)
    passed = attend(1 - side, length, place, arrived, rows, fresh, "attend_other")
    partner = flipped(passed, 1)
    kept = attend(side, length, place, arrived, rows, fresh, "attend_own")
    moved = take(arrived, place.reshape(-1, 1), "take_arrived")

    both = jnp.stack([kept, partner]).reshape(2 * steps, groups * head)
    partial = jnp.dot(both, old_weight, preferred_element_type=jnp.float32)
    own, other = partial[:steps], partial[steps:]
    own = own + flipped(other.astype(jnp.bfloat16), 1).astype(jnp.float32)
    sent = own.astype(jnp.bfloat16)
    parts = [flipped(sent, bits) for bits in range(2, lax.axis_size("tp"), 2)]
    for part in parts:
        own = own + part.astype(jnp.float32)
    return own.reshape(1, steps, -1).astype(jnp.bfloat16), moved


def solution(mesh):
    placed = (
        P(BOTH, None, None),
        P("tp", None),
        P(BOTH, None),
        P(BOTH, None),
        P("inst", None, None),
        P(BOTH, None, None),
        P(BOTH, None, None),
    )
    return jax.shard_map(
        on_device,
        mesh=mesh,
        in_specs=placed,
        out_specs=(P(BOTH, None, None), P(BOTH, None, None)),
        check_vma=False,
    )
```

time: 955 us -> 548 us (0.57)
  blocking collectives: 556 us -> 18.8 us
  Pallas kernels: 0 us -> 395 us
  waiting for transfers between devices: 272 us -> 107 us
  starting transfers between devices: 79.6 us -> 18.2 us
  local copies, waits for them, and re-layouts: 18.1 us -> 1.4 us
  matrix products: 14.4 us -> 4.58 us
    all_gather x2 -> x0, blocking collectives: 556 us -> none  [the longest x1 278 us: on_device(): lax.all_gather(plan_page, ('inst', 'tp'), axis=0, tiled=True)]
    pallas_call x0 -> x5, Pallas kernels: none -> 395 us  [the longest x2 387 us: take(): pl.pallas_call(take_kernel, out_shape=jax.ShapeDtypeStruct(shape, pages.d...]
    ppermute x3 -> x5, waiting for transfers between devices: 169 us -> 2.95 us  [flipped(): return lax.ppermute(value, 'tp', [(i, i ^ bits) for i in range(size)])]
    all_to_all x1, starting transfers between devices: 74.3 us -> 7.15 us  [on_device(): lax.all_to_all(outgoing, BOTH, split_axis=0, concat_axis=0, tiled=True)]
    all_to_all x0 -> x1, blocking collectives: none -> 18.8 us  [on_device(): lax.all_to_all(wanted, BOTH, split_axis=0, concat_axis=0, tiled=True)]
    gather x2 -> x0, local copies, waits for them, and re-layouts: 16.9 us -> none  [the longest x1 10.7 us: on_device(): old_cache[picked] * filled[:, :, None, None].astype(old_cache.dtype)]
    dot_general x6 -> x1, matrix products: 14.4 us -> 4.58 us  [on_device(): partial = jnp.dot(both, old_weight, preferred_element_type=jnp.float32)]
  transfers between devices with their start and end apart: 4 -> 6, of which waited for: 4 -> 3; matrix products, arithmetic and copies ran while one was open for 1% -> 0% of each run, Pallas kernels for 0% -> 24%
where the time goes in v1:
time: 548 us; the launch traced here: 547 us
  Pallas kernels  395 us (72%)
  waiting for transfers between devices  107 us (20%)
  blocking collectives  18.8 us (3%)
  starting transfers between devices  18.2 us (3%)
    pallas_call x2, Pallas kernels, take(): pl.pallas_call(take_kernel, out_shape=jax.ShapeDtypeStruct(shape, pages.d...  387 us
    all_to_all x1, waiting for transfers between devices, on_device(): lax.all_to_all(outgoing, BOTH, split_axis=0, concat_axis=0, tiled=True)  104 us
    all_to_all x1, blocking collectives, on_device(): lax.all_to_all(wanted, BOTH, split_axis=0, concat_axis=0, tiled=True)  18.8 us
    ppermute x5, starting transfers between devices, flipped(): return lax.ppermute(value, 'tp', [(i, i ^ bits) for i in range(size)])  11 us
  transfers between devices with their start and end apart: 6, of which 3 were waited for; matrix products, arithmetic and copies ran while one was open for 0% of the time, Pallas kernels for 24%

profile of v1, /device:TPU:24, one launch (start us, length us, event | category | flops | bytes accessed | tf_op | source)
XLA Modules:
  0.0 547.0 jit_solution(2659429971862472077)
XLA Ops:
  0.6 0.0 copy-start
  0.6 1.5 make_plan.1
  2.2 18.8 %all_to_all.16 = s32[128,1,2]{2,1,0:T(1,128)} all-to-all(s32[128,1,2]{2,1,0:T(1,128)} %bitcast.35), channel_id=1, replica_groups=mesh['inst'=16,'tp'=8] {'inst','tp'}, dimensions={0} | all-to-all | bytes 2048 | tf_op jit(solution)/shard_map/all_to_all | solution.py:161
  20.9 257.0 %take_outgoing.1 = bf16[256,64,256]{2,1,0:T(8,128)(2,1)} custom-call(s32[128,2]{1,0:T(8,128)} %bitcast.34, bf16[128,64,256]{2,1,0:T(8,128)(2,1)} %from_ref.1), custom_call_target="tpu_custom_call" | custom-call | bytes 16777216 | tf_op jit(solution)/shard_map/take_outgoing/pallas_call | solution.py:71
  277.9 0.0 copy-start.3
  277.9 0.0 copy-start.1
  277.9 7.2 %all-to-all-start.1 = ((bf16[128,2,64,256]{3,2,1,0:T(8,128)(2,1)}), bf16[128,2,64,256]{3,2,1,0:T(8,128)(2,1)}, u32[]{:S(2)}, u32[]{:S(2)}) async-start(bf16[128,2,64,256]{3,2,1,0:T(8,128)(2,1)} %bitcast.33), calls=%async_computation.1 | async-start | bytes 16777216 | tf_op jit(solution)/shard_map/all_to_all | solution.py:164
  285.1 0.6 constant_dynamic-slice_fusion
  285.7 0.7 pad_add_fusion
  286.4 104.4 %all-to-all-done.1 = bf16[128,2,64,256]{3,2,1,0:T(8,128)(2,1)} async-done(((bf16[128,2,64,256]{3,2,1,0:T(8,128)(2,1)}), bf16[128,2,64,256]{3,2,1,0:T(8,128)(2,1)}, u32[]{:S(2)}, u32[]{:S(2)}) %all-to-all-start.1) | async-done | bytes 8388640 | tf_op jit(solution)/shard_map/all_to_all | solution.py:164
  390.9 3.1 attend_other.1
  394.0 0.1 collective-permute-start
  394.1 3.1 attend_own.1
  397.2 0.5 collective-permute-done
  397.7 4.6 fusion.2
  402.3 1.6 collective-permute-start.1
  403.9 2.4 collective-permute-done.1
  406.4 5.4 collective-permute-start.4
  411.8 1.0 collective-permute-start.3
  412.8 2.9 collective-permute-start.2
  415.7 0.7 copy.13.at_ref
  416.4 129.9 %take_arrived.1 = bf16[128,64,256]{2,1,0:T(8,128)(2,1)} custom-call(s32[128,1]{1,0:T(8,128)} %copy.13.at_ref, bf16[256,64,256]{2,1,0:T(8,128)(2,1)} %bitcast.6.pages_ref.from_ref), custom_call_target="tpu_custom_call" | custom-call | bytes 8388608 | tf_op jit(solution)/shard_map/take_arrived/pallas_call | solution.py:71
  546.4 0.0 collective-permute-done.4
  546.4 0.7 fusion.1
  (12 shorter events, 0.1 us)
Async XLA Ops:
  0.6 284.5 %copy-start = (s32[1,2,1]{1,2,0:T(1,128)S(1)}, s32[1,2,1]{1,2,0:T(1,128)}, u32[]{:S(2)}) copy-start(s32[1,2,1]{1,2,0:T(1,128)} %param.11) | copy-start | bytes 28
  277.9 8.5 %copy-start.3 = (bf16[1,4,2048]{2,1,0:T(4,128)(2,1)S(1)}, bf16[1,4,2048]{2,1,0:T(4,128)(2,1)}, u32[]{:S(2)}) copy-start(bf16[1,4,2048]{2,1,0:T(4,128)(2,1)} %param.12) | copy-start | bytes 49156
  277.9 113.0 %copy-start.1 = (bf16[1,4,512]{2,1,0:T(4,128)(2,1)S(1)}, bf16[1,4,512]{2,1,0:T(4,128)(2,1)}, u32[]{:S(2)}) copy-start(bf16[1,4,512]{2,1,0:T(4,128)(2,1)} %param.13) | copy-start | bytes 12292
  277.9 113.0 %copy-start.2 = (s32[1,128]{1,0:T(1,128)S(1)}, s32[1,128]{1,0:T(1,128)}, u32[]{:S(2)}) copy-start(s32[1,128]{1,0:T(1,128)} %get-tuple-element.4.place_ref) | copy-start | bytes 1540
  277.9 112.9 %all-to-all-start.1 = ((bf16[128,2,64,256]{3,2,1,0:T(8,128)(2,1)}), bf16[128,2,64,256]{3,2,1,0:T(8,128)(2,1)}, u32[]{:S(2)}, u32[]{:S(2)}) async-start(bf16[128,2,64,256]{3,2,1,0:T(8,128)(2,1)} %bitcast.33), calls=%async_computation.1 | async-start | bytes 16777216 | tf_op jit(solution)/shard_map/all_to_all | solution.py:164
  394.0 3.7 collective-permute-start
  402.3 4.0 collective-permute-start.1
  406.4 140.0 %collective-permute-start.4 = (bf16[4,4096]{1,0:T(4,128)(2,1)S(1)}, bf16[4,4096]{1,0:T(4,128)(2,1)S(1)}, u32[]{:S(2)}, u32[]{:S(2)}) collective-permute-start(bf16[4,4096]{1,0:T(4,128)(2,1)S(1)} %fusion), channel_id=1, source_target_pairs={{0,6},{1,7},{2,4},{3,5},{4,2},{5,3},{6,0},{7,1},{8,14},{9,15},{10,... | collective-permute-start | bytes 98312 | tf_op jit(solution)/shard_map/ppermute | solution.py:19
  411.8 134.6 %collective-permute-start.3 = (bf16[4,4096]{1,0:T(4,128)(2,1)S(1)}, bf16[4,4096]{1,0:T(4,128)(2,1)S(1)}, u32[]{:S(2)}, u32[]{:S(2)}) collective-permute-start(bf16[4,4096]{1,0:T(4,128)(2,1)S(1)} %fusion), channel_id=1, source_target_pairs={{0,4},{1,5},{2,6},{3,7},{4,0},{5,1},{6,2},{7,3},{8,12},{9,13},{10,... | collective-permute-start | bytes 98312 | tf_op jit(solution)/shard_map/ppermute | solution.py:19
  412.8 133.6 %collective-permute-start.2 = (bf16[4,4096]{1,0:T(4,128)(2,1)S(1)}, bf16[4,4096]{1,0:T(4,128)(2,1)S(1)}, u32[]{:S(2)}, u32[]{:S(2)}) collective-permute-start(bf16[4,4096]{1,0:T(4,128)(2,1)S(1)} %fusion), channel_id=1, source_target_pairs={{0,2},{1,3},{2,0},{3,1},{4,6},{5,7},{6,4},{7,5},{8,10},{9,11},{10,... | collective-permute-start | bytes 98312 | tf_op jit(solution)/shard_map/ppermute | solution.py:19

commit v2 on v1

--- a/solution.py
+++ b/solution.py
@@ -11,7 +11,7 @@
 ANY = pl.BlockSpec(memory_space=pl.ANY)
 VMEM = pl.BlockSpec(memory_space=pltpu.VMEM)
 SMEM = pl.BlockSpec(memory_space=pltpu.SMEM)
-LIMIT = 48 * 1024 * 1024
+LIMIT = 24 * 1024 * 1024
 
 
 def flipped(value, bits):
@@ -55,7 +55,7 @@
 def take_kernel(at_ref, from_ref, to_ref, sem):
     columns = at_ref.shape[1]
 
-    @pl.loop(0, at_ref.shape[0])
+    @pl.loop(0, at_ref.shape[0], unroll=4)
     def _(row):
         for column in range(columns):
             pltpu.make_async_copy(
@@ -65,29 +65,31 @@
     pltpu.make_async_copy(to_ref, to_ref, sem).wait()
 
 
-def take(pages, at, name):
+def take(pages, at):
     count = at.shape[0] * at.shape[1]
     shape = (count,) + pages.shape[1:]
     return pl.pallas_call(
         take_kernel,
         out_shape=jax.ShapeDtypeStruct(shape, pages.dtype),
-        in_specs=[SMEM, ANY],
+        in_specs=[SMEM, VMEM],
         out_specs=ANY,
         scratch_shapes=[pltpu.SemaphoreType.DMA],
+        compiler_params=pltpu.CompilerParams(vmem_limit_bytes=LIMIT),
         cost_estimate=pl.CostEstimate(
             flops=0, bytes_accessed=2 * count * pages.shape[1] * pages.shape[2] * 2, transcendentals=0
         ),
-        name=name,
-    )(at, pages)
-
-
-def attend_kernel(info_ref, place_ref, pages_ref, query_ref, fresh_ref, out_ref, cache, sem):
+        name="take_outgoing",
+    )(at, pltpu.with_memory_space_constraint(pages, pltpu.VMEM))
+
+
+def attend_kernel(info_ref, place_ref, pages_ref, query_ref, fresh_ref, *rest):
+    out_ref, moved_ref, cache, sem, out_sem = rest[-5:]
     half, page, width = cache.shape
     head = width // 2
     which = info_ref[0]
     length = info_ref[1]
 
-    @pl.loop(0, half)
+    @pl.loop(0, half, unroll=4)
     def _(slot):
         pltpu.make_async_copy(
             pages_ref.at[place_ref[0, which * half + slot]], cache.at[slot], sem
@@ -102,10 +104,12 @@
     fresh_scores = (
         lax.dot_general(query, fresh[:, :head], contract_last, preferred_element_type=jnp.float32) * scale
     )
-    step_of = lax.broadcasted_iota(jnp.int32, (rows, steps), 0) // (rows // steps)
+    step_of = lax.broadcasted_iota(jnp.int32, (rows, steps), 0) % steps
     key_step = lax.broadcasted_iota(jnp.int32, (rows, steps), 1)
     fresh_scores = jnp.where(step_of >= key_step, fresh_scores, jnp.float32(-1e30))
     pltpu.make_async_copy(cache, cache, sem).wait()
+    store = pltpu.make_async_copy(cache, moved_ref.at[pl.ds(which * half, half)], out_sem)
+    store.start()
     keys = cache[:, :, :head].reshape(half * page, head)
     scores = lax.dot_general(query, keys, contract_last, preferred_element_type=jnp.float32) * scale
     position = lax.broadcasted_iota(jnp.int32, scores.shape, 1)
@@ -123,29 +127,70 @@
     for step in range(steps):
         mixed = mixed + fresh_prob[:, step : step + 1] * fresh_values[step : step + 1, :]
     out_ref[...] = mixed.astype(jnp.bfloat16)
-
-
-def attend(which, length, place, arrived, queries, fresh, name):
+    store.wait()
+
+
+def attend(which, length, place, arrived, queries, fresh, moved, name):
     half = place.shape[1] // 2
     rows, head = queries.shape[1:]
     info = jnp.stack([which, length]).astype(jnp.int32)
+    begun = [] if moved is None else [moved]
     return pl.pallas_call(
         attend_kernel,
-        out_shape=jax.ShapeDtypeStruct((rows, head), jnp.bfloat16),
-        in_specs=[SMEM, SMEM, ANY, VMEM, VMEM],
-        out_specs=VMEM,
+        out_shape=(
+            jax.ShapeDtypeStruct((rows, head), jnp.bfloat16),
+            jax.ShapeDtypeStruct((2 * half,) + arrived.shape[1:], arrived.dtype),
+        ),
+        in_specs=[SMEM, SMEM, ANY, VMEM, VMEM] + [ANY for _ in begun],
+        out_specs=(VMEM, ANY),
+        input_output_aliases={5: 1} if begun else {},
         scratch_shapes=[
             pltpu.VMEM((half,) + arrived.shape[1:], arrived.dtype),
+            pltpu.SemaphoreType.DMA,
             pltpu.SemaphoreType.DMA,
         ],
         compiler_params=pltpu.CompilerParams(vmem_limit_bytes=LIMIT),
         cost_estimate=pl.CostEstimate(
             flops=4 * rows * half * arrived.shape[1] * head,
-            bytes_accessed=half * arrived.shape[1] * arrived.shape[2] * 2,
+            bytes_accessed=2 * half * arrived.shape[1] * arrived.shape[2] * 2,
             transcendentals=rows * half * arrived.shape[1],
         ),
         name=name,
-    )(info, place, arrived, queries, fresh)
+    )(info, place, arrived, queries, fresh, *begun)
+
+
+def project_kernel(kept_ref, partner_ref, weight_ref, own_ref, other_ref):
+    steps = own_ref.shape[0]
+    rows = []
+    for ref in (kept_ref, partner_ref):
+        value = ref[...].astype(jnp.float32)
+        rows.append(
+            jnp.concatenate([value[at : at + steps] for at in range(0, value.shape[0], steps)], axis=1)
+        )
+    both = jnp.concatenate(rows, axis=0).astype(jnp.bfloat16)
+    tile = 1024
+    for at in range(0, weight_ref.shape[1], tile):
+        product = jnp.dot(both, weight_ref[:, at : at + tile], preferred_element_type=jnp.float32)
+        own_ref[:, at : at + tile] = product[:steps]
+        other_ref[:, at : at + tile] = product[steps:].astype(jnp.bfloat16)
+
+
+def project(kept, partner, weight, steps):
+    wide = weight.shape[1]
+    return pl.pallas_call(
+        project_kernel,
+        out_shape=(
+            jax.ShapeDtypeStruct((steps, wide), jnp.float32),
+            jax.ShapeDtypeStruct((steps, wide), jnp.bfloat16),
+        ),
+        in_specs=[VMEM, VMEM, VMEM],
+        out_specs=(VMEM, VMEM),
+        compiler_params=pltpu.CompilerParams(vmem_limit_bytes=LIMIT),
+        cost_estimate=pl.CostEstimate(
+            flops=4 * steps * weight.size, bytes_accessed=weight.size * 2, transcendentals=0
+        ),
+        name="project",
+    )(kept, partner, pltpu.with_memory_space_constraint(weight, pltpu.VMEM))
 
 
 def on_device(old_cache, old_weight, plan_src, plan_page, lengths, queries, new_kv):
@@ -159,24 +204,21 @@
 
     wanted, place = make_plan(plan_src, plan_page, devices)
     asked = lax.all_to_all(wanted, BOTH, split_axis=0, concat_axis=0, tiled=True)
-    outgoing = take(old_cache, asked, "take_outgoing")
+    outgoing = take(old_cache, asked)
     outgoing = outgoing.reshape((devices, 2) + old_cache.shape[1:])
     arrived = lax.all_to_all(outgoing, BOTH, split_axis=0, concat_axis=0, tiled=True)
     arrived = arrived.reshape((devices * 2,) + old_cache.shape[1:])
 
-    rows = queries.reshape(steps, heads, groups, head).transpose(1, 0, 2, 3)
-    rows = rows.reshape(heads, steps * groups, head)
+    rows = queries.reshape(steps, heads, groups, head).transpose(1, 2, 0, 3)
+    rows = rows.reshape(heads, groups * steps, head)
     fresh = new_kv.reshape(steps, heads, width).transpose(1, 0, 2)
     length = lax.dynamic_index_in_dim(lengths[0, :, 0], side, 0, keepdims=False)
-    passed = attend(1 - side, length, place, arrived, rows, fresh, "attend_other")
+    passed, moved = attend(1 - side, length, place, arrived, rows, fresh, None, "attend_other")
     partner = flipped(passed, 1)
-    kept = attend(side, length, place, arrived, rows, fresh, "attend_own")
-    moved = take(arrived, place.reshape(-1, 1), "take_arrived")
-
-    both = jnp.stack([kept, partner]).reshape(2 * steps, groups * head)
-    partial = jnp.dot(both, old_weight, preferred_element_type=jnp.float32)
-    own, other = partial[:steps], partial[steps:]
-    own = own + flipped(other.astype(jnp.bfloat16), 1).astype(jnp.float32)
+    kept, moved = attend(side, length, place, arrived, rows, fresh, moved, "attend_own")
+
+    own, other = project(kept, partner, old_weight, steps)
+    own = own + flipped(other, 1).astype(jnp.float32)
     sent = own.astype(jnp.bfloat16)
     parts = [flipped(sent, bits) for bits in range(2, lax.axis_size("tp"), 2)]
     for part in parts:

time: 548 us -> 179 us (0.33)
  Pallas kernels: 395 us -> 24.3 us
    pallas_call x2 -> x1, Pallas kernels: 387 us -> 13.6 us  [take(): pl.pallas_call(take_kernel, out_shape=jax.ShapeDtypeStruct(shape, pages.d...]
  transfers between devices with their start and end apart: 6 -> 6, of which waited for: 3 -> 4; matrix products, arithmetic and copies ran while one was open for 0% -> 1% of each run, Pallas kernels for 24% -> 2%
where the time goes in v2:
time: 179 us; the launch traced here: 178 us
  waiting for transfers between devices  109 us (61%)
  Pallas kernels  24.3 us (14%)
  starting transfers between devices  18.5 us (10%)
  blocking collectives  18.3 us (10%)
  local copies, waits for them, and re-layouts  6.03 us (3%)
    all_to_all x1, waiting for transfers between devices, on_device(): lax.all_to_all(outgoing, BOTH, split_axis=0, concat_axis=0, tiled=True)  104 us
    all_to_all x1, blocking collectives, on_device(): lax.all_to_all(wanted, BOTH, split_axis=0, concat_axis=0, tiled=True)  18.3 us
    pallas_call x1, Pallas kernels, take(): pl.pallas_call(take_kernel, out_shape=jax.ShapeDtypeStruct(shape, pages.d...  13.6 us
    ppermute x5, starting transfers between devices, flipped(): return lax.ppermute(value, 'tp', [(i, i ^ bits) for i in range(size)])  11.4 us
    pallas_call x2, Pallas kernels, attend(): pl.pallas_call(attend_kernel, out_shape=(jax.ShapeDtypeStruct((rows, head...  7.97 us
    all_to_all x1, starting transfers between devices, on_device(): lax.all_to_all(outgoing, BOTH, split_axis=0, concat_axis=0, tiled=True)  7.11 us
    unnamed x16, local copies, waits for them, and re-layouts  5.44 us
    ppermute x5, waiting for transfers between devices, flipped(): return lax.ppermute(value, 'tp', [(i, i ^ bits) for i in range(size)])  4.47 us
  transfers between devices with their start and end apart: 6, of which 4 were waited for; matrix products, arithmetic and copies ran while one was open for 1% of the time, Pallas kernels for 2%

profile of v2, /device:TPU:24, one launch (start us, length us, event | category | flops | bytes accessed | tf_op | source)
XLA Modules:
  0.0 178.3 jit_solution(7525404067309619221)
XLA Ops:
  0.6 0.0 copy-start
  0.6 1.5 make_plan.1
  2.2 18.3 %all_to_all.16 = s32[128,1,2]{2,1,0:T(1,128)S(1)} all-to-all(s32[128,1,2]{2,1,0:T(1,128)} %bitcast.27), channel_id=1, replica_groups=mesh['inst'=16,'tp'=8] {'inst','tp'}, dimensions={0} | all-to-all | bytes 2048 | tf_op jit(solution)/shard_map/all_to_all | solution.py:206
  20.5 2.2 %copy-done.2 = bf16[128,64,256]{2,1,0:T(8,128)(2,1)S(1)} copy-done((bf16[128,64,256]{2,1,0:T(8,128)(2,1)S(1)}, bf16[128,64,256]{2,1,0:T(8,128)(2,1)}, u32[]{:S(2)}) %copy-start.2) | copy-done | bytes 4194328
  22.7 13.6 %take_outgoing.1 = bf16[256,64,256]{2,1,0:T(8,128)(2,1)S(1)} custom-call(s32[128,2]{1,0:T(8,128)S(1)} %bitcast.22, bf16[128,64,256]{2,1,0:T(8,128)(2,1)S(1)} %copy-done.2), custom_call_target="tpu_custom_call" | custom-call | bytes 16777216 | tf_op jit(solution)/shard_map/take_outgoing/pallas_call | solution.py:71
  36.3 3.2 %copy-done.1 = bf16[256,64,256]{2,1,0:T(8,128)(2,1)} copy-done((bf16[256,64,256]{2,1,0:T(8,128)(2,1)}, bf16[256,64,256]{2,1,0:T(8,128)(2,1)S(1)}, u32[]{:S(2)}) %copy-start.1) | copy-done | bytes 8388632
  39.6 7.1 %all-to-all-start.1 = ((bf16[128,2,64,256]{3,2,1,0:T(8,128)(2,1)}), bf16[128,2,64,256]{3,2,1,0:T(8,128)(2,1)}, u32[]{:S(2)}, u32[]{:S(2)}) async-start(bf16[128,2,64,256]{3,2,1,0:T(8,128)(2,1)} %bitcast.19), calls=%async_computation.1 | async-start | bytes 16777216 | tf_op jit(solution)/shard_map/all_to_all | solution.py:209
  46.7 0.6 constant_dynamic-slice_fusion
  47.3 0.7 pad_add_fusion
  48.0 104.5 %all-to-all-done.1 = bf16[128,2,64,256]{3,2,1,0:T(8,128)(2,1)} async-done(((bf16[128,2,64,256]{3,2,1,0:T(8,128)(2,1)}), bf16[128,2,64,256]{3,2,1,0:T(8,128)(2,1)}, u32[]{:S(2)}, u32[]{:S(2)}) %all-to-all-start.1) | async-done | bytes 8388640 | tf_op jit(solution)/shard_map/all_to_all | solution.py:209
  152.5 0.0 slice-start
  152.5 4.0 %attend_other.1 = (bf16[32,128]{1,0:T(8,128)(2,1)S(1)}, bf16[128,64,256]{2,1,0:T(8,128)(2,1)}) custom-call(s32[2]{0:T(128)S(1)} %get-tuple-element.19.info_ref, s32[1,128]{1,0:T(1,128)S(1)} %copy-done.5, bf16[256,64,256]{2,1,0:T(8,128)(2,1)} %bitcast.6.pages_ref, bf16[2,32,128]{2,1,0:T(8,128)(2,1)S(1)} %bitcast.23, bf16[2,4,256]{2,1,0:T(4,128)(2,1)S(1)} %bitcast.25), custom_call_target="tpu_custom_call" | custom-call | flops 67108864 | bytes 4194304 | tf_op jit(solution)/shard_map/attend_other/pallas_call | solution.py:138
  156.5 0.1 collective-permute-start
  156.6 0.0 slice-start.1
  156.6 4.0 %attend_own.1 = (bf16[32,128]{1,0:T(8,128)(2,1)S(1)}, bf16[128,64,256]{2,1,0:T(8,128)(2,1)}) custom-call(s32[2]{0:T(128)S(1)} %get-tuple-element.18.info_ref, s32[1,128]{1,0:T(1,128)S(1)} %copy-done.5, bf16[256,64,256]{2,1,0:T(8,128)(2,1)} %bitcast.6.pages_ref, bf16[2,32,128]{2,1,0:T(8,128)(2,1)S(1)} %bitcast.24, ...), custom_call_target="tpu_custom_call", output_to_operand_aliasing={{1}: (5, {})} | custom-call | flops 67108864 | bytes 4194304 | tf_op jit(solution)/shard_map/attend_own/pallas_call | solution.py:138
  160.6 1.2 project.1
  161.8 2.0 %collective-permute-start.1 = (bf16[4,4096]{1,0:T(4,128)(2,1)S(1)}, bf16[4,4096]{1,0:T(4,128)(2,1)S(1)}, u32[]{:S(2)}, u32[]{:S(2)}) collective-permute-start(bf16[4,4096]{1,0:T(4,128)(2,1)S(1)} %get-tuple-element.16), channel_id=1, source_target_pairs={{0,1},{1,0},{2,3},{3,2},{4,5},{5,4},{6,7},{7,6},{8,9},{9,8},{10,11... | collective-permute-start | bytes 98312 | tf_op jit(solution)/shard_map/ppermute | solution.py:19
  163.8 1.9 %collective-permute-done.1 = bf16[4,4096]{1,0:T(4,128)(2,1)S(1)} collective-permute-done((bf16[4,4096]{1,0:T(4,128)(2,1)S(1)}, bf16[4,4096]{1,0:T(4,128)(2,1)S(1)}, u32[]{:S(2)}, u32[]{:S(2)}) %collective-permute-start.1) | collective-permute-done | bytes 32800 | tf_op jit(solution)/shard_map/ppermute | solution.py:19
  165.8 5.5 %collective-permute-start.4 = (bf16[4,4096]{1,0:T(4,128)(2,1)S(1)}, bf16[4,4096]{1,0:T(4,128)(2,1)S(1)}, u32[]{:S(2)}, u32[]{:S(2)}) collective-permute-start(bf16[4,4096]{1,0:T(4,128)(2,1)S(1)} %fusion), channel_id=1, source_target_pairs={{0,6},{1,7},{2,4},{3,5},{4,2},{5,3},{6,0},{7,1},{8,14},{9,15},{10,... | collective-permute-start | bytes 98312 | tf_op jit(solution)/shard_map/ppermute | solution.py:19
  171.3 1.0 collective-permute-start.3
  172.2 2.9 %collective-permute-start.2 = (bf16[4,4096]{1,0:T(4,128)(2,1)S(1)}, bf16[4,4096]{1,0:T(4,128)(2,1)S(1)}, u32[]{:S(2)}, u32[]{:S(2)}) collective-permute-start(bf16[4,4096]{1,0:T(4,128)(2,1)S(1)} %fusion), channel_id=1, source_target_pairs={{0,2},{1,3},{2,0},{3,1},{4,6},{5,7},{6,4},{7,5},{8,10},{9,11},{10,... | collective-permute-start | bytes 98312 | tf_op jit(solution)/shard_map/ppermute | solution.py:19
  175.1 1.6 collective-permute-done.3
  176.7 1.0 collective-permute-done.2
  177.7 0.7 fusion.1
  (15 shorter events, 0.0 us)
Async XLA Ops:
  0.6 46.1 %copy-start = (s32[1,2,1]{1,2,0:T(1,128)S(1)}, s32[1,2,1]{1,2,0:T(1,128)}, u32[]{:S(2)}) copy-start(s32[1,2,1]{1,2,0:T(1,128)} %param.11) | copy-start | bytes 28
  20.5 2.2 %copy-start.2 = (bf16[128,64,256]{2,1,0:T(8,128)(2,1)S(1)}, bf16[128,64,256]{2,1,0:T(8,128)(2,1)}, u32[]{:S(2)}) copy-start(bf16[128,64,256]{2,1,0:T(8,128)(2,1)} %from_ref.1) | copy-start | bytes 12582916
  36.3 3.2 %copy-start.1 = (bf16[256,64,256]{2,1,0:T(8,128)(2,1)}, bf16[256,64,256]{2,1,0:T(8,128)(2,1)S(1)}, u32[]{:S(2)}) copy-start(bf16[256,64,256]{2,1,0:T(8,128)(2,1)S(1)} %take_outgoing.1) | copy-start | bytes 25165828
  39.6 112.9 %copy-start.3 = (bf16[1,4,2048]{2,1,0:T(4,128)(2,1)S(1)}, bf16[1,4,2048]{2,1,0:T(4,128)(2,1)}, u32[]{:S(2)}) copy-start(bf16[1,4,2048]{2,1,0:T(4,128)(2,1)} %param.12) | copy-start | bytes 49156
  39.6 112.9 %copy-start.4 = (bf16[1,4,512]{2,1,0:T(4,128)(2,1)S(1)}, bf16[1,4,512]{2,1,0:T(4,128)(2,1)}, u32[]{:S(2)}) copy-start(bf16[1,4,512]{2,1,0:T(4,128)(2,1)} %param.13) | copy-start | bytes 12292
  39.6 112.9 %copy-start.5 = (s32[1,128]{1,0:T(1,128)S(1)}, s32[1,128]{1,0:T(1,128)}, u32[]{:S(2)}) copy-start(s32[1,128]{1,0:T(1,128)} %get-tuple-element.10.place_ref) | copy-start | bytes 1540
  39.6 112.9 %all-to-all-start.1 = ((bf16[128,2,64,256]{3,2,1,0:T(8,128)(2,1)}), bf16[128,2,64,256]{3,2,1,0:T(8,128)(2,1)}, u32[]{:S(2)}, u32[]{:S(2)}) async-start(bf16[128,2,64,256]{3,2,1,0:T(8,128)(2,1)} %bitcast.19), calls=%async_computation.1 | async-start | bytes 16777216 | tf_op jit(solution)/shard_map/all_to_all | solution.py:209
  152.5 8.1 %slice-start = ((s8[8388608]{0:T(1024)(128)(4,1)}), s8[4194304]{0:T(1024)(128)(4,1)S(1)}, s32[]{:S(2)}) async-start(s8[8388608]{0:T(1024)(128)(4,1)} %bitcast.20), calls=%async_computation.2 | async-start | bytes 8388608
  156.5 4.1 %collective-permute-start = (bf16[32,128]{1,0:T(8,128)(2,1)S(1)}, bf16[32,128]{1,0:T(8,128)(2,1)S(1)}, u32[]{:S(2)}, u32[]{:S(2)}) collective-permute-start(bf16[32,128]{1,0:T(8,128)(2,1)S(1)} %get-tuple-element.14), channel_id=1, source_target_pairs={{0,1},{1,0},{2,3},{3,2},{4,5},{5,4},{6,7},{7,6},{8,9},{9,8},{10,11... | collective-permute-start | bytes 24584 | tf_op jit(solution)/shard_map/ppermute | solution.py:19
  156.6 4.0 %slice-start.1 = ((s8[8388608]{0:T(1024)(128)(4,1)}), s8[4194304]{0:T(1024)(128)(4,1)S(1)}, s32[]{:S(2)}) async-start(s8[8388608]{0:T(1024)(128)(4,1)} %bitcast.20), calls=%async_computation.3 | async-start | bytes 8388608
  161.8 3.9 %collective-permute-start.1 = (bf16[4,4096]{1,0:T(4,128)(2,1)S(1)}, bf16[4,4096]{1,0:T(4,128)(2,1)S(1)}, u32[]{:S(2)}, u32[]{:S(2)}) collective-permute-start(bf16[4,4096]{1,0:T(4,128)(2,1)S(1)} %get-tuple-element.16), channel_id=1, source_target_pairs={{0,1},{1,0},{2,3},{3,2},{4,5},{5,4},{6,7},{7,6},{8,9},{9,8},{10,11... | collective-permute-start | bytes 98312 | tf_op jit(solution)/shard_map/ppermute | solution.py:19
  165.8 9.3 %collective-permute-start.4 = (bf16[4,4096]{1,0:T(4,128)(2,1)S(1)}, bf16[4,4096]{1,0:T(4,128)(2,1)S(1)}, u32[]{:S(2)}, u32[]{:S(2)}) collective-permute-start(bf16[4,4096]{1,0:T(4,128)(2,1)S(1)} %fusion), channel_id=1, source_target_pairs={{0,6},{1,7},{2,4},{3,5},{4,2},{5,3},{6,0},{7,1},{8,14},{9,15},{10,... | collective-permute-start | bytes 98312 | tf_op jit(solution)/shard_map/ppermute | solution.py:19
  171.3 5.4 %collective-permute-start.3 = (bf16[4,4096]{1,0:T(4,128)(2,1)S(1)}, bf16[4,4096]{1,0:T(4,128)(2,1)S(1)}, u32[]{:S(2)}, u32[]{:S(2)}) collective-permute-start(bf16[4,4096]{1,0:T(4,128)(2,1)S(1)} %fusion), channel_id=1, source_target_pairs={{0,4},{1,5},{2,6},{3,7},{4,0},{5,1},{6,2},{7,3},{8,12},{9,13},{10,... | collective-permute-start | bytes 98312 | tf_op jit(solution)/shard_map/ppermute | solution.py:19
  172.2 5.4 %collective-permute-start.2 = (bf16[4,4096]{1,0:T(4,128)(2,1)S(1)}, bf16[4,4096]{1,0:T(4,128)(2,1)S(1)}, u32[]{:S(2)}, u32[]{:S(2)}) collective-permute-start(bf16[4,4096]{1,0:T(4,128)(2,1)S(1)} %fusion), channel_id=1, source_target_pairs={{0,2},{1,3},{2,0},{3,1},{4,6},{5,7},{6,4},{7,5},{8,10},{9,11},{10,... | collective-permute-start | bytes 98312 | tf_op jit(solution)/shard_map/ppermute | solution.py:19

commit v3 on v2

--- a/solution.py
+++ b/solution.py
@@ -8,7 +8,7 @@
 from jax.sharding import PartitionSpec as P
 
 BOTH = ("inst", "tp")
-ANY = pl.BlockSpec(memory_space=pl.ANY)
+HBM = pl.BlockSpec(memory_space=pltpu.HBM)
 VMEM = pl.BlockSpec(memory_space=pltpu.VMEM)
 SMEM = pl.BlockSpec(memory_space=pltpu.SMEM)
 LIMIT = 24 * 1024 * 1024
@@ -19,7 +19,9 @@
     return lax.ppermute(value, "tp", [(i, i ^ bits) for i in range(size)])
 
 
-def plan_kernel(src_ref, page_ref, wanted_ref, place_ref):
+def plan_kernel(src_ref, page_ref, cache_ref, wanted_ref, place_ref, held_ref, sem):
+    hold = pltpu.make_async_copy(cache_ref, held_ref, sem)
+    hold.start()
     slots = src_ref.shape[1]
     sources = wanted_ref.shape[0]
     src = src_ref[...]
@@ -36,20 +38,24 @@
     src_column = jnp.max(jnp.where(rows == columns, src, 0), axis=1, keepdims=True)
     again = jnp.max(jnp.where((src_column == src) & (rows < columns), 1, 0), axis=0, keepdims=True)
     place_ref[...] = src * 2 + again
-
-
-def make_plan(plan_src, plan_page, sources):
+    hold.wait()
+
+
+def make_plan(plan_src, plan_page, pages, sources):
     slots = plan_src.shape[1]
     return pl.pallas_call(
         plan_kernel,
         out_shape=(
             jax.ShapeDtypeStruct((sources, 2), jnp.int32),
             jax.ShapeDtypeStruct((1, slots), jnp.int32),
-        ),
-        in_specs=[VMEM, VMEM],
-        out_specs=(VMEM, VMEM),
+            pltpu.VMEM(pages.shape, pages.dtype),
+        ),
+        in_specs=[VMEM, VMEM, HBM],
+        out_specs=(VMEM, VMEM, VMEM),
+        scratch_shapes=[pltpu.SemaphoreType.DMA],
+        compiler_params=pltpu.CompilerParams(vmem_limit_bytes=LIMIT),
         name="make_plan",
-    )(plan_src, plan_page)
+    )(plan_src, plan_page, pltpu.with_memory_space_constraint(pages, pltpu.HBM))
 
 
 def take_kernel(at_ref, from_ref, to_ref, sem):
@@ -70,9 +76,9 @@
     shape = (count,) + pages.shape[1:]
     return pl.pallas_call(
         take_kernel,
-        out_shape=jax.ShapeDtypeStruct(shape, pages.dtype),
+        out_shape=pltpu.HBM(shape, pages.dtype),
         in_specs=[SMEM, VMEM],
-        out_specs=ANY,
+        out_specs=HBM,
         scratch_shapes=[pltpu.SemaphoreType.DMA],
         compiler_params=pltpu.CompilerParams(vmem_limit_bytes=LIMIT),
         cost_estimate=pl.CostEstimate(
@@ -141,8 +147,8 @@
             jax.ShapeDtypeStruct((rows, head), jnp.bfloat16),
             jax.ShapeDtypeStruct((2 * half,) + arrived.shape[1:], arrived.dtype),
         ),
-        in_specs=[SMEM, SMEM, ANY, VMEM, VMEM] + [ANY for _ in begun],
-        out_specs=(VMEM, ANY),
+        in_specs=[SMEM, SMEM, HBM, VMEM, VMEM] + [HBM for _ in begun],
+        out_specs=(VMEM, HBM),
         input_output_aliases={5: 1} if begun else {},
         scratch_shapes=[
             pltpu.VMEM((half,) + arrived.shape[1:], arrived.dtype),
@@ -202,9 +208,9 @@
     groups = queries.shape[2] // (heads * head)
     side = lax.axis_index("tp") % 2
 
-    wanted, place = make_plan(plan_src, plan_page, devices)
+    wanted, place, held = make_plan(plan_src, plan_page, old_cache, devices)
     asked = lax.all_to_all(wanted, BOTH, split_axis=0, concat_axis=0, tiled=True)
-    outgoing = take(old_cache, asked)
+    outgoing = take(held, asked)
     outgoing = outgoing.reshape((devices, 2) + old_cache.shape[1:])
     arrived = lax.all_to_all(outgoing, BOTH, split_axis=0, concat_axis=0, tiled=True)
     arrived = arrived.reshape((devices * 2,) + old_cache.shape[1:])
@@ -219,10 +225,10 @@
 
     own, other = project(kept, partner, old_weight, steps)
     own = own + flipped(other, 1).astype(jnp.float32)
-    sent = own.astype(jnp.bfloat16)
-    parts = [flipped(sent, bits) for bits in range(2, lax.axis_size("tp"), 2)]
-    for part in parts:
-        own = own + part.astype(jnp.float32)
+    bits = 2
+    while bits < lax.axis_size("tp"):
+        own = own + flipped(own.astype(jnp.bfloat16), bits).astype(jnp.float32)
+        bits *= 2
     return own.reshape(1, steps, -1).astype(jnp.bfloat16), moved
 
 

time: 179 us -> 169 us (0.944)
  Pallas kernels: 24.3 us -> 16.2 us
  local copies, waits for them, and re-layouts: 6.03 us -> 1.93 us
  waiting for transfers between devices: 109 us -> 113 us
  starting transfers between devices: 18.5 us -> 16.2 us
    pallas_call x1, Pallas kernels: 13.6 us -> 4.86 us  [take(): pl.pallas_call(take_kernel, out_shape=pltpu.HBM(shape, pages.dtype), in_s...]
    ppermute x5 -> x4, waiting for transfers between devices: 4.47 us -> 8.61 us  [flipped(): return lax.ppermute(value, 'tp', [(i, i ^ bits) for i in range(size)])]
    unnamed x16 -> x14, local copies, waits for them, and re-layouts: 5.44 us -> 1.34 us
    ppermute x5 -> x4, starting transfers between devices: 11.4 us -> 9.17 us  [flipped(): return lax.ppermute(value, 'tp', [(i, i ^ bits) for i in range(size)])]
  transfers between devices with their start and end apart: 6 -> 5, of which waited for: 4 -> 4; matrix products, arithmetic and copies ran while one was open for 1% -> 1% of each run, Pallas kernels for 2% -> 2%
where the time goes in v3:
time: 169 us; the launch traced here: 168 us
  waiting for transfers between devices  113 us (67%)
  blocking collectives  18.2 us (11%)
  Pallas kernels  16.2 us (10%)
  starting transfers between devices  16.2 us (10%)
  local copies, waits for them, and re-layouts  1.93 us (1%)
    all_to_all x1, waiting for transfers between devices, on_device(): lax.all_to_all(outgoing, BOTH, split_axis=0, concat_axis=0, tiled=True)  104 us
    all_to_all x1, blocking collectives, on_device(): lax.all_to_all(wanted, BOTH, split_axis=0, concat_axis=0, tiled=True)  18.2 us
    ppermute x4, starting transfers between devices, flipped(): return lax.ppermute(value, 'tp', [(i, i ^ bits) for i in range(size)])  9.17 us
    ppermute x4, waiting for transfers between devices, flipped(): return lax.ppermute(value, 'tp', [(i, i ^ bits) for i in range(size)])  8.61 us
    pallas_call x2, Pallas kernels, attend(): pl.pallas_call(attend_kernel, out_shape=(jax.ShapeDtypeStruct((rows, head...  7.96 us
    all_to_all x1, starting transfers between devices, on_device(): lax.all_to_all(outgoing, BOTH, split_axis=0, concat_axis=0, tiled=True)  7 us
    pallas_call x1, Pallas kernels, take(): pl.pallas_call(take_kernel, out_shape=pltpu.HBM(shape, pages.dtype), in_s...  4.86 us
  transfers between devices with their start and end apart: 5, of which 4 were waited for; matrix products, arithmetic and copies ran while one was open for 1% of the time, Pallas kernels for 2%

profile of v3, /device:TPU:24, one launch (start us, length us, event | category | flops | bytes accessed | tf_op | source)
XLA Modules:
  0.0 167.8 jit_solution(6886804135406184468)
XLA Ops:
  0.6 0.0 copy-start
  0.7 0.7 copy-done.3
  1.3 0.7 copy-done.4
  2.0 2.2 %make_plan.1 = (s32[128,2]{1,0:T(8,128)S(1)}, s32[1,128]{1,0:T(1,128)S(1)}, bf16[128,64,256]{2,1,0:T(8,128)(2,1)S(1)}) custom-call(s32[1,128]{1,0:T(1,128)S(1)} %copy-done.3, s32[1,128]{1,0:T(1,128)S(1)} %copy-done.4, bf16[128,64,256]{2,1,0:T(8,128)(2,1)} %cache_ref.1), custom_call_target="tpu_custom_call" | custom-call | tf_op jit(solution)/shard_map/make_plan/pallas_call | solution.py:46
  4.2 18.2 %all_to_all.16 = s32[128,1,2]{2,1,0:T(1,128)S(1)} all-to-all(s32[128,1,2]{2,1,0:T(1,128)S(1)} %bitcast.24), channel_id=1, replica_groups=mesh['inst'=16,'tp'=8] {'inst','tp'}, dimensions={0} | all-to-all | bytes 2048 | tf_op jit(solution)/shard_map/all_to_all | solution.py:212
  22.4 4.9 %take_outgoing.1 = bf16[256,64,256]{2,1,0:T(8,128)(2,1)} custom-call(s32[128,2]{1,0:T(8,128)S(1)} %bitcast.21, bf16[128,64,256]{2,1,0:T(8,128)(2,1)S(1)} %get-tuple-element.13.from_ref), custom_call_target="tpu_custom_call" | custom-call | bytes 16777216 | tf_op jit(solution)/shard_map/take_outgoing/pallas_call | solution.py:77
  27.3 0.0 copy-start.1
  27.3 0.0 copy-start.2
  27.3 7.0 %all-to-all-start.1 = ((bf16[128,2,64,256]{3,2,1,0:T(8,128)(2,1)}), bf16[128,2,64,256]{3,2,1,0:T(8,128)(2,1)}, u32[]{:S(2)}, u32[]{:S(2)}) async-start(bf16[128,2,64,256]{3,2,1,0:T(8,128)(2,1)} %bitcast.27), calls=%async_computation.1 | async-start | bytes 16777216 | tf_op jit(solution)/shard_map/all_to_all | solution.py:215
  34.3 0.6 constant_dynamic-slice_fusion
  34.9 0.7 pad_add_fusion
  35.6 104.5 %all-to-all-done.1 = bf16[128,2,64,256]{3,2,1,0:T(8,128)(2,1)} async-done(((bf16[128,2,64,256]{3,2,1,0:T(8,128)(2,1)}), bf16[128,2,64,256]{3,2,1,0:T(8,128)(2,1)}, u32[]{:S(2)}, u32[]{:S(2)}) %all-to-all-start.1) | async-done | bytes 8388640 | tf_op jit(solution)/shard_map/all_to_all | solution.py:215
  140.1 4.0 %attend_other.1 = (bf16[32,128]{1,0:T(8,128)(2,1)S(1)}, bf16[128,64,256]{2,1,0:T(8,128)(2,1)}) custom-call(s32[2]{0:T(128)S(1)} %get-tuple-element.21.info_ref, s32[1,128]{1,0:T(1,128)S(1)} %get-tuple-element.11.place_ref, bf16[256,64,256]{2,1,0:T(8,128)(2,1)} %bitcast.6.pages_ref, bf16[2,32,128]{2,1,0:T(8,128)(2,1)S(1)} %bitcast.22, ...), custom_call_target="tpu_custom_call" | custom-call | flops 67108864 | bytes 4194304 | tf_op jit(solution)/shard_map/attend_other/pallas_call | solution.py:144
  144.1 0.1 collective-permute-start
  144.2 0.0 slice-start.1
  144.2 4.0 %attend_own.1 = (bf16[32,128]{1,0:T(8,128)(2,1)S(1)}, bf16[128,64,256]{2,1,0:T(8,128)(2,1)}) custom-call(s32[2]{0:T(128)S(1)} %get-tuple-element.20.info_ref, s32[1,128]{1,0:T(1,128)S(1)} %get-tuple-element.11.place_ref, bf16[256,64,256]{2,1,0:T(8,128)(2,1)} %bitcast.6.pages_ref, bf16[2,32,128]{2,1,0:T(8,128)(2,1)S(1)} %bitcast.23, ...), custom_call_target="tpu_custom_call", output_to_operand_aliasing={{1}: (5, {})} | custom-call | flops 67108864 | bytes 4194304 | tf_op jit(solution)/shard_map/attend_own/pallas_call | solution.py:144
  148.2 1.2 project.1
  149.4 2.0 %collective-permute-start.1 = (bf16[4,4096]{1,0:T(4,128)(2,1)S(1)}, bf16[4,4096]{1,0:T(4,128)(2,1)S(1)}, u32[]{:S(2)}, u32[]{:S(2)}) collective-permute-start(bf16[4,4096]{1,0:T(4,128)(2,1)S(1)} %get-tuple-element.18), channel_id=1, source_target_pairs={{0,1},{1,0},{2,3},{3,2},{4,5},{5,4},{6,7},{7,6},{8,9},{9,8},{10,11... | collective-permute-start | bytes 98312 | tf_op jit(solution)/shard_map/ppermute | solution.py:19
  151.4 1.9 %collective-permute-done.1 = bf16[4,4096]{1,0:T(4,128)(2,1)S(1)} collective-permute-done((bf16[4,4096]{1,0:T(4,128)(2,1)S(1)}, bf16[4,4096]{1,0:T(4,128)(2,1)S(1)}, u32[]{:S(2)}, u32[]{:S(2)}) %collective-permute-start.1) | collective-permute-done | bytes 32800 | tf_op jit(solution)/shard_map/ppermute | solution.py:19
  153.3 0.7 collective-permute-start.2
  154.1 4.8 %collective-permute-done.2 = bf16[4,4096]{1,0:T(4,128)(2,1)S(1)} collective-permute-done((bf16[4,4096]{1,0:T(4,128)(2,1)S(1)}, bf16[4,4096]{1,0:T(4,128)(2,1)S(1)}, u32[]{:S(2)}, u32[]{:S(2)}) %collective-permute-start.2) | collective-permute-done | bytes 32800 | tf_op jit(solution)/shard_map/ppermute | solution.py:19
  158.9 6.4 %collective-permute-start.3 = (bf16[4,4096]{1,0:T(4,128)(2,1)S(1)}, bf16[4,4096]{1,0:T(4,128)(2,1)S(1)}, u32[]{:S(2)}, u32[]{:S(2)}) collective-permute-start(bf16[4,4096]{1,0:T(4,128)(2,1)S(1)} %fusion.2), channel_id=1, source_target_pairs={{0,4},{1,5},{2,6},{3,7},{4,0},{5,1},{6,2},{7,3},{8,12},{9,13},{10,... | collective-permute-start | bytes 98312 | tf_op jit(solution)/shard_map/ppermute | solution.py:19
  165.3 1.9 %collective-permute-done.3 = bf16[4,4096]{1,0:T(4,128)(2,1)S(1)} collective-permute-done((bf16[4,4096]{1,0:T(4,128)(2,1)S(1)}, bf16[4,4096]{1,0:T(4,128)(2,1)S(1)}, u32[]{:S(2)}, u32[]{:S(2)}) %collective-permute-start.3) | collective-permute-done | bytes 32800 | tf_op jit(solution)/shard_map/ppermute | solution.py:19
  167.1 0.7 fusion.1
  (12 shorter events, 0.1 us)
Async XLA Ops:
  0.6 33.7 %copy-start = (s32[1,2,1]{1,2,0:T(1,128)S(1)}, s32[1,2,1]{1,2,0:T(1,128)}, u32[]{:S(2)}) copy-start(s32[1,2,1]{1,2,0:T(1,128)} %param.11) | copy-start | bytes 28
  0.6 0.7 copy-start.3
  1.3 0.7 copy-start.4
  27.3 112.8 %copy-start.1 = (bf16[1,4,2048]{2,1,0:T(4,128)(2,1)S(1)}, bf16[1,4,2048]{2,1,0:T(4,128)(2,1)}, u32[]{:S(2)}) copy-start(bf16[1,4,2048]{2,1,0:T(4,128)(2,1)} %param.12) | copy-start | bytes 49156
  27.3 112.8 %copy-start.2 = (bf16[1,4,512]{2,1,0:T(4,128)(2,1)S(1)}, bf16[1,4,512]{2,1,0:T(4,128)(2,1)}, u32[]{:S(2)}) copy-start(bf16[1,4,512]{2,1,0:T(4,128)(2,1)} %param.13) | copy-start | bytes 12292
  27.3 112.8 %all-to-all-start.1 = ((bf16[128,2,64,256]{3,2,1,0:T(8,128)(2,1)}), bf16[128,2,64,256]{3,2,1,0:T(8,128)(2,1)}, u32[]{:S(2)}, u32[]{:S(2)}) async-start(bf16[128,2,64,256]{3,2,1,0:T(8,128)(2,1)} %bitcast.27), calls=%async_computation.1 | async-start | bytes 16777216 | tf_op jit(solution)/shard_map/all_to_all | solution.py:215
  140.1 8.1 %slice-start = ((s8[8388608]{0:T(1024)(128)(4,1)}), s8[4194304]{0:T(1024)(128)(4,1)S(1)}, s32[]{:S(2)}) async-start(s8[8388608]{0:T(1024)(128)(4,1)} %bitcast.19), calls=%async_computation.2 | async-start | bytes 8388608
  144.1 4.1 %collective-permute-start = (bf16[32,128]{1,0:T(8,128)(2,1)S(1)}, bf16[32,128]{1,0:T(8,128)(2,1)S(1)}, u32[]{:S(2)}, u32[]{:S(2)}) collective-permute-start(bf16[32,128]{1,0:T(8,128)(2,1)S(1)} %get-tuple-element.16), channel_id=1, source_target_pairs={{0,1},{1,0},{2,3},{3,2},{4,5},{5,4},{6,7},{7,6},{8,9},{9,8},{10,11... | collective-permute-start | bytes 24584 | tf_op jit(solution)/shard_map/ppermute | solution.py:19
  144.2 4.0 %slice-start.1 = ((s8[8388608]{0:T(1024)(128)(4,1)}), s8[4194304]{0:T(1024)(128)(4,1)S(1)}, s32[]{:S(2)}) async-start(s8[8388608]{0:T(1024)(128)(4,1)} %bitcast.19), calls=%async_computation.3 | async-start | bytes 8388608
  149.4 3.9 %collective-permute-start.1 = (bf16[4,4096]{1,0:T(4,128)(2,1)S(1)}, bf16[4,4096]{1,0:T(4,128)(2,1)S(1)}, u32[]{:S(2)}, u32[]{:S(2)}) collective-permute-start(bf16[4,4096]{1,0:T(4,128)(2,1)S(1)} %get-tuple-element.18), channel_id=1, source_target_pairs={{0,1},{1,0},{2,3},{3,2},{4,5},{5,4},{6,7},{7,6},{8,9},{9,8},{10,11... | collective-permute-start | bytes 98312 | tf_op jit(solution)/shard_map/ppermute | solution.py:19
  153.3 5.5 %collective-permute-start.2 = (bf16[4,4096]{1,0:T(4,128)(2,1)S(1)}, bf16[4,4096]{1,0:T(4,128)(2,1)S(1)}, u32[]{:S(2)}, u32[]{:S(2)}) collective-permute-start(bf16[4,4096]{1,0:T(4,128)(2,1)S(1)} %fusion), channel_id=1, source_target_pairs={{0,2},{1,3},{2,0},{3,1},{4,6},{5,7},{6,4},{7,5},{8,10},{9,11},{10,... | collective-permute-start | bytes 98312 | tf_op jit(solution)/shard_map/ppermute | solution.py:19
  158.9 8.3 %collective-permute-start.3 = (bf16[4,4096]{1,0:T(4,128)(2,1)S(1)}, bf16[4,4096]{1,0:T(4,128)(2,1)S(1)}, u32[]{:S(2)}, u32[]{:S(2)}) collective-permute-start(bf16[4,4096]{1,0:T(4,128)(2,1)S(1)} %fusion.2), channel_id=1, source_target_pairs={{0,4},{1,5},{2,6},{3,7},{4,0},{5,1},{6,2},{7,3},{8,12},{9,13},{10,... | collective-permute-start | bytes 98312 | tf_op jit(solution)/shard_map/ppermute | solution.py:19

commit v4 on v3

v4 whole, which is shorter than its diff:
```python
import functools

import jax
import jax.numpy as jnp
from jax import lax
from jax.experimental import pallas as pl
from jax.experimental.pallas import tpu as pltpu
from jax.sharding import PartitionSpec as P

BOTH = ("inst", "tp")
HBM = pl.BlockSpec(memory_space=pltpu.HBM)
VMEM = pl.BlockSpec(memory_space=pltpu.VMEM)
SMEM = pl.BlockSpec(memory_space=pltpu.SMEM)
LIMIT = 24 * 1024 * 1024


def flipped(value, bits):
    size = lax.axis_size("tp")
    return lax.ppermute(value, "tp", [(i, i ^ bits) for i in range(size)])


def in_hbm(value):
    return pltpu.with_memory_space_constraint(value, pltpu.HBM)


def plan_kernel(src_hbm, page_hbm, cache_ref, wanted_ref, place_ref, held_ref, src_ref, page_ref, sems):
    copies = [
        pltpu.make_async_copy(src_hbm, src_ref, sems.at[0]),
        pltpu.make_async_copy(page_hbm, page_ref, sems.at[1]),
        pltpu.make_async_copy(cache_ref, held_ref, sems.at[2]),
    ]
    for copy in copies:
        copy.start()
    slots = src_ref.shape[1]
    sources = wanted_ref.shape[0]
    order = lax.broadcasted_iota(jnp.int32, (1, slots), 1)
    copies[0].wait()
    copies[1].wait()
    src = src_ref[...]
    coded = order * 65536 + page_ref[...]
    named = lax.broadcasted_iota(jnp.int32, (sources, slots), 0) == src
    first = jnp.min(jnp.where(named, coded, slots * 65536), axis=1, keepdims=True)
    last = jnp.max(jnp.where(named, coded, -1), axis=1, keepdims=True)
    wanted_ref[:, 0:1] = jnp.where(last >= 0, first & 65535, -1)
    wanted_ref[:, 1:2] = jnp.where(last > first, last & 65535, -1)
    rows = lax.broadcasted_iota(jnp.int32, (slots, slots), 0)
    columns = lax.broadcasted_iota(jnp.int32, (slots, slots), 1)
    src_column = jnp.max(jnp.where(rows == columns, src, 0), axis=1, keepdims=True)
    again = jnp.max(jnp.where((src_column == src) & (rows < columns), 1, 0), axis=0, keepdims=True)
    place_ref[...] = src * 2 + again
    copies[2].wait()


def make_plan(plan_src, plan_page, pages, sources):
    slots = plan_src.shape[1]
    return pl.pallas_call(
        plan_kernel,
        out_shape=(
            jax.ShapeDtypeStruct((sources, 2), jnp.int32),
            jax.ShapeDtypeStruct((1, slots), jnp.int32),
            pltpu.VMEM(pages.shape, pages.dtype),
        ),
        in_specs=[HBM, HBM, HBM],
        out_specs=(VMEM, VMEM, VMEM),
        scratch_shapes=[
            pltpu.VMEM((1, slots), jnp.int32),
            pltpu.VMEM((1, slots), jnp.int32),
            pltpu.SemaphoreType.DMA((3,)),
        ],
        compiler_params=pltpu.CompilerParams(vmem_limit_bytes=LIMIT),
        name="make_plan",
    )(in_hbm(plan_src), in_hbm(plan_page), in_hbm(pages))


def take_kernel(at_ref, from_ref, to_ref, sem):
    columns = at_ref.shape[1]

    @pl.loop(0, at_ref.shape[0], init_carry=jnp.int32(0), unroll=4)
    def started(row, count):
        for column in range(columns):
            page = at_ref[row, column]

            @pl.when(page >= 0)
            def _():
                pltpu.make_async_copy(from_ref.at[page], to_ref.at[row * columns + column], sem).start()

            count = count + (page >= 0).astype(jnp.int32)
        return count

    @pl.loop(0, started)
    def _(_):
        pltpu.make_async_copy(from_ref.at[0], to_ref.at[0], sem).wait()


def take(pages, at):
    count = at.shape[0] * at.shape[1]
    shape = (count,) + pages.shape[1:]
    return pl.pallas_call(
        take_kernel,
        out_shape=pltpu.HBM(shape, pages.dtype),
        in_specs=[SMEM, VMEM],
        out_specs=HBM,
        scratch_shapes=[pltpu.SemaphoreType.DMA],
        compiler_params=pltpu.CompilerParams(vmem_limit_bytes=LIMIT),
        cost_estimate=pl.CostEstimate(
            flops=0, bytes_accessed=count * pages.shape[1] * pages.shape[2] * 2, transcendentals=0
        ),
        name="take_outgoing",
    )(at, pages)


def hold_kernel(weight_ref, after_ref, held_ref, sem):
    copy = pltpu.make_async_copy(weight_ref, held_ref, sem)
    copy.start()
    copy.wait()


def hold(weight, after):
    return pl.pallas_call(
        hold_kernel,
        out_shape=pltpu.VMEM(weight.shape, weight.dtype),
        in_specs=[HBM, HBM],
        out_specs=VMEM,
        scratch_shapes=[pltpu.SemaphoreType.DMA],
        compiler_params=pltpu.CompilerParams(vmem_limit_bytes=LIMIT),
        cost_estimate=pl.CostEstimate(flops=0, bytes_accessed=2 * weight.size, transcendentals=0),
        name="hold_weight",
    )(in_hbm(weight), in_hbm(after))


def attention(which, length, query_ref, fresh_ref, pages_ref, ready):
    slots, page, width = pages_ref.shape
    head = width // 2
    half = slots // 2
    parts = len(ready)
    size = half // parts
    query = query_ref[which]
    fresh = fresh_ref[which]
    rows = query.shape[0]
    steps = fresh.shape[0]
    scale = head ** (-0.5)
    contract_last = (((1,), (1,)), ((), ()))
    fresh_scores = (
        lax.dot_general(query, fresh[:, :head], contract_last, preferred_element_type=jnp.float32) * scale
    )
    step_of = lax.broadcasted_iota(jnp.int32, (rows, steps), 0) % steps
    key_step = lax.broadcasted_iota(jnp.int32, (rows, steps), 1)
    fresh_scores = jnp.where(step_of >= key_step, fresh_scores, jnp.float32(-1e30))
    highest = jnp.max(fresh_scores, axis=1, keepdims=True)
    scores = []
    for part in range(parts):
        ready[part]()
        keys = pages_ref[pl.ds(which * half + part * size, size), :, :head].reshape(size * page, head)
        found = lax.dot_general(query, keys, contract_last, preferred_element_type=jnp.float32) * scale
        position = lax.broadcasted_iota(jnp.int32, found.shape, 1) + part * size * page
        found = jnp.where(position < length, found, jnp.float32(-1e30))
        highest = jnp.maximum(highest, jnp.max(found, axis=1, keepdims=True))
        scores.append(found)
    fresh_weights = jnp.exp(fresh_scores - highest)
    total = jnp.sum(fresh_weights, axis=1, keepdims=True)
    fresh_values = fresh[:, head:].astype(jnp.float32)
    mixed = jnp.zeros((rows, head), jnp.float32)
    for step in range(steps):
        mixed = mixed + fresh_weights[:, step : step + 1] * fresh_values[step : step + 1, :]
    for part in range(parts):
        weights = jnp.exp(scores[part] - highest)
        total = total + jnp.sum(weights, axis=1, keepdims=True)
        values = pages_ref[pl.ds(which * half + part * size, size), :, head:].reshape(size * page, head)
        mixed = mixed + jnp.dot(weights.astype(jnp.bfloat16), values, preferred_element_type=jnp.float32)
    return (mixed / total).astype(jnp.bfloat16)


def other_kernel(info_ref, arrived_ref, query_ref, fresh_ref, weight_ref, out_ref, pages_ref, sems):
    slots = pages_ref.shape[0]
    half = slots // 2
    parts = sems.shape[0] - 1
    size = half // parts
    which = info_ref[slots]
    length = info_ref[slots + 1]

    def gather(first, count, sem):
        @pl.loop(0, count, unroll=8)
        def _(at):
            slot = first + at
            pltpu.make_async_copy(arrived_ref.at[info_ref[slot]], pages_ref.at[slot], sem).start()

    def wait(first, count, sem):
        block = pages_ref.at[pl.ds(first, count)]
        pltpu.make_async_copy(block, block, sem).wait()

    for part in range(parts):
        gather(which * half + part * size, size, sems.at[part])
    gather((1 - which) * half, half, sems.at[parts])
    ready = [
        functools.partial(wait, which * half + part * size, size, sems.at[part]) for part in range(parts)
    ]
    out_ref[...] = attention(which, length, query_ref, fresh_ref, pages_ref, ready)
    wait((1 - which) * half, half, sems.at[parts])


def own_kernel(info_ref, pages_ref, query_ref, fresh_ref, out_ref, moved_ref, sem):
    slots = pages_ref.shape[0]
    store = pltpu.make_async_copy(pages_ref, moved_ref, sem)
    store.start()
    which = 1 - info_ref[slots]
    out_ref[...] = attention(which, info_ref[slots + 1], query_ref, fresh_ref, pages_ref, [lambda: None])
    store.wait()


def attend_cost(slots, rows, page, head):
    return pl.CostEstimate(
        flops=2 * rows * slots * page * head,
        bytes_accessed=4 * slots * page * head,
        transcendentals=rows * slots * page // 2,
    )


def attend_other(info, arrived, queries, fresh, weight):
    rows, head = queries.shape[1:]
    slots = info.shape[0] - 2
    page = arrived.shape[1]
    return pl.pallas_call(
        other_kernel,
        out_shape=(
            jax.ShapeDtypeStruct((rows, head), jnp.bfloat16),
            pltpu.VMEM((slots,) + arrived.shape[1:], arrived.dtype),
        ),
        in_specs=[SMEM, HBM, VMEM, VMEM, VMEM],
        out_specs=(VMEM, VMEM),
        scratch_shapes=[pltpu.SemaphoreType.DMA((3,))],
        compiler_params=pltpu.CompilerParams(vmem_limit_bytes=LIMIT),
        cost_estimate=attend_cost(slots, rows, page, head),
        name="attend_other",
    )(info, in_hbm(arrived), queries, fresh, weight)


def attend_own(info, pages, queries, fresh):
    rows, head = queries.shape[1:]
    return pl.pallas_call(
        own_kernel,
        out_shape=(
            jax.ShapeDtypeStruct((rows, head), jnp.bfloat16),
            pltpu.HBM(pages.shape, pages.dtype),
        ),
        in_specs=[SMEM, VMEM, VMEM, VMEM],
        out_specs=(VMEM, HBM),
        scratch_shapes=[pltpu.SemaphoreType.DMA],
        compiler_params=pltpu.CompilerParams(vmem_limit_bytes=LIMIT),
        cost_estimate=attend_cost(pages.shape[0], rows, pages.shape[1], head),
        name="attend_own",
    )(info, pages, queries, fresh)


def project_kernel(kept_ref, partner_ref, weight_ref, sum_ref, sent_ref):
    steps = sum_ref.shape[0] // 2
    rows = []
    for ref in (kept_ref, partner_ref):
        value = ref[...].astype(jnp.float32)
        rows.append(
            jnp.concatenate([value[at : at + steps] for at in range(0, value.shape[0], steps)], axis=1)
        )
    both = jnp.concatenate(rows, axis=0).astype(jnp.bfloat16)
    tile = 1024
    for at in range(0, weight_ref.shape[1], tile):
        product = jnp.dot(both, weight_ref[:, at : at + tile], preferred_element_type=jnp.float32)
        sum_ref[:, at : at + tile] = product
        turned = jnp.concatenate([product[steps:], product[:steps]], axis=0)
        sent_ref[:, at : at + tile] = turned.astype(jnp.bfloat16)


def project(kept, partner, weight, steps):
    wide = weight.shape[1]
    return pl.pallas_call(
        project_kernel,
        out_shape=(
            jax.ShapeDtypeStruct((2 * steps, wide), jnp.float32),
            jax.ShapeDtypeStruct((2 * steps, wide), jnp.bfloat16),
        ),
        in_specs=[VMEM, VMEM, VMEM],
        out_specs=(VMEM, VMEM),
        compiler_params=pltpu.CompilerParams(vmem_limit_bytes=LIMIT),
        cost_estimate=pl.CostEstimate(
            flops=4 * steps * weight.size, bytes_accessed=weight.size * 2, transcendentals=0
        ),
        name="project",
    )(kept, partner, weight)


def on_device(old_cache, old_weight, plan_src, plan_page, lengths, queries, new_kv):
    devices = lax.axis_size("inst") * lax.axis_size("tp")
    steps = queries.shape[1]
    width = old_cache.shape[2]
    heads = new_kv.shape[2] // width
    head = width // 2
    groups = queries.shape[2] // (heads * head)
    side = lax.axis_index("tp") % 2

    wanted, place, held = make_plan(plan_src, plan_page, old_cache, devices)
    asked = lax.all_to_all(wanted, BOTH, split_axis=0, concat_axis=0, tiled=True)
    taken = take(held, asked)
    outgoing = taken.reshape((devices, 2) + old_cache.shape[1:])
    arrived = lax.all_to_all(outgoing, BOTH, split_axis=0, concat_axis=0, tiled=True)
    arrived = arrived.reshape((devices * 2,) + old_cache.shape[1:])
    weight = hold(old_weight, taken)

    rows = queries.reshape(steps, heads, groups, head).transpose(1, 2, 0, 3)
    rows = rows.reshape(heads, groups * steps, head)
    fresh = new_kv.reshape(steps, heads, width).transpose(1, 0, 2)
    length = lax.dynamic_index_in_dim(lengths[0, :, 0], side, 0, keepdims=False)
    info = jnp.concatenate([place[0], jnp.stack([1 - side, length]).astype(jnp.int32)])
    passed, pages = attend_other(info, arrived, rows, fresh, weight)
    partner = flipped(passed, 1)
    kept, moved = attend_own(info, pages, rows, fresh)

    total, sent = project(kept, partner, weight, steps)
    total = total + flipped(sent, 1).astype(jnp.float32)
    own = total[:steps] + flipped(total[steps:].astype(jnp.bfloat16), 3).astype(jnp.float32)
    bits = 4
    while bits < lax.axis_size("tp"):
        own = own + flipped(own.astype(jnp.bfloat16), bits).astype(jnp.float32)
        bits *= 2
    return own.reshape(1, steps, -1).astype(jnp.bfloat16), moved


def solution(mesh):
    placed = (
        P(BOTH, None, None),
        P("tp", None),
        P(BOTH, None),
        P(BOTH, None),
        P("inst", None, None),
        P(BOTH, None, None),
        P(BOTH, None, None),
    )
    return jax.shard_map(
        on_device,
        mesh=mesh,
        in_specs=placed,
        out_specs=(P(BOTH, None, None), P(BOTH, None, None)),
        check_vma=False,
    )
```

time: 169 us -> 168 us (level)
  local copies, waits for them, and re-layouts: 1.93 us -> 7.22 us
  waiting for transfers between devices: 113 us -> 109 us
    all_to_all x1, waiting for transfers between devices: 104 us -> 97.8 us  [on_device(): lax.all_to_all(outgoing, BOTH, split_axis=0, concat_axis=0, tiled=True)]
    unnamed x14 -> x12, local copies, waits for them, and re-layouts: 1.34 us -> 6.61 us
    ppermute x4, waiting for transfers between devices: 8.61 us -> 11.4 us  [flipped(): return lax.ppermute(value, 'tp', [(i, i ^ bits) for i in range(size)])]
    pallas_call x3 -> x4, Pallas kernels: 9.17 us -> 10.2 us  [the longest x1 3.41 us: hold(): pl.pallas_call(hold_kernel, out_shape=pltpu.VMEM(weight.shape, weight.dty...]
  transfers between devices with their start and end apart: 5 -> 5, of which waited for: 4 -> 5; matrix products, arithmetic and copies ran while one was open for 1% -> 1% of each run, Pallas kernels for 2% -> 4%
where the time goes in v4:
time: 168 us; the launch traced here: 167 us
  waiting for transfers between devices  109 us (65%)
  blocking collectives  18.2 us (11%)
  Pallas kernels  16.1 us (10%)
  starting transfers between devices  14.6 us (9%)
  local copies, waits for them, and re-layouts  7.22 us (4%)
    all_to_all x1, waiting for transfers between devices, on_device(): lax.all_to_all(outgoing, BOTH, split_axis=0, concat_axis=0, tiled=True)  97.8 us
    all_to_all x1, blocking collectives, on_device(): lax.all_to_all(wanted, BOTH, split_axis=0, concat_axis=0, tiled=True)  18.2 us
    ppermute x4, waiting for transfers between devices, flipped(): return lax.ppermute(value, 'tp', [(i, i ^ bits) for i in range(size)])  11.4 us
    ppermute x4, starting transfers between devices, flipped(): return lax.ppermute(value, 'tp', [(i, i ^ bits) for i in range(size)])  7.53 us
    all_to_all x1, starting transfers between devices, on_device(): lax.all_to_all(outgoing, BOTH, split_axis=0, concat_axis=0, tiled=True)  7.02 us
    unnamed x12, local copies, waits for them, and re-layouts  6.61 us
    pallas_call x1, Pallas kernels, take(): pl.pallas_call(take_kernel, out_shape=pltpu.HBM(shape, pages.dtype), in_s...  3.63 us
    pallas_call x1, Pallas kernels, hold(): pl.pallas_call(hold_kernel, out_shape=pltpu.VMEM(weight.shape, weight.dty...  3.41 us
  transfers between devices with their start and end apart: 5, of which 5 were waited for; matrix products, arithmetic and copies ran while one was open for 1% of the time, Pallas kernels for 4%

profile of v4, /device:TPU:24, one launch (start us, length us, event | category | flops | bytes accessed | tf_op | source)
XLA Modules:
  0.0 167.4 jit_solution(1658043748198243765)
XLA Ops:
  0.6 0.0 copy-start
  0.6 2.3 %make_plan.1 = (s32[128,2]{1,0:T(8,128)S(1)}, s32[1,128]{1,0:T(1,128)S(1)}, bf16[128,64,256]{2,1,0:T(8,128)(2,1)S(1)}) custom-call(s32[1,128]{1,0:T(1,128)} %src_hbm.1, s32[1,128]{1,0:T(1,128)} %page_hbm.1, bf16[128,64,256]{2,1,0:T(8,128)(2,1)} %cache_ref.1), custom_call_target="tpu_custom_call" | custom-call | tf_op jit(solution)/shard_map/make_plan/pallas_call | solution.py:56
  2.9 18.2 %all_to_all.16 = s32[128,1,2]{2,1,0:T(1,128)S(1)} all-to-all(s32[128,1,2]{2,1,0:T(1,128)S(1)} %bitcast.20), channel_id=1, replica_groups=mesh['inst'=16,'tp'=8] {'inst','tp'}, dimensions={0} | all-to-all | bytes 2048 | tf_op jit(solution)/shard_map/all_to_all | solution.py:299
  21.1 3.6 %take_outgoing.1.after_ref = bf16[256,64,256]{2,1,0:T(8,128)(2,1)} custom-call(s32[128,2]{1,0:T(8,128)S(1)} %bitcast.19, bf16[128,64,256]{2,1,0:T(8,128)(2,1)S(1)} %get-tuple-element.13.from_ref), custom_call_target="tpu_custom_call" | custom-call | bytes 8388608 | tf_op jit(solution)/shard_map/take_outgoing/pallas_call | solution.py:98
  24.8 7.0 %all-to-all-start.1 = ((bf16[128,2,64,256]{3,2,1,0:T(8,128)(2,1)}), bf16[128,2,64,256]{3,2,1,0:T(8,128)(2,1)}, u32[]{:S(2)}, u32[]{:S(2)}) async-start(bf16[128,2,64,256]{3,2,1,0:T(8,128)(2,1)} %bitcast.26), calls=%async_computation.1 | async-start | bytes 16777216 | tf_op jit(solution)/shard_map/all_to_all | solution.py:302
  31.8 0.6 constant_dynamic-slice_fusion
  32.4 0.7 pad_add_fusion.info_ref
  33.1 3.4 %hold_weight.1.weight_ref = bf16[1024,4096]{1,0:T(8,128)(2,1)S(1)} custom-call(bf16[1024,4096]{1,0:T(8,128)(2,1)} %weight_ref.1, bf16[256,64,256]{2,1,0:T(8,128)(2,1)} %take_outgoing.1.after_ref), custom_call_target="tpu_custom_call" | custom-call | bytes 8388608 | tf_op jit(solution)/shard_map/hold_weight/pallas_call | solution.py:119
  36.5 0.0 copy-start.1
  36.6 3.2 %copy-done.1 = bf16[1024,4096]{1,0:T(8,128)(2,1)} copy-done((bf16[1024,4096]{1,0:T(8,128)(2,1)}, bf16[1024,4096]{1,0:T(8,128)(2,1)S(1)}, u32[]{:S(2)}) %copy-start.1) | copy-done | bytes 8388632
  39.8 97.8 %all-to-all-done.1 = bf16[128,2,64,256]{3,2,1,0:T(8,128)(2,1)} async-done(((bf16[128,2,64,256]{3,2,1,0:T(8,128)(2,1)}), bf16[128,2,64,256]{3,2,1,0:T(8,128)(2,1)}, u32[]{:S(2)}, u32[]{:S(2)}) %all-to-all-start.1) | async-done | bytes 8388640 | tf_op jit(solution)/shard_map/all_to_all | solution.py:302
  137.6 3.4 %copy-done.2 = bf16[1024,4096]{1,0:T(8,128)(2,1)S(1)} copy-done((bf16[1024,4096]{1,0:T(8,128)(2,1)S(1)}, bf16[1024,4096]{1,0:T(8,128)(2,1)}, u32[]{:S(2)}) %copy-start.2) | copy-done | bytes 8388632
  141.0 3.0 %attend_other.1 = (bf16[32,128]{1,0:T(8,128)(2,1)S(1)}, bf16[128,64,256]{2,1,0:T(8,128)(2,1)S(1)}) custom-call(s32[130]{0:T(256)S(1)} %pad_add_fusion.info_ref, bf16[256,64,256]{2,1,0:T(8,128)(2,1)} %bitcast.7.arrived_ref, bf16[2,32,128]{2,1,0:T(8,128)(2,1)S(1)} %bitcast.21, bf16[2,4,256]{2,1,0:T(4,128)(2,1)S(1)} %bitcast.23, bf16[1024,4096]{1,0:T(8,128)(2,1)S(1)} %copy-done.2), custom_call_target="tpu_custom_call" | custom-call | flops 67108864 | bytes 4194304 | tf_op jit(solution)/shard_map/attend_other/pallas_call | solution.py:222
  144.0 0.1 collective-permute-start
  144.1 2.6 %attend_own.1 = (bf16[32,128]{1,0:T(8,128)(2,1)S(1)}, bf16[128,64,256]{2,1,0:T(8,128)(2,1)}) custom-call(s32[130]{0:T(256)S(1)} %pad_add_fusion.info_ref, bf16[128,64,256]{2,1,0:T(8,128)(2,1)S(1)} %get-tuple-element.14.pages_ref, bf16[2,32,128]{2,1,0:T(8,128)(2,1)S(1)} %bitcast.22, bf16[2,4,256]{2,1,0:T(4,128)(2,1)S(1)} %bitcast.24), custom_call_target="tpu_custom_call" | custom-call | flops 67108864 | bytes 4194304 | tf_op jit(solution)/shard_map/attend_own/pallas_call | solution.py:239
  146.7 1.1 collective-permute-done.partner_ref
  147.7 1.2 project.1
  148.9 1.0 collective-permute-start.1
  149.9 3.3 %collective-permute-done.1 = bf16[8,4096]{1,0:T(8,128)(2,1)S(1)} collective-permute-done((bf16[8,4096]{1,0:T(8,128)(2,1)S(1)}, bf16[8,4096]{1,0:T(8,128)(2,1)S(1)}, u32[]{:S(2)}, u32[]{:S(2)}) %collective-permute-start.1) | collective-permute-done | bytes 65568 | tf_op jit(solution)/shard_map/ppermute | solution.py:19
  153.2 0.1 collective-permute-start.2
  153.3 5.1 %collective-permute-done.2 = bf16[4,4096]{1,0:T(4,128)(2,1)S(1)} collective-permute-done((bf16[4,4096]{1,0:T(4,128)(2,1)S(1)}, bf16[4,4096]{1,0:T(4,128)(2,1)S(1)}, u32[]{:S(2)}, u32[]{:S(2)}) %collective-permute-start.2) | collective-permute-done | bytes 32800 | tf_op jit(solution)/shard_map/ppermute | solution.py:19
  158.5 6.4 %collective-permute-start.3 = (bf16[4,4096]{1,0:T(4,128)(2,1)S(1)}, bf16[4,4096]{1,0:T(4,128)(2,1)S(1)}, u32[]{:S(2)}, u32[]{:S(2)}) collective-permute-start(bf16[4,4096]{1,0:T(4,128)(2,1)S(1)} %fusion), channel_id=1, source_target_pairs={{0,4},{1,5},{2,6},{3,7},{4,0},{5,1},{6,2},{7,3},{8,12},{9,13},{10,... | collective-permute-start | bytes 98312 | tf_op jit(solution)/shard_map/ppermute | solution.py:19
  164.8 1.9 %collective-permute-done.3 = bf16[4,4096]{1,0:T(4,128)(2,1)S(1)} collective-permute-done((bf16[4,4096]{1,0:T(4,128)(2,1)S(1)}, bf16[4,4096]{1,0:T(4,128)(2,1)S(1)}, u32[]{:S(2)}, u32[]{:S(2)}) %collective-permute-start.3) | collective-permute-done | bytes 32800 | tf_op jit(solution)/shard_map/ppermute | solution.py:19
  166.7 0.6 fusion.1
  (11 shorter events, 0.1 us)
Async XLA Ops:
  0.6 31.2 %copy-start = (s32[1,2,1]{1,2,0:T(1,128)S(1)}, s32[1,2,1]{1,2,0:T(1,128)}, u32[]{:S(2)}) copy-start(s32[1,2,1]{1,2,0:T(1,128)} %param.11) | copy-start | bytes 28
  24.8 112.8 %all-to-all-start.1 = ((bf16[128,2,64,256]{3,2,1,0:T(8,128)(2,1)}), bf16[128,2,64,256]{3,2,1,0:T(8,128)(2,1)}, u32[]{:S(2)}, u32[]{:S(2)}) async-start(bf16[128,2,64,256]{3,2,1,0:T(8,128)(2,1)} %bitcast.26), calls=%async_computation.1 | async-start | bytes 16777216 | tf_op jit(solution)/shard_map/all_to_all | solution.py:302
  33.1 104.5 %copy-start.4 = (bf16[1,4,2048]{2,1,0:T(4,128)(2,1)S(1)}, bf16[1,4,2048]{2,1,0:T(4,128)(2,1)}, u32[]{:S(2)}) copy-start(bf16[1,4,2048]{2,1,0:T(4,128)(2,1)} %param.12) | copy-start | bytes 49156
  33.1 104.5 %copy-start.5 = (bf16[1,4,512]{2,1,0:T(4,128)(2,1)S(1)}, bf16[1,4,512]{2,1,0:T(4,128)(2,1)}, u32[]{:S(2)}) copy-start(bf16[1,4,512]{2,1,0:T(4,128)(2,1)} %param.13) | copy-start | bytes 12292
  36.5 3.2 %copy-start.1 = (bf16[1024,4096]{1,0:T(8,128)(2,1)}, bf16[1024,4096]{1,0:T(8,128)(2,1)S(1)}, u32[]{:S(2)}) copy-start(bf16[1024,4096]{1,0:T(8,128)(2,1)S(1)} %hold_weight.1.weight_ref) | copy-start | bytes 25165828
  137.6 3.4 %copy-start.2 = (bf16[1024,4096]{1,0:T(8,128)(2,1)S(1)}, bf16[1024,4096]{1,0:T(8,128)(2,1)}, u32[]{:S(2)}) copy-start(bf16[1024,4096]{1,0:T(8,128)(2,1)} %copy-done.1) | copy-start | bytes 25165828
  141.0 6.7 %copy-start.3 = (bf16[1024,4096]{1,0:T(8,128)(2,1)S(1)}, bf16[1024,4096]{1,0:T(8,128)(2,1)}, u32[]{:S(2)}) copy-start(bf16[1024,4096]{1,0:T(8,128)(2,1)} %copy-done.1) | copy-start | bytes 25165828
  144.0 3.7 %collective-permute-start = (bf16[32,128]{1,0:T(8,128)(2,1)S(1)}, bf16[32,128]{1,0:T(8,128)(2,1)S(1)}, u32[]{:S(2)}, u32[]{:S(2)}) collective-permute-start(bf16[32,128]{1,0:T(8,128)(2,1)S(1)} %get-tuple-element.16), channel_id=1, source_target_pairs={{0,1},{1,0},{2,3},{3,2},{4,5},{5,4},{6,7},{7,6},{8,9},{9,8},{10,11... | collective-permute-start | bytes 24584 | tf_op jit(solution)/shard_map/ppermute | solution.py:19
  148.9 4.3 %collective-permute-start.1 = (bf16[8,4096]{1,0:T(8,128)(2,1)S(1)}, bf16[8,4096]{1,0:T(8,128)(2,1)S(1)}, u32[]{:S(2)}, u32[]{:S(2)}) collective-permute-start(bf16[8,4096]{1,0:T(8,128)(2,1)S(1)} %get-tuple-element.18), channel_id=1, source_target_pairs={{0,1},{1,0},{2,3},{3,2},{4,5},{5,4},{6,7},{7,6},{8,9},{9,8},{10,11... | collective-permute-start | bytes 196616 | tf_op jit(solution)/shard_map/ppermute | solution.py:19
  153.2 5.2 %collective-permute-start.2 = (bf16[4,4096]{1,0:T(4,128)(2,1)S(1)}, bf16[4,4096]{1,0:T(4,128)(2,1)S(1)}, u32[]{:S(2)}, u32[]{:S(2)}) collective-permute-start(bf16[4,4096]{1,0:T(4,128)(2,1)S(1)} %slice.19), channel_id=1, source_target_pairs={{0,3},{1,2},{2,1},{3,0},{4,7},{5,6},{6,5},{7,4},{8,11},{9,10},{10,... | collective-permute-start | bytes 98312 | tf_op jit(solution)/shard_map/ppermute | solution.py:19
  158.5 8.3 %collective-permute-start.3 = (bf16[4,4096]{1,0:T(4,128)(2,1)S(1)}, bf16[4,4096]{1,0:T(4,128)(2,1)S(1)}, u32[]{:S(2)}, u32[]{:S(2)}) collective-permute-start(bf16[4,4096]{1,0:T(4,128)(2,1)S(1)} %fusion), channel_id=1, source_target_pairs={{0,4},{1,5},{2,6},{3,7},{4,0},{5,1},{6,2},{7,3},{8,12},{9,13},{10,... | collective-permute-start | bytes 98312 | tf_op jit(solution)/shard_map/ppermute | solution.py:19

commit v5 on v4

--- a/solution.py
+++ b/solution.py
@@ -11,7 +11,7 @@
 HBM = pl.BlockSpec(memory_space=pltpu.HBM)
 VMEM = pl.BlockSpec(memory_space=pltpu.VMEM)
 SMEM = pl.BlockSpec(memory_space=pltpu.SMEM)
-LIMIT = 24 * 1024 * 1024
+LIMIT = 6 * 1024 * 1024
 
 
 def flipped(value, bits):
@@ -21,6 +21,10 @@
 
 def in_hbm(value):
     return pltpu.with_memory_space_constraint(value, pltpu.HBM)
+
+
+def in_vmem(value):
+    return pltpu.with_memory_space_constraint(value, pltpu.VMEM)
 
 
 def plan_kernel(src_hbm, page_hbm, cache_ref, wanted_ref, place_ref, held_ref, src_ref, page_ref, sems):
@@ -106,26 +110,7 @@
             flops=0, bytes_accessed=count * pages.shape[1] * pages.shape[2] * 2, transcendentals=0
         ),
         name="take_outgoing",
-    )(at, pages)
-
-
-def hold_kernel(weight_ref, after_ref, held_ref, sem):
-    copy = pltpu.make_async_copy(weight_ref, held_ref, sem)
-    copy.start()
-    copy.wait()
-
-
-def hold(weight, after):
-    return pl.pallas_call(
-        hold_kernel,
-        out_shape=pltpu.VMEM(weight.shape, weight.dtype),
-        in_specs=[HBM, HBM],
-        out_specs=VMEM,
-        scratch_shapes=[pltpu.SemaphoreType.DMA],
-        compiler_params=pltpu.CompilerParams(vmem_limit_bytes=LIMIT),
-        cost_estimate=pl.CostEstimate(flops=0, bytes_accessed=2 * weight.size, transcendentals=0),
-        name="hold_weight",
-    )(in_hbm(weight), in_hbm(after))
+    )(at, in_vmem(pages))
 
 
 def attention(which, length, query_ref, fresh_ref, pages_ref, ready):
@@ -170,7 +155,8 @@
     return (mixed / total).astype(jnp.bfloat16)
 
 
-def other_kernel(info_ref, arrived_ref, query_ref, fresh_ref, weight_ref, out_ref, pages_ref, sems):
+def other_kernel(info_ref, arrived_ref, query_ref, fresh_ref, weight_ref, *rest):
+    out_ref, pages_ref, held_ref, sems, held_sem = rest
     slots = pages_ref.shape[0]
     half = slots // 2
     parts = sems.shape[0] - 1
@@ -191,20 +177,27 @@
     for part in range(parts):
         gather(which * half + part * size, size, sems.at[part])
     gather((1 - which) * half, half, sems.at[parts])
+    hold = pltpu.make_async_copy(weight_ref.at[pl.ds(0, held_ref.shape[0])], held_ref, held_sem)
+    hold.start()
     ready = [
         functools.partial(wait, which * half + part * size, size, sems.at[part]) for part in range(parts)
     ]
     out_ref[...] = attention(which, length, query_ref, fresh_ref, pages_ref, ready)
     wait((1 - which) * half, half, sems.at[parts])
-
-
-def own_kernel(info_ref, pages_ref, query_ref, fresh_ref, out_ref, moved_ref, sem):
+    hold.wait()
+
+
+def own_kernel(info_ref, pages_ref, query_ref, fresh_ref, weight_ref, *rest):
+    out_ref, held_ref, held_sem = rest
     slots = pages_ref.shape[0]
-    store = pltpu.make_async_copy(pages_ref, moved_ref, sem)
-    store.start()
+    count = held_ref.shape[0]
+    hold = pltpu.make_async_copy(
+        weight_ref.at[pl.ds(weight_ref.shape[0] - count, count)], held_ref, held_sem
+    )
+    hold.start()
     which = 1 - info_ref[slots]
     out_ref[...] = attention(which, info_ref[slots + 1], query_ref, fresh_ref, pages_ref, [lambda: None])
-    store.wait()
+    hold.wait()
 
 
 def attend_cost(slots, rows, page, head):
@@ -215,7 +208,7 @@
     )
 
 
-def attend_other(info, arrived, queries, fresh, weight):
+def attend_other(info, arrived, queries, fresh, weight, count):
     rows, head = queries.shape[1:]
     slots = info.shape[0] - 2
     page = arrived.shape[1]
@@ -224,34 +217,54 @@
         out_shape=(
             jax.ShapeDtypeStruct((rows, head), jnp.bfloat16),
             pltpu.VMEM((slots,) + arrived.shape[1:], arrived.dtype),
-        ),
-        in_specs=[SMEM, HBM, VMEM, VMEM, VMEM],
-        out_specs=(VMEM, VMEM),
-        scratch_shapes=[pltpu.SemaphoreType.DMA((3,))],
+            pltpu.VMEM((count, weight.shape[1]), weight.dtype),
+        ),
+        in_specs=[SMEM, HBM, VMEM, VMEM, HBM],
+        out_specs=(VMEM, VMEM, VMEM),
+        scratch_shapes=[pltpu.SemaphoreType.DMA((3,)), pltpu.SemaphoreType.DMA],
         compiler_params=pltpu.CompilerParams(vmem_limit_bytes=LIMIT),
         cost_estimate=attend_cost(slots, rows, page, head),
         name="attend_other",
-    )(info, in_hbm(arrived), queries, fresh, weight)
-
-
-def attend_own(info, pages, queries, fresh):
+    )(info, in_hbm(arrived), queries, fresh, in_hbm(weight))
+
+
+def attend_own(info, pages, queries, fresh, weight, count):
     rows, head = queries.shape[1:]
     return pl.pallas_call(
         own_kernel,
         out_shape=(
             jax.ShapeDtypeStruct((rows, head), jnp.bfloat16),
-            pltpu.HBM(pages.shape, pages.dtype),
-        ),
-        in_specs=[SMEM, VMEM, VMEM, VMEM],
-        out_specs=(VMEM, HBM),
+            pltpu.VMEM((count, weight.shape[1]), weight.dtype),
+        ),
+        in_specs=[SMEM, VMEM, VMEM, VMEM, HBM],
+        out_specs=(VMEM, VMEM),
         scratch_shapes=[pltpu.SemaphoreType.DMA],
         compiler_params=pltpu.CompilerParams(vmem_limit_bytes=LIMIT),
         cost_estimate=attend_cost(pages.shape[0], rows, pages.shape[1], head),
         name="attend_own",
-    )(info, pages, queries, fresh)
-
-
-def project_kernel(kept_ref, partner_ref, weight_ref, sum_ref, sent_ref):
+    )(info, in_vmem(pages), queries, fresh, in_hbm(weight))
+
+
+def store_kernel(pages_ref, _, moved_ref, sem):
+    copy = pltpu.make_async_copy(pages_ref, moved_ref, sem)
+    copy.start()
+    copy.wait()
+
+
+def store(pages, after):
+    return pl.pallas_call(
+        store_kernel,
+        out_shape=pltpu.HBM(pages.shape, pages.dtype),
+        in_specs=[VMEM, VMEM],
+        out_specs=HBM,
+        scratch_shapes=[pltpu.SemaphoreType.DMA],
+        compiler_params=pltpu.CompilerParams(vmem_limit_bytes=LIMIT),
+        cost_estimate=pl.CostEstimate(flops=0, bytes_accessed=2 * pages.size, transcendentals=0),
+        name="store_moved",
+    )(in_vmem(pages), in_vmem(after))
+
+
+def project_kernel(kept_ref, partner_ref, first_ref, second_ref, sum_ref, sent_ref):
     steps = sum_ref.shape[0] // 2
     rows = []
     for ref in (kept_ref, partner_ref):
@@ -261,29 +274,35 @@
         )
     both = jnp.concatenate(rows, axis=0).astype(jnp.bfloat16)
     tile = 1024
-    for at in range(0, weight_ref.shape[1], tile):
-        product = jnp.dot(both, weight_ref[:, at : at + tile], preferred_element_type=jnp.float32)
+    cut = first_ref.shape[0]
+    for at in range(0, first_ref.shape[1], tile):
+        product = jnp.dot(both[:, :cut], first_ref[:, at : at + tile], preferred_element_type=jnp.float32)
+        product = product + jnp.dot(
+            both[:, cut:], second_ref[:, at : at + tile], preferred_element_type=jnp.float32
+        )
         sum_ref[:, at : at + tile] = product
         turned = jnp.concatenate([product[steps:], product[:steps]], axis=0)
         sent_ref[:, at : at + tile] = turned.astype(jnp.bfloat16)
 
 
-def project(kept, partner, weight, steps):
-    wide = weight.shape[1]
+def project(kept, partner, first, second, steps):
+    wide = first.shape[1]
     return pl.pallas_call(
         project_kernel,
         out_shape=(
             jax.ShapeDtypeStruct((2 * steps, wide), jnp.float32),
             jax.ShapeDtypeStruct((2 * steps, wide), jnp.bfloat16),
         ),
-        in_specs=[VMEM, VMEM, VMEM],
+        in_specs=[VMEM, VMEM, VMEM, VMEM],
         out_specs=(VMEM, VMEM),
         compiler_params=pltpu.CompilerParams(vmem_limit_bytes=LIMIT),
         cost_estimate=pl.CostEstimate(
-            flops=4 * steps * weight.size, bytes_accessed=weight.size * 2, transcendentals=0
+            flops=4 * steps * (first.size + second.size),
+            bytes_accessed=2 * (first.size + second.size),
+            transcendentals=0,
         ),
         name="project",
-    )(kept, partner, weight)
+    )(kept, partner, in_vmem(first), in_vmem(second))
 
 
 def on_device(old_cache, old_weight, plan_src, plan_page, lengths, queries, new_kv):
@@ -301,24 +320,27 @@
     outgoing = taken.reshape((devices, 2) + old_cache.shape[1:])
     arrived = lax.all_to_all(outgoing, BOTH, split_axis=0, concat_axis=0, tiled=True)
     arrived = arrived.reshape((devices * 2,) + old_cache.shape[1:])
-    weight = hold(old_weight, taken)
 
     rows = queries.reshape(steps, heads, groups, head).transpose(1, 2, 0, 3)
     rows = rows.reshape(heads, groups * steps, head)
     fresh = new_kv.reshape(steps, heads, width).transpose(1, 0, 2)
     length = lax.dynamic_index_in_dim(lengths[0, :, 0], side, 0, keepdims=False)
     info = jnp.concatenate([place[0], jnp.stack([1 - side, length]).astype(jnp.int32)])
-    passed, pages = attend_other(info, arrived, rows, fresh, weight)
+    early = old_weight.shape[0] // 4
+    passed, pages, first = attend_other(info, arrived, rows, fresh, old_weight, early)
     partner = flipped(passed, 1)
-    kept, moved = attend_own(info, pages, rows, fresh)
-
-    total, sent = project(kept, partner, weight, steps)
+    kept, second = attend_own(info, pages, rows, fresh, old_weight, old_weight.shape[0] - early)
+
+    total, sent = project(kept, partner, first, second, steps)
+    moved = store(pages, sent)
     total = total + flipped(sent, 1).astype(jnp.float32)
-    own = total[:steps] + flipped(total[steps:].astype(jnp.bfloat16), 3).astype(jnp.float32)
-    bits = 4
-    while bits < lax.axis_size("tp"):
-        own = own + flipped(own.astype(jnp.bfloat16), bits).astype(jnp.float32)
-        bits *= 2
+    rounded = total.astype(jnp.bfloat16)
+    own = total[:steps]
+    for high in range(0, lax.axis_size("tp"), 4):
+        for low in (0, 3):
+            if high + low:
+                rows = rounded[:steps] if low == 0 else rounded[steps:]
+                own = own + flipped(rows, high + low).astype(jnp.float32)
     return own.reshape(1, steps, -1).astype(jnp.bfloat16), moved
 
 

time: 168 us -> 165 us (0.982)
  local copies, waits for them, and re-layouts: 7.22 us -> 0.63 us
  starting transfers between devices: 14.6 us -> 17.9 us
    all_to_all x1, waiting for transfers between devices: 97.8 us -> 104 us  [on_device(): lax.all_to_all(outgoing, BOTH, split_axis=0, concat_axis=0, tiled=True)]
    unnamed x12 -> x6, local copies, waits for them, and re-layouts: 6.61 us -> 0.02 us
    ppermute x4 -> x5, waiting for transfers between devices: 11.4 us -> 5.71 us  [flipped(): return lax.ppermute(value, 'tp', [(i, i ^ bits) for i in range(size)])]
    ppermute x4 -> x5, starting transfers between devices: 7.53 us -> 10.8 us  [flipped(): return lax.ppermute(value, 'tp', [(i, i ^ bits) for i in range(size)])]
  transfers between devices with their start and end apart: 5 -> 6, of which waited for: 5 -> 4; matrix products, arithmetic and copies ran while one was open for 1% -> 1% of each run, Pallas kernels for 4% -> 3%
where the time goes in v5:
time: 165 us
  waiting for transfers between devices  110 us (67%)
  blocking collectives  18.2 us (11%)
  starting transfers between devices  17.9 us (11%)
  Pallas kernels  16.1 us (10%)
    all_to_all x1, waiting for transfers between devices, on_device(): lax.all_to_all(outgoing, BOTH, split_axis=0, concat_axis=0, tiled=True)  104 us
    all_to_all x1, blocking collectives, on_device(): lax.all_to_all(wanted, BOTH, split_axis=0, concat_axis=0, tiled=True)  18.2 us
    ppermute x5, starting transfers between devices, flipped(): return lax.ppermute(value, 'tp', [(i, i ^ bits) for i in range(size)])  10.8 us
    all_to_all x1, starting transfers between devices, on_device(): lax.all_to_all(outgoing, BOTH, split_axis=0, concat_axis=0, tiled=True)  7.06 us
    ppermute x5, waiting for transfers between devices, flipped(): return lax.ppermute(value, 'tp', [(i, i ^ bits) for i in range(size)])  5.71 us
    pallas_call x1, Pallas kernels, attend_other(): pl.pallas_call(other_kernel, out_shape=(jax.ShapeDtypeStruct((rows, head)...  3.63 us
    pallas_call x1, Pallas kernels, take(): pl.pallas_call(take_kernel, out_shape=pltpu.HBM(shape, pages.dtype), in_s...  3.62 us
    pallas_call x1, Pallas kernels, attend_own(): pl.pallas_call(own_kernel, out_shape=(jax.ShapeDtypeStruct((rows, head),...  3.34 us
  transfers between devices with their start and end apart: 6, of which 4 were waited for; matrix products, arithmetic and copies ran while one was open for 1% of the time, Pallas kernels for 3%

profile of v5, /device:TPU:24, one launch (start us, length us, event | category | flops | bytes accessed | tf_op | source)
XLA Modules:
  0.0 165.1 jit_solution(11804575827267471044)
XLA Ops:
  0.6 0.0 copy-start
  0.6 2.3 %make_plan.1 = (s32[128,2]{1,0:T(8,128)S(1)}, s32[1,128]{1,0:T(1,128)S(1)}, bf16[128,64,256]{2,1,0:T(8,128)(2,1)S(1)}) custom-call(s32[1,128]{1,0:T(1,128)} %src_hbm.1, s32[1,128]{1,0:T(1,128)} %page_hbm.1, bf16[128,64,256]{2,1,0:T(8,128)(2,1)} %cache_ref.1), custom_call_target="tpu_custom_call" | custom-call | tf_op jit(solution)/shard_map/make_plan/pallas_call | solution.py:60
  2.9 18.2 %all_to_all.16 = s32[128,1,2]{2,1,0:T(1,128)S(1)} all-to-all(s32[128,1,2]{2,1,0:T(1,128)S(1)} %bitcast.20), channel_id=1, replica_groups=mesh['inst'=16,'tp'=8] {'inst','tp'}, dimensions={0} | all-to-all | bytes 2048 | tf_op jit(solution)/shard_map/all_to_all | solution.py:318
  21.1 3.6 %take_outgoing.1 = bf16[256,64,256]{2,1,0:T(8,128)(2,1)} custom-call(s32[128,2]{1,0:T(8,128)S(1)} %bitcast.19, bf16[128,64,256]{2,1,0:T(8,128)(2,1)S(1)} %get-tuple-element.14.from_ref), custom_call_target="tpu_custom_call" | custom-call | bytes 8388608 | tf_op jit(solution)/shard_map/take_outgoing/pallas_call | solution.py:102
  24.8 0.0 copy-start.1
  24.8 0.0 copy-start.2
  24.8 7.1 %all-to-all-start.1 = ((bf16[128,2,64,256]{3,2,1,0:T(8,128)(2,1)}), bf16[128,2,64,256]{3,2,1,0:T(8,128)(2,1)}, u32[]{:S(2)}, u32[]{:S(2)}) async-start(bf16[128,2,64,256]{3,2,1,0:T(8,128)(2,1)} %bitcast.26), calls=%async_computation.1 | async-start | bytes 16777216 | tf_op jit(solution)/shard_map/all_to_all | solution.py:321
  31.9 0.6 constant_dynamic-slice_fusion
  32.5 0.7 pad_add_fusion.info_ref
  33.2 104.5 %all-to-all-done.1 = bf16[128,2,64,256]{3,2,1,0:T(8,128)(2,1)} async-done(((bf16[128,2,64,256]{3,2,1,0:T(8,128)(2,1)}), bf16[128,2,64,256]{3,2,1,0:T(8,128)(2,1)}, u32[]{:S(2)}, u32[]{:S(2)}) %all-to-all-start.1) | async-done | bytes 8388640 | tf_op jit(solution)/shard_map/all_to_all | solution.py:321
  137.6 3.6 %attend_other.1 = (bf16[32,128]{1,0:T(8,128)(2,1)S(1)}, bf16[128,64,256]{2,1,0:T(8,128)(2,1)S(1)}, bf16[256,4096]{1,0:T(8,128)(2,1)S(1)}) custom-call(s32[130]{0:T(256)S(1)} %pad_add_fusion.info_ref, bf16[256,64,256]{2,1,0:T(8,128)(2,1)} %bitcast.7.arrived_ref, bf16[2,32,128]{2,1,0:T(8,128)(2,1)S(1)} %bitcast.21, bf16[2,4,256]{2,1,0:T(4,128)(2,1)S(1)} %bitcast.23, ...), custom_call_target="tpu_custom_call" | custom-call | flops 67108864 | bytes 4194304 | tf_op jit(solution)/shard_map/attend_other/pallas_call | solution.py:215
  141.3 0.1 collective-permute-start
  141.4 3.3 %attend_own.1 = (bf16[32,128]{1,0:T(8,128)(2,1)S(1)}, bf16[768,4096]{1,0:T(8,128)(2,1)S(1)}) custom-call(s32[130]{0:T(256)S(1)} %pad_add_fusion.info_ref, bf16[128,64,256]{2,1,0:T(8,128)(2,1)S(1)} %get-tuple-element.15.pages_ref, bf16[2,32,128]{2,1,0:T(8,128)(2,1)S(1)} %bitcast.22, bf16[2,4,256]{2,1,0:T(4,128)(2,1)S(1)} %bitcast.24, ...), custom_call_target="tpu_custom_call" | custom-call | flops 67108864 | bytes 4194304 | tf_op jit(solution)/shard_map/attend_own/pallas_call | solution.py:233
  144.7 0.4 collective-permute-done.partner_ref
  145.1 1.2 project.1
  146.3 1.7 %collective-permute-start.1 = (bf16[8,4096]{1,0:T(8,128)(2,1)S(1)}, bf16[8,4096]{1,0:T(8,128)(2,1)S(1)}, u32[]{:S(2)}, u32[]{:S(2)}) collective-permute-start(bf16[8,4096]{1,0:T(8,128)(2,1)S(1)} %get-tuple-element.21._), channel_id=1, source_target_pairs={{0,1},{1,0},{2,3},{3,2},{4,5},{5,4},{6,7},{7,6},{8,9},{9,8},{10,11... | collective-permute-start | bytes 196616 | tf_op jit(solution)/shard_map/ppermute | solution.py:19
  147.9 2.6 %collective-permute-done.1 = bf16[8,4096]{1,0:T(8,128)(2,1)S(1)} collective-permute-done((bf16[8,4096]{1,0:T(8,128)(2,1)S(1)}, bf16[8,4096]{1,0:T(8,128)(2,1)S(1)}, u32[]{:S(2)}, u32[]{:S(2)}) %collective-permute-start.1) | collective-permute-done | bytes 65568 | tf_op jit(solution)/shard_map/ppermute | solution.py:19
  150.6 6.3 %collective-permute-start.3 = (bf16[4,4096]{1,0:T(4,128)(2,1)S(1)}, bf16[4,4096]{1,0:T(4,128)(2,1)S(1)}, u32[]{:S(2)}, u32[]{:S(2)}) collective-permute-start(bf16[4,4096]{1,0:T(4,128)(2,1)S(1)} %get-tuple-element.24), channel_id=1, source_target_pairs={{0,4},{1,5},{2,6},{3,7},{4,0},{5,1},{6,2},{7,3},{8,12},{9,13},{10,... | collective-permute-start | bytes 98312 | tf_op jit(solution)/shard_map/ppermute | solution.py:19
  156.9 0.0 collective-permute-start.4
  156.9 2.8 %collective-permute-start.2 = (bf16[4,4096]{1,0:T(4,128)(2,1)S(1)}, bf16[4,4096]{1,0:T(4,128)(2,1)S(1)}, u32[]{:S(2)}, u32[]{:S(2)}) collective-permute-start(bf16[4,4096]{1,0:T(4,128)(2,1)S(1)} %get-tuple-element.25), channel_id=1, source_target_pairs={{0,3},{1,2},{2,1},{3,0},{4,7},{5,6},{6,5},{7,4},{8,11},{9,10},{10,... | collective-permute-start | bytes 98312 | tf_op jit(solution)/shard_map/ppermute | solution.py:19
  159.7 2.0 %store_moved.1 = bf16[128,64,256]{2,1,0:T(8,128)(2,1)} custom-call(bf16[128,64,256]{2,1,0:T(8,128)(2,1)S(1)} %get-tuple-element.15.pages_ref, bf16[8,4096]{1,0:T(8,128)(2,1)S(1)} %get-tuple-element.21._), custom_call_target="tpu_custom_call" | custom-call | bytes 4194304 | tf_op jit(solution)/shard_map/store_moved/pallas_call | solution.py:255
  161.7 0.0 collective-permute-done.3
  161.7 2.7 %collective-permute-done.4 = bf16[4,4096]{1,0:T(4,128)(2,1)S(1)} collective-permute-done((bf16[4,4096]{1,0:T(4,128)(2,1)S(1)}, bf16[4,4096]{1,0:T(4,128)(2,1)S(1)}, u32[]{:S(2)}, u32[]{:S(2)}) %collective-permute-start.4) | collective-permute-done | bytes 32800 | tf_op jit(solution)/shard_map/ppermute | solution.py:19
  164.4 0.7 fusion.3
  (6 shorter events, 0.1 us)
Async XLA Ops:
  0.6 31.2 %copy-start = (s32[1,2,1]{1,2,0:T(1,128)S(1)}, s32[1,2,1]{1,2,0:T(1,128)}, u32[]{:S(2)}) copy-start(s32[1,2,1]{1,2,0:T(1,128)} %param.11) | copy-start | bytes 28
  24.8 112.9 %copy-start.1 = (bf16[1,4,2048]{2,1,0:T(4,128)(2,1)S(1)}, bf16[1,4,2048]{2,1,0:T(4,128)(2,1)}, u32[]{:S(2)}) copy-start(bf16[1,4,2048]{2,1,0:T(4,128)(2,1)} %param.12) | copy-start | bytes 49156
  24.8 112.9 %copy-start.2 = (bf16[1,4,512]{2,1,0:T(4,128)(2,1)S(1)}, bf16[1,4,512]{2,1,0:T(4,128)(2,1)}, u32[]{:S(2)}) copy-start(bf16[1,4,512]{2,1,0:T(4,128)(2,1)} %param.13) | copy-start | bytes 12292
  24.8 112.9 %all-to-all-start.1 = ((bf16[128,2,64,256]{3,2,1,0:T(8,128)(2,1)}), bf16[128,2,64,256]{3,2,1,0:T(8,128)(2,1)}, u32[]{:S(2)}, u32[]{:S(2)}) async-start(bf16[128,2,64,256]{3,2,1,0:T(8,128)(2,1)} %bitcast.26), calls=%async_computation.1 | async-start | bytes 16777216 | tf_op jit(solution)/shard_map/all_to_all | solution.py:321
  141.3 3.8 %collective-permute-start = (bf16[32,128]{1,0:T(8,128)(2,1)S(1)}, bf16[32,128]{1,0:T(8,128)(2,1)S(1)}, u32[]{:S(2)}, u32[]{:S(2)}) collective-permute-start(bf16[32,128]{1,0:T(8,128)(2,1)S(1)} %get-tuple-element.17), channel_id=1, source_target_pairs={{0,1},{1,0},{2,3},{3,2},{4,5},{5,4},{6,7},{7,6},{8,9},{9,8},{10,11... | collective-permute-start | bytes 24584 | tf_op jit(solution)/shard_map/ppermute | solution.py:19
  146.3 4.3 %collective-permute-start.1 = (bf16[8,4096]{1,0:T(8,128)(2,1)S(1)}, bf16[8,4096]{1,0:T(8,128)(2,1)S(1)}, u32[]{:S(2)}, u32[]{:S(2)}) collective-permute-start(bf16[8,4096]{1,0:T(8,128)(2,1)S(1)} %get-tuple-element.21._), channel_id=1, source_target_pairs={{0,1},{1,0},{2,3},{3,2},{4,5},{5,4},{6,7},{7,6},{8,9},{9,8},{10,11... | collective-permute-start | bytes 196616 | tf_op jit(solution)/shard_map/ppermute | solution.py:19
  150.6 11.1 %collective-permute-start.3 = (bf16[4,4096]{1,0:T(4,128)(2,1)S(1)}, bf16[4,4096]{1,0:T(4,128)(2,1)S(1)}, u32[]{:S(2)}, u32[]{:S(2)}) collective-permute-start(bf16[4,4096]{1,0:T(4,128)(2,1)S(1)} %get-tuple-element.24), channel_id=1, source_target_pairs={{0,4},{1,5},{2,6},{3,7},{4,0},{5,1},{6,2},{7,3},{8,12},{9,13},{10,... | collective-permute-start | bytes 98312 | tf_op jit(solution)/shard_map/ppermute | solution.py:19
  156.9 7.5 %collective-permute-start.4 = (bf16[4,4096]{1,0:T(4,128)(2,1)S(1)}, bf16[4,4096]{1,0:T(4,128)(2,1)S(1)}, u32[]{:S(2)}, u32[]{:S(2)}) collective-permute-start(bf16[4,4096]{1,0:T(4,128)(2,1)S(1)} %get-tuple-element.25), channel_id=1, source_target_pairs={{0,7},{1,6},{2,5},{3,4},{4,3},{5,2},{6,1},{7,0},{8,15},{9,14},{10,... | collective-permute-start | bytes 98312 | tf_op jit(solution)/shard_map/ppermute | solution.py:19
  156.9 7.5 %collective-permute-start.2 = (bf16[4,4096]{1,0:T(4,128)(2,1)S(1)}, bf16[4,4096]{1,0:T(4,128)(2,1)S(1)}, u32[]{:S(2)}, u32[]{:S(2)}) collective-permute-start(bf16[4,4096]{1,0:T(4,128)(2,1)S(1)} %get-tuple-element.25), channel_id=1, source_target_pairs={{0,3},{1,2},{2,1},{3,0},{4,7},{5,6},{6,5},{7,4},{8,11},{9,10},{10,... | collective-permute-start | bytes 98312 | tf_op jit(solution)/shard_map/ppermute | solution.py:19

commit v6 on v5

--- a/solution.py
+++ b/solution.py
@@ -76,13 +76,23 @@
     )(in_hbm(plan_src), in_hbm(plan_page), in_hbm(pages))
 
 
-def take_kernel(at_ref, from_ref, to_ref, sem):
-    columns = at_ref.shape[1]
-
-    @pl.loop(0, at_ref.shape[0], init_carry=jnp.int32(0), unroll=4)
+def take_kernel(asked_ref, from_ref, to_ref, turned_ref, at_ref, sem, at_sem):
+    count, columns = asked_ref.shape
+    same = lax.broadcasted_iota(jnp.int32, (count, count), 0) == lax.broadcasted_iota(
+        jnp.int32, (count, count), 1
+    )
+    for column in range(columns):
+        turned_ref[column : column + 1, :] = jnp.sum(
+            jnp.where(same, asked_ref[:, column : column + 1], 0), axis=0, keepdims=True
+        )
+    scalars = pltpu.make_async_copy(turned_ref, at_ref, at_sem)
+    scalars.start()
+    scalars.wait()
+
+    @pl.loop(0, count, init_carry=jnp.int32(0), unroll=4)
     def started(row, count):
         for column in range(columns):
-            page = at_ref[row, column]
+            page = at_ref[column, row]
 
             @pl.when(page >= 0)
             def _():
@@ -102,9 +112,14 @@
     return pl.pallas_call(
         take_kernel,
         out_shape=pltpu.HBM(shape, pages.dtype),
-        in_specs=[SMEM, VMEM],
+        in_specs=[VMEM, VMEM],
         out_specs=HBM,
-        scratch_shapes=[pltpu.SemaphoreType.DMA],
+        scratch_shapes=[
+            pltpu.VMEM(at.shape[::-1], jnp.int32),
+            pltpu.SMEM(at.shape[::-1], jnp.int32),
+            pltpu.SemaphoreType.DMA,
+            pltpu.SemaphoreType.DMA,
+        ],
         compiler_params=pltpu.CompilerParams(vmem_limit_bytes=LIMIT),
         cost_estimate=pl.CostEstimate(
             flops=0, bytes_accessed=count * pages.shape[1] * pages.shape[2] * 2, transcendentals=0
@@ -333,14 +348,12 @@
 
     total, sent = project(kept, partner, first, second, steps)
     moved = store(pages, sent)
-    total = total + flipped(sent, 1).astype(jnp.float32)
-    rounded = total.astype(jnp.bfloat16)
+    mine = sent[steps:]
+    theirs = sent[:steps]
     own = total[:steps]
-    for high in range(0, lax.axis_size("tp"), 4):
-        for low in (0, 3):
-            if high + low:
-                rows = rounded[:steps] if low == 0 else rounded[steps:]
-                own = own + flipped(rows, high + low).astype(jnp.float32)
+    own = own + flipped(theirs, 1).astype(jnp.float32) + flipped(theirs, 3).astype(jnp.float32)
+    own = own + flipped(mine, 2).astype(jnp.float32)
+    own = own + flipped(own.astype(jnp.bfloat16), 4).astype(jnp.float32)
     return own.reshape(1, steps, -1).astype(jnp.bfloat16), moved
 
 

time: 165 us -> 163 us (0.988)
  transfers between devices with their start and end apart: 6 -> 6, of which waited for: 4 -> 5; matrix products, arithmetic and copies ran while one was open for 1% -> 1% of each run, Pallas kernels for 3% -> 3%
where the time goes in v6:
time: 163 us
  waiting for transfers between devices  109 us (67%)
  blocking collectives  18.2 us (11%)
  starting transfers between devices  18.1 us (11%)
  Pallas kernels  15 us (9%)
    all_to_all x1, waiting for transfers between devices, on_device(): lax.all_to_all(outgoing, BOTH, split_axis=0, concat_axis=0, tiled=True)  104 us
    all_to_all x1, blocking collectives, on_device(): lax.all_to_all(wanted, BOTH, split_axis=0, concat_axis=0, tiled=True)  18.2 us
    ppermute x5, starting transfers between devices, flipped(): return lax.ppermute(value, 'tp', [(i, i ^ bits) for i in range(size)])  11 us
    all_to_all x1, starting transfers between devices, on_device(): lax.all_to_all(outgoing, BOTH, split_axis=0, concat_axis=0, tiled=True)  7.16 us
    ppermute x5, waiting for transfers between devices, flipped(): return lax.ppermute(value, 'tp', [(i, i ^ bits) for i in range(size)])  4.2 us
    pallas_call x1, Pallas kernels, attend_other(): pl.pallas_call(other_kernel, out_shape=(jax.ShapeDtypeStruct((rows, head)...  3.62 us
    pallas_call x1, Pallas kernels, attend_own(): pl.pallas_call(own_kernel, out_shape=(jax.ShapeDtypeStruct((rows, head),...  3.34 us
  transfers between devices with their start and end apart: 6, of which 5 were waited for; matrix products, arithmetic and copies ran while one was open for 1% of the time, Pallas kernels for 3%

profile of v6, /device:TPU:24, one launch (start us, length us, event | category | flops | bytes accessed | tf_op | source)
XLA Modules:
  0.0 162.8 jit_solution(4016203049130585884)
XLA Ops:
  0.6 0.0 copy-start
  0.6 2.3 %make_plan.1 = (s32[128,2]{1,0:T(8,128)S(1)}, s32[1,128]{1,0:T(1,128)S(1)}, bf16[128,64,256]{2,1,0:T(8,128)(2,1)S(1)}) custom-call(s32[1,128]{1,0:T(1,128)} %src_hbm.1, s32[1,128]{1,0:T(1,128)} %page_hbm.1, bf16[128,64,256]{2,1,0:T(8,128)(2,1)} %cache_ref.1), custom_call_target="tpu_custom_call" | custom-call | tf_op jit(solution)/shard_map/make_plan/pallas_call | solution.py:60
  2.9 18.2 %all_to_all.16 = s32[128,1,2]{2,1,0:T(1,128)S(1)} all-to-all(s32[128,1,2]{2,1,0:T(1,128)S(1)} %bitcast.20), channel_id=1, replica_groups=mesh['inst'=16,'tp'=8] {'inst','tp'}, dimensions={0} | all-to-all | bytes 2048 | tf_op jit(solution)/shard_map/all_to_all | solution.py:333
  21.1 2.6 %take_outgoing.1 = bf16[256,64,256]{2,1,0:T(8,128)(2,1)} custom-call(s32[128,2]{1,0:T(8,128)S(1)} %bitcast.19, bf16[128,64,256]{2,1,0:T(8,128)(2,1)S(1)} %get-tuple-element.14.from_ref), custom_call_target="tpu_custom_call" | custom-call | bytes 8388608 | tf_op jit(solution)/shard_map/take_outgoing/pallas_call | solution.py:112
  23.7 0.0 copy-start.1
  23.7 0.0 copy-start.2
  23.7 7.2 %all-to-all-start.1 = ((bf16[128,2,64,256]{3,2,1,0:T(8,128)(2,1)}), bf16[128,2,64,256]{3,2,1,0:T(8,128)(2,1)}, u32[]{:S(2)}, u32[]{:S(2)}) async-start(bf16[128,2,64,256]{3,2,1,0:T(8,128)(2,1)} %bitcast.26), calls=%async_computation.1 | async-start | bytes 16777216 | tf_op jit(solution)/shard_map/all_to_all | solution.py:336
  30.9 0.6 constant_dynamic-slice_fusion
  31.5 0.7 pad_add_fusion.info_ref
  32.2 104.5 %all-to-all-done.1 = bf16[128,2,64,256]{3,2,1,0:T(8,128)(2,1)} async-done(((bf16[128,2,64,256]{3,2,1,0:T(8,128)(2,1)}), bf16[128,2,64,256]{3,2,1,0:T(8,128)(2,1)}, u32[]{:S(2)}, u32[]{:S(2)}) %all-to-all-start.1) | async-done | bytes 8388640 | tf_op jit(solution)/shard_map/all_to_all | solution.py:336
  136.7 3.6 %attend_other.1 = (bf16[32,128]{1,0:T(8,128)(2,1)S(1)}, bf16[128,64,256]{2,1,0:T(8,128)(2,1)S(1)}, bf16[256,4096]{1,0:T(8,128)(2,1)S(1)}) custom-call(s32[130]{0:T(256)S(1)} %pad_add_fusion.info_ref, bf16[256,64,256]{2,1,0:T(8,128)(2,1)} %bitcast.7.arrived_ref, bf16[2,32,128]{2,1,0:T(8,128)(2,1)S(1)} %bitcast.21, bf16[2,4,256]{2,1,0:T(4,128)(2,1)S(1)} %bitcast.23, ...), custom_call_target="tpu_custom_call" | custom-call | flops 67108864 | bytes 4194304 | tf_op jit(solution)/shard_map/attend_other/pallas_call | solution.py:230
  140.3 0.1 collective-permute-start
  140.4 3.3 %attend_own.1 = (bf16[32,128]{1,0:T(8,128)(2,1)S(1)}, bf16[768,4096]{1,0:T(8,128)(2,1)S(1)}) custom-call(s32[130]{0:T(256)S(1)} %pad_add_fusion.info_ref, bf16[128,64,256]{2,1,0:T(8,128)(2,1)S(1)} %get-tuple-element.15.pages_ref, bf16[2,32,128]{2,1,0:T(8,128)(2,1)S(1)} %bitcast.22, bf16[2,4,256]{2,1,0:T(4,128)(2,1)S(1)} %bitcast.24, ...), custom_call_target="tpu_custom_call" | custom-call | flops 67108864 | bytes 4194304 | tf_op jit(solution)/shard_map/attend_own/pallas_call | solution.py:248
  143.7 0.3 collective-permute-done.partner_ref
  144.0 1.2 project.1
  145.3 0.6 collective-permute-start.3
  145.9 3.9 %collective-permute-start.2 = (bf16[4,4096]{1,0:T(4,128)(2,1)S(1)}, bf16[4,4096]{1,0:T(4,128)(2,1)S(1)}, u32[]{:S(2)}, u32[]{:S(2)}) collective-permute-start(bf16[4,4096]{1,0:T(4,128)(2,1)S(1)} %get-tuple-element.22), channel_id=1, source_target_pairs={{0,3},{1,2},{2,1},{3,0},{4,7},{5,6},{6,5},{7,4},{8,11},{9,10},{10,... | collective-permute-start | bytes 98312 | tf_op jit(solution)/shard_map/ppermute | solution.py:19
  149.7 0.0 collective-permute-start.1
  149.8 1.0 collective-permute-done.3
  150.8 0.9 collective-permute-done.2
  151.6 2.0 %collective-permute-done.1 = bf16[4,4096]{1,0:T(4,128)(2,1)S(1)} collective-permute-done((bf16[4,4096]{1,0:T(4,128)(2,1)S(1)}, bf16[4,4096]{1,0:T(4,128)(2,1)S(1)}, u32[]{:S(2)}, u32[]{:S(2)}) %collective-permute-start.1) | collective-permute-done | bytes 32800 | tf_op jit(solution)/shard_map/ppermute | solution.py:19
  153.7 6.4 %collective-permute-start.4 = (bf16[4,4096]{1,0:T(4,128)(2,1)S(1)}, bf16[4,4096]{1,0:T(4,128)(2,1)S(1)}, u32[]{:S(2)}, u32[]{:S(2)}) collective-permute-start(bf16[4,4096]{1,0:T(4,128)(2,1)S(1)} %fusion.1), channel_id=1, source_target_pairs={{0,4},{1,5},{2,6},{3,7},{4,0},{5,1},{6,2},{7,3},{8,12},{9,13},{10,... | collective-permute-start | bytes 98312 | tf_op jit(solution)/shard_map/ppermute | solution.py:19
  160.1 2.0 %store_moved.1 = bf16[128,64,256]{2,1,0:T(8,128)(2,1)} custom-call(bf16[128,64,256]{2,1,0:T(8,128)(2,1)S(1)} %get-tuple-element.15.pages_ref, bf16[8,4096]{1,0:T(8,128)(2,1)S(1)} %get-tuple-element.21._), custom_call_target="tpu_custom_call" | custom-call | bytes 4194304 | tf_op jit(solution)/shard_map/store_moved/pallas_call | solution.py:270
  162.1 0.7 fusion
  (6 shorter events, 0.1 us)
Async XLA Ops:
  0.6 30.3 %copy-start = (s32[1,2,1]{1,2,0:T(1,128)S(1)}, s32[1,2,1]{1,2,0:T(1,128)}, u32[]{:S(2)}) copy-start(s32[1,2,1]{1,2,0:T(1,128)} %param.11) | copy-start | bytes 28
  23.7 113.0 %copy-start.1 = (bf16[1,4,2048]{2,1,0:T(4,128)(2,1)S(1)}, bf16[1,4,2048]{2,1,0:T(4,128)(2,1)}, u32[]{:S(2)}) copy-start(bf16[1,4,2048]{2,1,0:T(4,128)(2,1)} %param.12) | copy-start | bytes 49156
  23.7 113.0 %copy-start.2 = (bf16[1,4,512]{2,1,0:T(4,128)(2,1)S(1)}, bf16[1,4,512]{2,1,0:T(4,128)(2,1)}, u32[]{:S(2)}) copy-start(bf16[1,4,512]{2,1,0:T(4,128)(2,1)} %param.13) | copy-start | bytes 12292
  23.7 113.0 %all-to-all-start.1 = ((bf16[128,2,64,256]{3,2,1,0:T(8,128)(2,1)}), bf16[128,2,64,256]{3,2,1,0:T(8,128)(2,1)}, u32[]{:S(2)}, u32[]{:S(2)}) async-start(bf16[128,2,64,256]{3,2,1,0:T(8,128)(2,1)} %bitcast.26), calls=%async_computation.1 | async-start | bytes 16777216 | tf_op jit(solution)/shard_map/all_to_all | solution.py:336
  140.3 3.7 %collective-permute-start = (bf16[32,128]{1,0:T(8,128)(2,1)S(1)}, bf16[32,128]{1,0:T(8,128)(2,1)S(1)}, u32[]{:S(2)}, u32[]{:S(2)}) collective-permute-start(bf16[32,128]{1,0:T(8,128)(2,1)S(1)} %get-tuple-element.17), channel_id=1, source_target_pairs={{0,1},{1,0},{2,3},{3,2},{4,5},{5,4},{6,7},{7,6},{8,9},{9,8},{10,11... | collective-permute-start | bytes 24584 | tf_op jit(solution)/shard_map/ppermute | solution.py:19
  145.3 5.5 %collective-permute-start.3 = (bf16[4,4096]{1,0:T(4,128)(2,1)S(1)}, bf16[4,4096]{1,0:T(4,128)(2,1)S(1)}, u32[]{:S(2)}, u32[]{:S(2)}) collective-permute-start(bf16[4,4096]{1,0:T(4,128)(2,1)S(1)} %get-tuple-element.23), channel_id=1, source_target_pairs={{0,2},{1,3},{2,0},{3,1},{4,6},{5,7},{6,4},{7,5},{8,10},{9,11},{10,... | collective-permute-start | bytes 98312 | tf_op jit(solution)/shard_map/ppermute | solution.py:19
  145.9 5.8 %collective-permute-start.2 = (bf16[4,4096]{1,0:T(4,128)(2,1)S(1)}, bf16[4,4096]{1,0:T(4,128)(2,1)S(1)}, u32[]{:S(2)}, u32[]{:S(2)}) collective-permute-start(bf16[4,4096]{1,0:T(4,128)(2,1)S(1)} %get-tuple-element.22), channel_id=1, source_target_pairs={{0,3},{1,2},{2,1},{3,0},{4,7},{5,6},{6,5},{7,4},{8,11},{9,10},{10,... | collective-permute-start | bytes 98312 | tf_op jit(solution)/shard_map/ppermute | solution.py:19
  149.7 3.9 %collective-permute-start.1 = (bf16[4,4096]{1,0:T(4,128)(2,1)S(1)}, bf16[4,4096]{1,0:T(4,128)(2,1)S(1)}, u32[]{:S(2)}, u32[]{:S(2)}) collective-permute-start(bf16[4,4096]{1,0:T(4,128)(2,1)S(1)} %get-tuple-element.22), channel_id=1, source_target_pairs={{0,1},{1,0},{2,3},{3,2},{4,5},{5,4},{6,7},{7,6},{8,9},{9,8},{10,11... | collective-permute-start | bytes 98312 | tf_op jit(solution)/shard_map/ppermute | solution.py:19
  153.7 8.4 %collective-permute-start.4 = (bf16[4,4096]{1,0:T(4,128)(2,1)S(1)}, bf16[4,4096]{1,0:T(4,128)(2,1)S(1)}, u32[]{:S(2)}, u32[]{:S(2)}) collective-permute-start(bf16[4,4096]{1,0:T(4,128)(2,1)S(1)} %fusion.1), channel_id=1, source_target_pairs={{0,4},{1,5},{2,6},{3,7},{4,0},{5,1},{6,2},{7,3},{8,12},{9,13},{10,... | collective-permute-start | bytes 98312 | tf_op jit(solution)/shard_map/ppermute | solution.py:19

commit v7 on v6

--- a/solution.py
+++ b/solution.py
@@ -27,60 +27,71 @@
     return pltpu.with_memory_space_constraint(value, pltpu.VMEM)
 
 
-def plan_kernel(src_hbm, page_hbm, cache_ref, wanted_ref, place_ref, held_ref, src_ref, page_ref, sems):
+def plan_kernel(tensor, src_hbm, page_hbm, length_hbm, cache_ref, *rest):
+    wanted_ref, place_ref, held_ref, src_ref, page_ref, length_ref, sems = rest
     copies = [
         pltpu.make_async_copy(src_hbm, src_ref, sems.at[0]),
         pltpu.make_async_copy(page_hbm, page_ref, sems.at[1]),
         pltpu.make_async_copy(cache_ref, held_ref, sems.at[2]),
+        pltpu.make_async_copy(length_hbm, length_ref, sems.at[3]),
     ]
     for copy in copies:
         copy.start()
     slots = src_ref.shape[1]
-    sources = wanted_ref.shape[0]
-    order = lax.broadcasted_iota(jnp.int32, (1, slots), 1)
+    pairs, most = wanted_ref.shape
+    side = lax.axis_index("inst") % 2
+    shift = tensor.bit_length() - 1
+    rows = lax.broadcasted_iota(jnp.int32, (slots, slots), 0)
+    columns = lax.broadcasted_iota(jnp.int32, (slots, slots), 1)
     copies[0].wait()
     copies[1].wait()
     src = src_ref[...]
-    coded = order * 65536 + page_ref[...]
-    named = lax.broadcasted_iota(jnp.int32, (sources, slots), 0) == src
-    first = jnp.min(jnp.where(named, coded, slots * 65536), axis=1, keepdims=True)
-    last = jnp.max(jnp.where(named, coded, -1), axis=1, keepdims=True)
-    wanted_ref[:, 0:1] = jnp.where(last >= 0, first & 65535, -1)
-    wanted_ref[:, 1:2] = jnp.where(last > first, last & 65535, -1)
-    rows = lax.broadcasted_iota(jnp.int32, (slots, slots), 0)
-    columns = lax.broadcasted_iota(jnp.int32, (slots, slots), 1)
-    src_column = jnp.max(jnp.where(rows == columns, src, 0), axis=1, keepdims=True)
-    again = jnp.max(jnp.where((src_column == src) & (rows < columns), 1, 0), axis=0, keepdims=True)
-    place_ref[...] = src * 2 + again
+    row_of = lax.shift_right_logical(src, shift)
+    pair = lax.shift_left(lax.shift_right_logical(row_of, 1), shift) + (src & (tensor - 1))
+    value = page_ref[...] + jnp.where((row_of & 1) == side, 0, cache_ref.shape[0])
+    pair_column = jnp.max(jnp.where(rows == columns, pair, 0), axis=1, keepdims=True)
+    rank = jnp.sum(jnp.where((pair_column == pair) & (rows < columns), 1, 0), axis=0, keepdims=True)
+    named = lax.broadcasted_iota(jnp.int32, (pairs, slots), 0) == pair
+    for at in range(most):
+        wanted_ref[:, at : at + 1] = jnp.max(
+            jnp.where(named & (rank == at), value, -1), axis=1, keepdims=True
+        )
+    place_ref[:, :slots] = pair * most + rank
+    copies[3].wait()
+    group = lax.axis_index("tp") % 2
+    length = jnp.where(group == 0, length_ref[0, 0], length_ref[0, 1])
+    lanes = lax.broadcasted_iota(jnp.int32, (1, place_ref.shape[1] - slots), 1)
+    place_ref[:, slots:] = jnp.where(lanes == 0, 1 - group, length)
     copies[2].wait()
 
 
-def make_plan(plan_src, plan_page, pages, sources):
+def make_plan(plan_src, plan_page, lengths, pages, pairs, tensor):
     slots = plan_src.shape[1]
     return pl.pallas_call(
-        plan_kernel,
+        functools.partial(plan_kernel, tensor),
         out_shape=(
-            jax.ShapeDtypeStruct((sources, 2), jnp.int32),
-            jax.ShapeDtypeStruct((1, slots), jnp.int32),
+            jax.ShapeDtypeStruct((pairs, 4), jnp.int32),
+            jax.ShapeDtypeStruct((1, slots + 128), jnp.int32),
             pltpu.VMEM(pages.shape, pages.dtype),
         ),
-        in_specs=[HBM, HBM, HBM],
+        in_specs=[HBM, HBM, HBM, HBM],
         out_specs=(VMEM, VMEM, VMEM),
         scratch_shapes=[
             pltpu.VMEM((1, slots), jnp.int32),
             pltpu.VMEM((1, slots), jnp.int32),
-            pltpu.SemaphoreType.DMA((3,)),
+            pltpu.SMEM(lengths.shape, jnp.int32),
+            pltpu.SemaphoreType.DMA((4,)),
         ],
         compiler_params=pltpu.CompilerParams(vmem_limit_bytes=LIMIT),
         name="make_plan",
-    )(in_hbm(plan_src), in_hbm(plan_page), in_hbm(pages))
-
-
-def take_kernel(asked_ref, from_ref, to_ref, turned_ref, at_ref, sem, at_sem):
+    )(in_hbm(plan_src), in_hbm(plan_page), in_hbm(lengths), in_hbm(pages))
+
+
+def take_kernel(asked_ref, own_ref, other_ref, to_ref, turned_ref, at_ref, sem, at_sem):
     count, columns = asked_ref.shape
-    same = lax.broadcasted_iota(jnp.int32, (count, count), 0) == lax.broadcasted_iota(
-        jnp.int32, (count, count), 1
-    )
+    pages = own_ref.shape[0]
+    shape = (count, turned_ref.shape[1])
+    same = lax.broadcasted_iota(jnp.int32, shape, 0) == lax.broadcasted_iota(jnp.int32, shape, 1)
     for column in range(columns):
         turned_ref[column : column + 1, :] = jnp.sum(
             jnp.where(same, asked_ref[:, column : column + 1], 0), axis=0, keepdims=True
@@ -89,43 +100,49 @@
     scalars.start()
     scalars.wait()
 
-    @pl.loop(0, count, init_carry=jnp.int32(0), unroll=4)
-    def started(row, count):
+    @pl.loop(0, count, init_carry=jnp.int32(0), unroll=2)
+    def started(row, total):
         for column in range(columns):
             page = at_ref[column, row]
-
-            @pl.when(page >= 0)
+            to = to_ref.at[row * columns + column]
+
+            @pl.when((page >= 0) & (page < pages))
             def _():
-                pltpu.make_async_copy(from_ref.at[page], to_ref.at[row * columns + column], sem).start()
-
-            count = count + (page >= 0).astype(jnp.int32)
-        return count
+                pltpu.make_async_copy(own_ref.at[page], to, sem).start()
+
+            @pl.when(page >= pages)
+            def _():
+                pltpu.make_async_copy(other_ref.at[page - pages], to, sem).start()
+
+            total = total + (page >= 0).astype(jnp.int32)
+        return total
 
     @pl.loop(0, started)
     def _(_):
-        pltpu.make_async_copy(from_ref.at[0], to_ref.at[0], sem).wait()
-
-
-def take(pages, at):
+        pltpu.make_async_copy(own_ref.at[0], to_ref.at[0], sem).wait()
+
+
+def take(own, other, at):
     count = at.shape[0] * at.shape[1]
-    shape = (count,) + pages.shape[1:]
+    shape = (count,) + own.shape[1:]
+    turned = (at.shape[1], -(-at.shape[0] // 128) * 128)
     return pl.pallas_call(
         take_kernel,
-        out_shape=pltpu.HBM(shape, pages.dtype),
-        in_specs=[VMEM, VMEM],
+        out_shape=pltpu.HBM(shape, own.dtype),
+        in_specs=[VMEM, VMEM, VMEM],
         out_specs=HBM,
         scratch_shapes=[
-            pltpu.VMEM(at.shape[::-1], jnp.int32),
-            pltpu.SMEM(at.shape[::-1], jnp.int32),
+            pltpu.VMEM(turned, jnp.int32),
+            pltpu.SMEM(turned, jnp.int32),
             pltpu.SemaphoreType.DMA,
             pltpu.SemaphoreType.DMA,
         ],
         compiler_params=pltpu.CompilerParams(vmem_limit_bytes=LIMIT),
         cost_estimate=pl.CostEstimate(
-            flops=0, bytes_accessed=count * pages.shape[1] * pages.shape[2] * 2, transcendentals=0
+            flops=0, bytes_accessed=count * own.shape[1] * own.shape[2] * 2, transcendentals=0
         ),
         name="take_outgoing",
-    )(at, in_vmem(pages))
+    )(at, in_vmem(own), in_vmem(other))
 
 
 def attention(which, length, query_ref, fresh_ref, pages_ref, ready):
@@ -176,14 +193,14 @@
     half = slots // 2
     parts = sems.shape[0] - 1
     size = half // parts
-    which = info_ref[slots]
-    length = info_ref[slots + 1]
+    which = info_ref[0, slots]
+    length = info_ref[0, slots + 1]
 
     def gather(first, count, sem):
         @pl.loop(0, count, unroll=8)
         def _(at):
             slot = first + at
-            pltpu.make_async_copy(arrived_ref.at[info_ref[slot]], pages_ref.at[slot], sem).start()
+            pltpu.make_async_copy(arrived_ref.at[info_ref[0, slot]], pages_ref.at[slot], sem).start()
 
     def wait(first, count, sem):
         block = pages_ref.at[pl.ds(first, count)]
@@ -210,8 +227,8 @@
         weight_ref.at[pl.ds(weight_ref.shape[0] - count, count)], held_ref, held_sem
     )
     hold.start()
-    which = 1 - info_ref[slots]
-    out_ref[...] = attention(which, info_ref[slots + 1], query_ref, fresh_ref, pages_ref, [lambda: None])
+    which = 1 - info_ref[0, slots]
+    out_ref[...] = attention(which, info_ref[0, slots + 1], query_ref, fresh_ref, pages_ref, [lambda: None])
     hold.wait()
 
 
@@ -225,7 +242,7 @@
 
 def attend_other(info, arrived, queries, fresh, weight, count):
     rows, head = queries.shape[1:]
-    slots = info.shape[0] - 2
+    slots = info.shape[1] - 128
     page = arrived.shape[1]
     return pl.pallas_call(
         other_kernel,
@@ -327,20 +344,24 @@
     heads = new_kv.shape[2] // width
     head = width // 2
     groups = queries.shape[2] // (heads * head)
-    side = lax.axis_index("tp") % 2
-
-    wanted, place, held = make_plan(plan_src, plan_page, old_cache, devices)
-    asked = lax.all_to_all(wanted, BOTH, split_axis=0, concat_axis=0, tiled=True)
-    taken = take(held, asked)
-    outgoing = taken.reshape((devices, 2) + old_cache.shape[1:])
-    arrived = lax.all_to_all(outgoing, BOTH, split_axis=0, concat_axis=0, tiled=True)
-    arrived = arrived.reshape((devices * 2,) + old_cache.shape[1:])
+
+    tensor = lax.axis_size("tp")
+    serving = lax.axis_size("inst")
+    pairs = devices // 2
+    sides = [[i * tensor + t for i in range(side, serving, 2) for t in range(tensor)] for side in (0, 1)]
+    exchange = functools.partial(
+        lax.all_to_all, axis_name=BOTH, split_axis=0, concat_axis=0, tiled=True, axis_index_groups=sides
+    )
+    neighbour_cache = lax.ppermute(old_cache, "inst", [(i, i ^ 1) for i in range(serving)])
+    wanted, info, held = make_plan(plan_src, plan_page, lengths[:, :, 0], old_cache, pairs, tensor)
+    asked = exchange(wanted)
+    taken = take(held, neighbour_cache, asked)
+    arrived = exchange(taken.reshape((pairs, 4) + old_cache.shape[1:]))
+    arrived = arrived.reshape((pairs * 4,) + old_cache.shape[1:])
 
     rows = queries.reshape(steps, heads, groups, head).transpose(1, 2, 0, 3)
     rows = rows.reshape(heads, groups * steps, head)
     fresh = new_kv.reshape(steps, heads, width).transpose(1, 0, 2)
-    length = lax.dynamic_index_in_dim(lengths[0, :, 0], side, 0, keepdims=False)
-    info = jnp.concatenate([place[0], jnp.stack([1 - side, length]).astype(jnp.int32)])
     early = old_weight.shape[0] // 4
     passed, pages, first = attend_other(info, arrived, rows, fresh, old_weight, early)
     partner = flipped(passed, 1)

time: 163 us -> 153 us (0.939); the launches traced: 163 us -> 151 us
  waiting for transfers between devices: 109 us -> 5.95 us
  blocking collectives: 18.2 us -> 121 us
  starting transfers between devices: 18.1 us -> 6.38 us
    all_to_all x1 -> x0, waiting for transfers between devices: 104 us -> none  [on_device(): lax.all_to_all(outgoing, BOTH, split_axis=0, concat_axis=0, tiled=True)]
    all_to_all x1 -> x2, blocking collectives: 18.2 us -> 121 us  [the longest x1 102 us: on_device(): arrived = exchange(taken.reshape((pairs, 4) + old_cache.shape[1:]))]
    all_to_all x1 -> x0, starting transfers between devices: 7.16 us -> none  [on_device(): lax.all_to_all(outgoing, BOTH, split_axis=0, concat_axis=0, tiled=True)]
    ppermute x5, starting transfers between devices: 11 us -> 6.29 us  [flipped(): return lax.ppermute(value, 'tp', [(i, i ^ bits) for i in range(size)])]
    ppermute x5, waiting for transfers between devices: 4.2 us -> 5.95 us  [flipped(): return lax.ppermute(value, 'tp', [(i, i ^ bits) for i in range(size)])]
  transfers between devices with their start and end apart: 6 -> 6, of which waited for: 5 -> 5; matrix products, arithmetic and copies ran while one was open for 1% -> 0% of each run, Pallas kernels for 3% -> 5%
where the time goes in v7:
time: 153 us; the launch traced here: 151 us
  blocking collectives  121 us (79%)
  Pallas kernels  15.6 us (10%)
  starting transfers between devices  6.38 us (4%)
  waiting for transfers between devices  5.95 us (4%)
    all_to_all x1, blocking collectives, on_device(): arrived = exchange(taken.reshape((pairs, 4) + old_cache.shape[1:]))  102 us
    all_to_all x1, blocking collectives, on_device(): asked = exchange(wanted)  18.8 us
    ppermute x5, starting transfers between devices, flipped(): return lax.ppermute(value, 'tp', [(i, i ^ bits) for i in range(size)])  6.29 us
    ppermute x5, waiting for transfers between devices, flipped(): return lax.ppermute(value, 'tp', [(i, i ^ bits) for i in range(size)])  5.95 us
    pallas_call x1, Pallas kernels, attend_other(): pl.pallas_call(other_kernel, out_shape=(jax.ShapeDtypeStruct((rows, head)...  3.63 us
    pallas_call x1, Pallas kernels, attend_own(): pl.pallas_call(own_kernel, out_shape=(jax.ShapeDtypeStruct((rows, head),...  3.34 us
    pallas_call x1, Pallas kernels, take(): pl.pallas_call(take_kernel, out_shape=pltpu.HBM(shape, own.dtype), in_spe...  3.14 us
  transfers between devices with their start and end apart: 6, of which 5 were waited for; matrix products, arithmetic and copies ran while one was open for 0% of the time, Pallas kernels for 5%

profile of v7, /device:TPU:24, one launch (start us, length us, event | category | flops | bytes accessed | tf_op | source)
XLA Modules:
  0.0 150.5 jit_solution(6301213192090127152)
XLA Ops:
  0.6 0.1 collective-permute-start
  0.7 2.3 %make_plan.1 = (s32[64,4]{1,0:T(8,128)S(1)}, s32[1,256]{1,0:T(1,128)S(1)}, bf16[128,64,256]{2,1,0:T(8,128)(2,1)S(1)}) custom-call(s32[1,128]{1,0:T(1,128)} %src_hbm.1, s32[1,128]{1,0:T(1,128)} %page_hbm.1, s32[1,2]{1,0:T(1,128)} %bitcast.25, bf16[128,64,256]{2,1,0:T(8,128)(2,1)} %cache_ref.1), custom_call_target="tpu_custom_call" | custom-call | tf_op jit(solution)/shard_map/make_plan/pallas_call | solution.py:70
  3.0 18.8 %all_to_all.16 = s32[64,1,4]{2,1,0:T(1,128)S(1)} all-to-all(s32[64,1,4]{2,1,0:T(1,128)S(1)} %bitcast.20), channel_id=1, replica_groups={{0,1,2,3,4,5,6,7,16,17,18,19,20,21,22,23,32,33,34,35,36,37,38,39,48,49,..., dimensions={0} | all-to-all | bytes 2048 | tf_op jit(solution)/shard_map/all_to_all | solution.py:357
  21.7 0.0 collective-permute-done.other_ref
  21.8 3.1 %take_outgoing.1 = bf16[256,64,256]{2,1,0:T(8,128)(2,1)} custom-call(s32[64,4]{1,0:T(8,128)S(1)} %bitcast.17, bf16[128,64,256]{2,1,0:T(8,128)(2,1)S(1)} %get-tuple-element.14.own_ref, bf16[128,64,256]{2,1,0:T(8,128)(2,1)S(1)} %collective-permute-done.other_ref), custom_call_target="tpu_custom_call" | custom-call | bytes 8388608 | tf_op jit(solution)/shard_map/take_outgoing/pallas_call | solution.py:129
  24.9 0.0 copy-start
  24.9 0.0 copy-start.1
  24.9 102.4 %all_to_all.17 = bf16[64,4,64,256]{3,2,1,0:T(8,128)(2,1)} all-to-all(bf16[64,4,64,256]{3,2,1,0:T(8,128)(2,1)} %bitcast.24), channel_id=1, replica_groups={{0,1,2,3,4,5,6,7,16,17,18,19,20,21,22,23,32,33,34,35,36,37,38,39,48,49,..., dimensions={0} | all-to-all | bytes 16777216 | tf_op jit(solution)/shard_map/all_to_all | solution.py:359
  127.3 0.0 copy-done
  127.3 3.6 %attend_other.1 = (bf16[32,128]{1,0:T(8,128)(2,1)S(1)}, bf16[128,64,256]{2,1,0:T(8,128)(2,1)S(1)}, bf16[256,4096]{1,0:T(8,128)(2,1)S(1)}) custom-call(s32[1,256]{1,0:T(1,128)S(1)} %get-tuple-element.12.info_ref, bf16[256,64,256]{2,1,0:T(8,128)(2,1)} %bitcast.23, bf16[2,32,128]{2,1,0:T(8,128)(2,1)S(1)} %bitcast.18, bf16[2,4,256]{2,1,0:T(4,128)(2,1)S(1)} %bitcast.21, ...), custom_call_target="tpu_custom_call" | custom-call | flops 67108864 | bytes 4194304 | tf_op jit(solution)/shard_map/attend_other/pallas_call | solution.py:247
  130.9 0.1 collective-permute-start.1
  131.0 3.3 %attend_own.1 = (bf16[32,128]{1,0:T(8,128)(2,1)S(1)}, bf16[768,4096]{1,0:T(8,128)(2,1)S(1)}) custom-call(s32[1,256]{1,0:T(1,128)S(1)} %get-tuple-element.12.info_ref, bf16[128,64,256]{2,1,0:T(8,128)(2,1)S(1)} %get-tuple-element.15.pages_ref, bf16[2,32,128]{2,1,0:T(8,128)(2,1)S(1)} %bitcast.19, bf16[2,4,256]{2,1,0:T(4,128)(2,1)S(1)} %bitcast.22, ...), custom_call_target="tpu_custom_call" | custom-call | flops 67108864 | bytes 4194304 | tf_op jit(solution)/shard_map/attend_own/pallas_call | solution.py:265
  134.4 0.3 collective-permute-done.1.partner_ref
  134.7 1.2 project.1
  135.9 2.2 %collective-permute-start.4 = (bf16[4,4096]{1,0:T(4,128)(2,1)S(1)}, bf16[4,4096]{1,0:T(4,128)(2,1)S(1)}, u32[]{:S(2)}, u32[]{:S(2)}) collective-permute-start(bf16[4,4096]{1,0:T(4,128)(2,1)S(1)} %get-tuple-element.23), channel_id=1, source_target_pairs={{0,2},{1,3},{2,0},{3,1},{4,6},{5,7},{6,4},{7,5},{8,10},{9,11},{10,... | collective-permute-start | bytes 98312 | tf_op jit(solution)/shard_map/ppermute | solution.py:19
  138.1 2.3 %collective-permute-start.3 = (bf16[4,4096]{1,0:T(4,128)(2,1)S(1)}, bf16[4,4096]{1,0:T(4,128)(2,1)S(1)}, u32[]{:S(2)}, u32[]{:S(2)}) collective-permute-start(bf16[4,4096]{1,0:T(4,128)(2,1)S(1)} %get-tuple-element.22), channel_id=1, source_target_pairs={{0,3},{1,2},{2,1},{3,0},{4,7},{5,6},{6,5},{7,4},{8,11},{9,10},{10,... | collective-permute-start | bytes 98312 | tf_op jit(solution)/shard_map/ppermute | solution.py:19
  140.4 0.0 collective-permute-start.2
  140.4 1.0 collective-permute-done.4
  141.4 1.8 %collective-permute-done.3 = bf16[4,4096]{1,0:T(4,128)(2,1)S(1)} collective-permute-done((bf16[4,4096]{1,0:T(4,128)(2,1)S(1)}, bf16[4,4096]{1,0:T(4,128)(2,1)S(1)}, u32[]{:S(2)}, u32[]{:S(2)}) %collective-permute-start.3) | collective-permute-done | bytes 32800 | tf_op jit(solution)/shard_map/ppermute | solution.py:19
  143.2 1.1 collective-permute-done.2
  144.4 1.7 %collective-permute-start.5 = (bf16[4,4096]{1,0:T(4,128)(2,1)S(1)}, bf16[4,4096]{1,0:T(4,128)(2,1)S(1)}, u32[]{:S(2)}, u32[]{:S(2)}) collective-permute-start(bf16[4,4096]{1,0:T(4,128)(2,1)S(1)} %fusion.1), channel_id=1, source_target_pairs={{0,4},{1,5},{2,6},{3,7},{4,0},{5,1},{6,2},{7,3},{8,12},{9,13},{10,... | collective-permute-start | bytes 98312 | tf_op jit(solution)/shard_map/ppermute | solution.py:19
  146.1 2.0 %store_moved.1 = bf16[128,64,256]{2,1,0:T(8,128)(2,1)} custom-call(bf16[128,64,256]{2,1,0:T(8,128)(2,1)S(1)} %get-tuple-element.15.pages_ref, bf16[8,4096]{1,0:T(8,128)(2,1)S(1)} %get-tuple-element.21._), custom_call_target="tpu_custom_call" | custom-call | bytes 4194304 | tf_op jit(solution)/shard_map/store_moved/pallas_call | solution.py:287
  148.1 1.8 %collective-permute-done.5 = bf16[4,4096]{1,0:T(4,128)(2,1)S(1)} collective-permute-done((bf16[4,4096]{1,0:T(4,128)(2,1)S(1)}, bf16[4,4096]{1,0:T(4,128)(2,1)S(1)}, u32[]{:S(2)}, u32[]{:S(2)}) %collective-permute-start.5) | collective-permute-done | bytes 32800 | tf_op jit(solution)/shard_map/ppermute | solution.py:19
  149.9 0.7 fusion
  (3 shorter events, 0.1 us)
Async XLA Ops:
  0.6 21.1 %collective-permute-start = (bf16[128,64,256]{2,1,0:T(8,128)(2,1)}, bf16[128,64,256]{2,1,0:T(8,128)(2,1)S(1)}, u32[]{:S(2)}, u32[]{:S(2)}) collective-permute-start(bf16[128,64,256]{2,1,0:T(8,128)(2,1)} %cache_ref.1), channel_id=1, source_target_pairs={{0,8},{8,0},{16,24},{24,16},{32,40},{40,32},{48,56},{56,48},{64,72... | collective-permute-start | bytes 12582920 | tf_op jit(solution)/shard_map/ppermute | solution.py:355
  24.9 102.4 %copy-start = (bf16[1,4,2048]{2,1,0:T(4,128)(2,1)S(1)}, bf16[1,4,2048]{2,1,0:T(4,128)(2,1)}, u32[]{:S(2)}) copy-start(bf16[1,4,2048]{2,1,0:T(4,128)(2,1)} %param.12) | copy-start | bytes 49156
  24.9 102.4 %copy-start.1 = (bf16[1,4,512]{2,1,0:T(4,128)(2,1)S(1)}, bf16[1,4,512]{2,1,0:T(4,128)(2,1)}, u32[]{:S(2)}) copy-start(bf16[1,4,512]{2,1,0:T(4,128)(2,1)} %param.13) | copy-start | bytes 12292
  130.9 3.7 %collective-permute-start.1 = (bf16[32,128]{1,0:T(8,128)(2,1)S(1)}, bf16[32,128]{1,0:T(8,128)(2,1)S(1)}, u32[]{:S(2)}, u32[]{:S(2)}) collective-permute-start(bf16[32,128]{1,0:T(8,128)(2,1)S(1)} %get-tuple-element.17), channel_id=1, source_target_pairs={{0,1},{1,0},{2,3},{3,2},{4,5},{5,4},{6,7},{7,6},{8,9},{9,8},{10,11... | collective-permute-start | bytes 24584 | tf_op jit(solution)/shard_map/ppermute | solution.py:19
  135.9 5.5 %collective-permute-start.4 = (bf16[4,4096]{1,0:T(4,128)(2,1)S(1)}, bf16[4,4096]{1,0:T(4,128)(2,1)S(1)}, u32[]{:S(2)}, u32[]{:S(2)}) collective-permute-start(bf16[4,4096]{1,0:T(4,128)(2,1)S(1)} %get-tuple-element.23), channel_id=1, source_target_pairs={{0,2},{1,3},{2,0},{3,1},{4,6},{5,7},{6,4},{7,5},{8,10},{9,11},{10,... | collective-permute-start | bytes 98312 | tf_op jit(solution)/shard_map/ppermute | solution.py:19
  138.1 5.1 %collective-permute-start.3 = (bf16[4,4096]{1,0:T(4,128)(2,1)S(1)}, bf16[4,4096]{1,0:T(4,128)(2,1)S(1)}, u32[]{:S(2)}, u32[]{:S(2)}) collective-permute-start(bf16[4,4096]{1,0:T(4,128)(2,1)S(1)} %get-tuple-element.22), channel_id=1, source_target_pairs={{0,3},{1,2},{2,1},{3,0},{4,7},{5,6},{6,5},{7,4},{8,11},{9,10},{10,... | collective-permute-start | bytes 98312 | tf_op jit(solution)/shard_map/ppermute | solution.py:19
  140.4 3.9 %collective-permute-start.2 = (bf16[4,4096]{1,0:T(4,128)(2,1)S(1)}, bf16[4,4096]{1,0:T(4,128)(2,1)S(1)}, u32[]{:S(2)}, u32[]{:S(2)}) collective-permute-start(bf16[4,4096]{1,0:T(4,128)(2,1)S(1)} %get-tuple-element.22), channel_id=1, source_target_pairs={{0,1},{1,0},{2,3},{3,2},{4,5},{5,4},{6,7},{7,6},{8,9},{9,8},{10,11... | collective-permute-start | bytes 98312 | tf_op jit(solution)/shard_map/ppermute | solution.py:19
  144.4 5.5 %collective-permute-start.5 = (bf16[4,4096]{1,0:T(4,128)(2,1)S(1)}, bf16[4,4096]{1,0:T(4,128)(2,1)S(1)}, u32[]{:S(2)}, u32[]{:S(2)}) collective-permute-start(bf16[4,4096]{1,0:T(4,128)(2,1)S(1)} %fusion.1), channel_id=1, source_target_pairs={{0,4},{1,5},{2,6},{3,7},{4,0},{5,1},{6,2},{7,3},{8,12},{9,13},{10,... | collective-permute-start | bytes 98312 | tf_op jit(solution)/shard_map/ppermute | solution.py:19

commit v8 on v7

--- a/solution.py
+++ b/solution.py
@@ -187,8 +187,7 @@
     return (mixed / total).astype(jnp.bfloat16)
 
 
-def other_kernel(info_ref, arrived_ref, query_ref, fresh_ref, weight_ref, *rest):
-    out_ref, pages_ref, held_ref, sems, held_sem = rest
+def other_kernel(info_ref, arrived_ref, query_ref, fresh_ref, out_ref, pages_ref, sems):
     slots = pages_ref.shape[0]
     half = slots // 2
     parts = sems.shape[0] - 1
@@ -209,27 +208,17 @@
     for part in range(parts):
         gather(which * half + part * size, size, sems.at[part])
     gather((1 - which) * half, half, sems.at[parts])
-    hold = pltpu.make_async_copy(weight_ref.at[pl.ds(0, held_ref.shape[0])], held_ref, held_sem)
-    hold.start()
     ready = [
         functools.partial(wait, which * half + part * size, size, sems.at[part]) for part in range(parts)
     ]
     out_ref[...] = attention(which, length, query_ref, fresh_ref, pages_ref, ready)
     wait((1 - which) * half, half, sems.at[parts])
-    hold.wait()
-
-
-def own_kernel(info_ref, pages_ref, query_ref, fresh_ref, weight_ref, *rest):
-    out_ref, held_ref, held_sem = rest
+
+
+def own_kernel(info_ref, pages_ref, query_ref, fresh_ref, out_ref):
     slots = pages_ref.shape[0]
-    count = held_ref.shape[0]
-    hold = pltpu.make_async_copy(
-        weight_ref.at[pl.ds(weight_ref.shape[0] - count, count)], held_ref, held_sem
-    )
-    hold.start()
     which = 1 - info_ref[0, slots]
     out_ref[...] = attention(which, info_ref[0, slots + 1], query_ref, fresh_ref, pages_ref, [lambda: None])
-    hold.wait()
 
 
 def attend_cost(slots, rows, page, head):
@@ -240,7 +229,7 @@
     )
 
 
-def attend_other(info, arrived, queries, fresh, weight, count):
+def attend_other(info, arrived, queries, fresh):
     rows, head = queries.shape[1:]
     slots = info.shape[1] - 128
     page = arrived.shape[1]
@@ -249,32 +238,27 @@
         out_shape=(
             jax.ShapeDtypeStruct((rows, head), jnp.bfloat16),
             pltpu.VMEM((slots,) + arrived.shape[1:], arrived.dtype),
-            pltpu.VMEM((count, weight.shape[1]), weight.dtype),
-        ),
-        in_specs=[SMEM, HBM, VMEM, VMEM, HBM],
-        out_specs=(VMEM, VMEM, VMEM),
-        scratch_shapes=[pltpu.SemaphoreType.DMA((3,)), pltpu.SemaphoreType.DMA],
+        ),
+        in_specs=[SMEM, HBM, VMEM, VMEM],
+        out_specs=(VMEM, VMEM),
+        scratch_shapes=[pltpu.SemaphoreType.DMA((3,))],
         compiler_params=pltpu.CompilerParams(vmem_limit_bytes=LIMIT),
         cost_estimate=attend_cost(slots, rows, page, head),
         name="attend_other",
-    )(info, in_hbm(arrived), queries, fresh, in_hbm(weight))
-
-
-def attend_own(info, pages, queries, fresh, weight, count):
+    )(info, in_hbm(arrived), queries, fresh)
+
+
+def attend_own(info, pages, queries, fresh):
     rows, head = queries.shape[1:]
     return pl.pallas_call(
         own_kernel,
-        out_shape=(
-            jax.ShapeDtypeStruct((rows, head), jnp.bfloat16),
-            pltpu.VMEM((count, weight.shape[1]), weight.dtype),
-        ),
-        in_specs=[SMEM, VMEM, VMEM, VMEM, HBM],
-        out_specs=(VMEM, VMEM),
-        scratch_shapes=[pltpu.SemaphoreType.DMA],
+        out_shape=jax.ShapeDtypeStruct((rows, head), jnp.bfloat16),
+        in_specs=[SMEM, VMEM, VMEM, VMEM],
+        out_specs=VMEM,
         compiler_params=pltpu.CompilerParams(vmem_limit_bytes=LIMIT),
         cost_estimate=attend_cost(pages.shape[0], rows, pages.shape[1], head),
         name="attend_own",
-    )(info, in_vmem(pages), queries, fresh, in_hbm(weight))
+    )(info, in_vmem(pages), queries, fresh)
 
 
 def store_kernel(pages_ref, _, moved_ref, sem):
@@ -296,7 +280,7 @@
     )(in_vmem(pages), in_vmem(after))
 
 
-def project_kernel(kept_ref, partner_ref, first_ref, second_ref, sum_ref, sent_ref):
+def project_kernel(kept_ref, partner_ref, weight_ref, sum_ref, sent_ref):
     steps = sum_ref.shape[0] // 2
     rows = []
     for ref in (kept_ref, partner_ref):
@@ -306,35 +290,31 @@
         )
     both = jnp.concatenate(rows, axis=0).astype(jnp.bfloat16)
     tile = 1024
-    cut = first_ref.shape[0]
-    for at in range(0, first_ref.shape[1], tile):
-        product = jnp.dot(both[:, :cut], first_ref[:, at : at + tile], preferred_element_type=jnp.float32)
-        product = product + jnp.dot(
-            both[:, cut:], second_ref[:, at : at + tile], preferred_element_type=jnp.float32
-        )
+    for at in range(0, weight_ref.shape[1], tile):
+        product = jnp.dot(both, weight_ref[:, at : at + tile], preferred_element_type=jnp.float32)
         sum_ref[:, at : at + tile] = product
         turned = jnp.concatenate([product[steps:], product[:steps]], axis=0)
         sent_ref[:, at : at + tile] = turned.astype(jnp.bfloat16)
 
 
-def project(kept, partner, first, second, steps):
-    wide = first.shape[1]
+def project(kept, partner, weight, steps):
+    wide = weight.shape[1]
     return pl.pallas_call(
         project_kernel,
         out_shape=(
             jax.ShapeDtypeStruct((2 * steps, wide), jnp.float32),
             jax.ShapeDtypeStruct((2 * steps, wide), jnp.bfloat16),
         ),
-        in_specs=[VMEM, VMEM, VMEM, VMEM],
+        in_specs=[VMEM, VMEM, VMEM],
         out_specs=(VMEM, VMEM),
         compiler_params=pltpu.CompilerParams(vmem_limit_bytes=LIMIT),
         cost_estimate=pl.CostEstimate(
-            flops=4 * steps * (first.size + second.size),
-            bytes_accessed=2 * (first.size + second.size),
+            flops=4 * steps * weight.size,
+            bytes_accessed=2 * weight.size,
             transcendentals=0,
         ),
         name="project",
-    )(kept, partner, in_vmem(first), in_vmem(second))
+    )(kept, partner, in_vmem(weight))
 
 
 def on_device(old_cache, old_weight, plan_src, plan_page, lengths, queries, new_kv):
@@ -362,12 +342,11 @@
     rows = queries.reshape(steps, heads, groups, head).transpose(1, 2, 0, 3)
     rows = rows.reshape(heads, groups * steps, head)
     fresh = new_kv.reshape(steps, heads, width).transpose(1, 0, 2)
-    early = old_weight.shape[0] // 4
-    passed, pages, first = attend_other(info, arrived, rows, fresh, old_weight, early)
+    passed, pages = attend_other(info, arrived, rows, fresh)
     partner = flipped(passed, 1)
-    kept, second = attend_own(info, pages, rows, fresh, old_weight, old_weight.shape[0] - early)
-
-    total, sent = project(kept, partner, first, second, steps)
+    kept = attend_own(info, pages, rows, fresh)
+
+    total, sent = project(kept, partner, old_weight, steps)
     moved = store(pages, sent)
     mine = sent[steps:]
     theirs = sent[:steps]

time: 153 us -> 151 us (0.987)
  Pallas kernels: 15.6 us -> 12.8 us
    pallas_call x1, Pallas kernels: 3.34 us -> 1.39 us  [attend_own(): pl.pallas_call(own_kernel, out_shape=jax.ShapeDtypeStruct((rows, head), j...]
  transfers between devices with their start and end apart: 6 -> 6, of which waited for: 5 -> 5; matrix products, arithmetic and copies ran while one was open for 0% -> 0% of each run, Pallas kernels for 5% -> 4%
where the time goes in v8:
time: 151 us; the launch traced here: 148 us
  blocking collectives  121 us (80%)
  Pallas kernels  12.8 us (8%)
  starting transfers between devices  6.45 us (4%)
  waiting for transfers between devices  6.1 us (4%)
    all_to_all x1, blocking collectives, on_device(): arrived = exchange(taken.reshape((pairs, 4) + old_cache.shape[1:]))  103 us
    all_to_all x1, blocking collectives, on_device(): asked = exchange(wanted)  18.8 us
    ppermute x5, starting transfers between devices, flipped(): return lax.ppermute(value, 'tp', [(i, i ^ bits) for i in range(size)])  6.37 us
    ppermute x5, waiting for transfers between devices, flipped(): return lax.ppermute(value, 'tp', [(i, i ^ bits) for i in range(size)])  6.09 us
    pallas_call x1, Pallas kernels, take(): pl.pallas_call(take_kernel, out_shape=pltpu.HBM(shape, own.dtype), in_spe...  3.12 us
  transfers between devices with their start and end apart: 6, of which 5 were waited for; matrix products, arithmetic and copies ran while one was open for 0% of the time, Pallas kernels for 4%

profile of v8, /device:TPU:24, one launch (start us, length us, event | category | flops | bytes accessed | tf_op | source)
XLA Modules:
  0.0 148.3 jit_solution(11422803526410262272)
XLA Ops:
  0.6 0.1 collective-permute-start
  0.7 2.3 %make_plan.1 = (s32[64,4]{1,0:T(8,128)S(1)}, s32[1,256]{1,0:T(1,128)S(1)}, bf16[128,64,256]{2,1,0:T(8,128)(2,1)S(1)}) custom-call(s32[1,128]{1,0:T(1,128)} %src_hbm.1, s32[1,128]{1,0:T(1,128)} %page_hbm.1, s32[1,2]{1,0:T(1,128)} %bitcast.27, bf16[128,64,256]{2,1,0:T(8,128)(2,1)} %cache_ref.1), custom_call_target="tpu_custom_call" | custom-call | tf_op jit(solution)/shard_map/make_plan/pallas_call | solution.py:70
  3.0 18.8 %all_to_all.16 = s32[64,1,4]{2,1,0:T(1,128)S(1)} all-to-all(s32[64,1,4]{2,1,0:T(1,128)S(1)} %bitcast.22), channel_id=1, replica_groups={{0,1,2,3,4,5,6,7,16,17,18,19,20,21,22,23,32,33,34,35,36,37,38,39,48,49,..., dimensions={0} | all-to-all | bytes 2048 | tf_op jit(solution)/shard_map/all_to_all | solution.py:337
  21.7 0.0 collective-permute-done.other_ref
  21.8 3.1 %take_outgoing.1 = bf16[256,64,256]{2,1,0:T(8,128)(2,1)} custom-call(s32[64,4]{1,0:T(8,128)S(1)} %bitcast.19, bf16[128,64,256]{2,1,0:T(8,128)(2,1)S(1)} %get-tuple-element.11.own_ref, bf16[128,64,256]{2,1,0:T(8,128)(2,1)S(1)} %collective-permute-done.other_ref), custom_call_target="tpu_custom_call" | custom-call | bytes 8388608 | tf_op jit(solution)/shard_map/take_outgoing/pallas_call | solution.py:129
  24.9 0.0 copy-start
  24.9 0.0 copy-start.1
  24.9 0.0 slice-start.1
  24.9 102.7 %all_to_all.17 = bf16[64,4,64,256]{3,2,1,0:T(8,128)(2,1)} all-to-all(bf16[64,4,64,256]{3,2,1,0:T(8,128)(2,1)} %bitcast.26), channel_id=1, replica_groups={{0,1,2,3,4,5,6,7,16,17,18,19,20,21,22,23,32,33,34,35,36,37,38,39,48,49,..., dimensions={0} | all-to-all | bytes 16777216 | tf_op jit(solution)/shard_map/all_to_all | solution.py:339
  127.6 2.8 %attend_other.1 = (bf16[32,128]{1,0:T(8,128)(2,1)S(1)}, bf16[128,64,256]{2,1,0:T(8,128)(2,1)S(1)}) custom-call(s32[1,256]{1,0:T(1,128)S(1)} %get-tuple-element.9.info_ref, bf16[256,64,256]{2,1,0:T(8,128)(2,1)} %bitcast.25, bf16[2,32,128]{2,1,0:T(8,128)(2,1)S(1)} %bitcast.20, bf16[2,4,256]{2,1,0:T(4,128)(2,1)S(1)} %bitcast.23), custom_call_target="tpu_custom_call" | custom-call | flops 67108864 | bytes 4194304 | tf_op jit(solution)/shard_map/attend_other/pallas_call | solution.py:236
  130.4 0.1 collective-permute-start.1
  130.5 1.4 attend_own.1.kept_ref
  131.9 2.2 %collective-permute-done.1.partner_ref = bf16[32,128]{1,0:T(8,128)(2,1)S(1)} collective-permute-done((bf16[32,128]{1,0:T(8,128)(2,1)S(1)}, bf16[32,128]{1,0:T(8,128)(2,1)S(1)}, u32[]{:S(2)}, u32[]{:S(2)}) %collective-permute-start.1) | collective-permute-done | bytes 8224 | tf_op jit(solution)/shard_map/ppermute | solution.py:19
  134.2 1.2 project.1
  135.4 0.9 collective-permute-start.4
  136.3 1.8 %collective-permute-start.3 = (bf16[4,4096]{1,0:T(4,128)(2,1)S(1)}, bf16[4,4096]{1,0:T(4,128)(2,1)S(1)}, u32[]{:S(2)}, u32[]{:S(2)}) collective-permute-start(bf16[4,4096]{1,0:T(4,128)(2,1)S(1)} %get-tuple-element.16), channel_id=1, source_target_pairs={{0,3},{1,2},{2,1},{3,0},{4,7},{5,6},{6,5},{7,4},{8,11},{9,10},{10,... | collective-permute-start | bytes 98312 | tf_op jit(solution)/shard_map/ppermute | solution.py:19
  138.2 0.8 collective-permute-start.2
  139.0 1.9 %collective-permute-done.4 = bf16[4,4096]{1,0:T(4,128)(2,1)S(1)} collective-permute-done((bf16[4,4096]{1,0:T(4,128)(2,1)S(1)}, bf16[4,4096]{1,0:T(4,128)(2,1)S(1)}, u32[]{:S(2)}, u32[]{:S(2)}) %collective-permute-start.4) | collective-permute-done | bytes 32800 | tf_op jit(solution)/shard_map/ppermute | solution.py:19
  140.9 0.6 collective-permute-done.3
  141.4 0.6 collective-permute-done.2
  142.1 2.7 %collective-permute-start.5 = (bf16[4,4096]{1,0:T(4,128)(2,1)S(1)}, bf16[4,4096]{1,0:T(4,128)(2,1)S(1)}, u32[]{:S(2)}, u32[]{:S(2)}) collective-permute-start(bf16[4,4096]{1,0:T(4,128)(2,1)S(1)} %fusion.1), channel_id=1, source_target_pairs={{0,4},{1,5},{2,6},{3,7},{4,0},{5,1},{6,2},{7,3},{8,12},{9,13},{10,... | collective-permute-start | bytes 98312 | tf_op jit(solution)/shard_map/ppermute | solution.py:19
  144.8 2.0 %store_moved.1 = bf16[128,64,256]{2,1,0:T(8,128)(2,1)} custom-call(bf16[128,64,256]{2,1,0:T(8,128)(2,1)S(1)} %get-tuple-element.12.pages_ref, bf16[8,4096]{1,0:T(8,128)(2,1)S(1)} %get-tuple-element.15._), custom_call_target="tpu_custom_call" | custom-call | bytes 4194304 | tf_op jit(solution)/shard_map/store_moved/pallas_call | solution.py:271
  146.9 0.8 collective-permute-done.5
  147.6 0.7 fusion
  (8 shorter events, 0.1 us)
Async XLA Ops:
  0.6 21.1 %collective-permute-start = (bf16[128,64,256]{2,1,0:T(8,128)(2,1)}, bf16[128,64,256]{2,1,0:T(8,128)(2,1)S(1)}, u32[]{:S(2)}, u32[]{:S(2)}) collective-permute-start(bf16[128,64,256]{2,1,0:T(8,128)(2,1)} %cache_ref.1), channel_id=1, source_target_pairs={{0,8},{8,0},{16,24},{24,16},{32,40},{40,32},{48,56},{56,48},{64,72... | collective-permute-start | bytes 12582920 | tf_op jit(solution)/shard_map/ppermute | solution.py:335
  21.8 112.4 %slice-start = ((s8[8388608]{0:T(1024)(128)(4,1)}), s8[4194304]{0:T(1024)(128)(4,1)S(1)}, s32[]{:S(2)}) async-start(s8[8388608]{0:T(1024)(128)(4,1)} %bitcast.17), calls=%async_computation.2 | async-start | bytes 8388608
  24.9 102.8 %copy-start = (bf16[1,4,2048]{2,1,0:T(4,128)(2,1)S(1)}, bf16[1,4,2048]{2,1,0:T(4,128)(2,1)}, u32[]{:S(2)}) copy-start(bf16[1,4,2048]{2,1,0:T(4,128)(2,1)} %param.12) | copy-start | bytes 49156
  24.9 102.7 %copy-start.1 = (bf16[1,4,512]{2,1,0:T(4,128)(2,1)S(1)}, bf16[1,4,512]{2,1,0:T(4,128)(2,1)}, u32[]{:S(2)}) copy-start(bf16[1,4,512]{2,1,0:T(4,128)(2,1)} %param.13) | copy-start | bytes 12292
  24.9 109.2 %slice-start.1 = ((s8[8388608]{0:T(1024)(128)(4,1)}), s8[4194304]{0:T(1024)(128)(4,1)S(1)}, s32[]{:S(2)}) async-start(s8[8388608]{0:T(1024)(128)(4,1)} %bitcast.17), calls=%async_computation.3 | async-start | bytes 8388608
  130.4 3.7 %collective-permute-start.1 = (bf16[32,128]{1,0:T(8,128)(2,1)S(1)}, bf16[32,128]{1,0:T(8,128)(2,1)S(1)}, u32[]{:S(2)}, u32[]{:S(2)}) collective-permute-start(bf16[32,128]{1,0:T(8,128)(2,1)S(1)} %get-tuple-element.13), channel_id=1, source_target_pairs={{0,1},{1,0},{2,3},{3,2},{4,5},{5,4},{6,7},{7,6},{8,9},{9,8},{10,11... | collective-permute-start | bytes 24584 | tf_op jit(solution)/shard_map/ppermute | solution.py:19
  135.4 5.5 %collective-permute-start.4 = (bf16[4,4096]{1,0:T(4,128)(2,1)S(1)}, bf16[4,4096]{1,0:T(4,128)(2,1)S(1)}, u32[]{:S(2)}, u32[]{:S(2)}) collective-permute-start(bf16[4,4096]{1,0:T(4,128)(2,1)S(1)} %get-tuple-element.17), channel_id=1, source_target_pairs={{0,2},{1,3},{2,0},{3,1},{4,6},{5,7},{6,4},{7,5},{8,10},{9,11},{10,... | collective-permute-start | bytes 98312 | tf_op jit(solution)/shard_map/ppermute | solution.py:19
  136.3 5.1 %collective-permute-start.3 = (bf16[4,4096]{1,0:T(4,128)(2,1)S(1)}, bf16[4,4096]{1,0:T(4,128)(2,1)S(1)}, u32[]{:S(2)}, u32[]{:S(2)}) collective-permute-start(bf16[4,4096]{1,0:T(4,128)(2,1)S(1)} %get-tuple-element.16), channel_id=1, source_target_pairs={{0,3},{1,2},{2,1},{3,0},{4,7},{5,6},{6,5},{7,4},{8,11},{9,10},{10,... | collective-permute-start | bytes 98312 | tf_op jit(solution)/shard_map/ppermute | solution.py:19
  138.2 3.9 %collective-permute-start.2 = (bf16[4,4096]{1,0:T(4,128)(2,1)S(1)}, bf16[4,4096]{1,0:T(4,128)(2,1)S(1)}, u32[]{:S(2)}, u32[]{:S(2)}) collective-permute-start(bf16[4,4096]{1,0:T(4,128)(2,1)S(1)} %get-tuple-element.16), channel_id=1, source_target_pairs={{0,1},{1,0},{2,3},{3,2},{4,5},{5,4},{6,7},{7,6},{8,9},{9,8},{10,11... | collective-permute-start | bytes 98312 | tf_op jit(solution)/shard_map/ppermute | solution.py:19
  142.1 5.5 %collective-permute-start.5 = (bf16[4,4096]{1,0:T(4,128)(2,1)S(1)}, bf16[4,4096]{1,0:T(4,128)(2,1)S(1)}, u32[]{:S(2)}, u32[]{:S(2)}) collective-permute-start(bf16[4,4096]{1,0:T(4,128)(2,1)S(1)} %fusion.1), channel_id=1, source_target_pairs={{0,4},{1,5},{2,6},{3,7},{4,0},{5,1},{6,2},{7,3},{8,12},{9,13},{10,... | collective-permute-start | bytes 98312 | tf_op jit(solution)/shard_map/ppermute | solution.py:19

commit v9 on v8

--- a/solution.py
+++ b/solution.py
@@ -11,7 +11,7 @@
 HBM = pl.BlockSpec(memory_space=pltpu.HBM)
 VMEM = pl.BlockSpec(memory_space=pltpu.VMEM)
 SMEM = pl.BlockSpec(memory_space=pltpu.SMEM)
-LIMIT = 6 * 1024 * 1024
+LIMIT = 12 * 1024 * 1024
 
 
 def flipped(value, bits):
@@ -145,12 +145,19 @@
     )(at, in_vmem(own), in_vmem(other))
 
 
-def attention(which, length, query_ref, fresh_ref, pages_ref, ready):
-    slots, page, width = pages_ref.shape
+def attend_kernel(kept, info_ref, arrived_ref, query_ref, fresh_ref, out_ref, pages_ref):
+    half, page, width = pages_ref.shape
     head = width // 2
-    half = slots // 2
-    parts = len(ready)
-    size = half // parts
+    slots = 2 * half
+    which = info_ref[0, slots]
+    if kept:
+        which = 1 - which
+    length = info_ref[0, slots + 1]
+
+    @pl.loop(0, half, unroll=4)
+    def _(slot):
+        pages_ref[slot] = arrived_ref[info_ref[0, which * half + slot]]
+
     query = query_ref[which]
     fresh = fresh_ref[which]
     rows = query.shape[0]
@@ -163,121 +170,66 @@
     step_of = lax.broadcasted_iota(jnp.int32, (rows, steps), 0) % steps
     key_step = lax.broadcasted_iota(jnp.int32, (rows, steps), 1)
     fresh_scores = jnp.where(step_of >= key_step, fresh_scores, jnp.float32(-1e30))
-    highest = jnp.max(fresh_scores, axis=1, keepdims=True)
-    scores = []
-    for part in range(parts):
-        ready[part]()
-        keys = pages_ref[pl.ds(which * half + part * size, size), :, :head].reshape(size * page, head)
-        found = lax.dot_general(query, keys, contract_last, preferred_element_type=jnp.float32) * scale
-        position = lax.broadcasted_iota(jnp.int32, found.shape, 1) + part * size * page
-        found = jnp.where(position < length, found, jnp.float32(-1e30))
-        highest = jnp.maximum(highest, jnp.max(found, axis=1, keepdims=True))
-        scores.append(found)
+    keys = pages_ref[:, :, :head].reshape(half * page, head)
+    scores = lax.dot_general(query, keys, contract_last, preferred_element_type=jnp.float32) * scale
+    position = lax.broadcasted_iota(jnp.int32, scores.shape, 1)
+    scores = jnp.where(position < length, scores, jnp.float32(-1e30))
+    highest = jnp.maximum(
+        jnp.max(scores, axis=1, keepdims=True), jnp.max(fresh_scores, axis=1, keepdims=True)
+    )
     fresh_weights = jnp.exp(fresh_scores - highest)
-    total = jnp.sum(fresh_weights, axis=1, keepdims=True)
+    weights = jnp.exp(scores - highest)
+    total = jnp.sum(weights, axis=1, keepdims=True) + jnp.sum(fresh_weights, axis=1, keepdims=True)
+    values = pages_ref[:, :, head:].reshape(half * page, head)
+    mixed = jnp.dot(weights.astype(jnp.bfloat16), values, preferred_element_type=jnp.float32)
     fresh_values = fresh[:, head:].astype(jnp.float32)
-    mixed = jnp.zeros((rows, head), jnp.float32)
     for step in range(steps):
         mixed = mixed + fresh_weights[:, step : step + 1] * fresh_values[step : step + 1, :]
-    for part in range(parts):
-        weights = jnp.exp(scores[part] - highest)
-        total = total + jnp.sum(weights, axis=1, keepdims=True)
-        values = pages_ref[pl.ds(which * half + part * size, size), :, head:].reshape(size * page, head)
-        mixed = mixed + jnp.dot(weights.astype(jnp.bfloat16), values, preferred_element_type=jnp.float32)
-    return (mixed / total).astype(jnp.bfloat16)
-
-
-def other_kernel(info_ref, arrived_ref, query_ref, fresh_ref, out_ref, pages_ref, sems):
-    slots = pages_ref.shape[0]
-    half = slots // 2
-    parts = sems.shape[0] - 1
-    size = half // parts
-    which = info_ref[0, slots]
-    length = info_ref[0, slots + 1]
-
-    def gather(first, count, sem):
-        @pl.loop(0, count, unroll=8)
-        def _(at):
-            slot = first + at
-            pltpu.make_async_copy(arrived_ref.at[info_ref[0, slot]], pages_ref.at[slot], sem).start()
-
-    def wait(first, count, sem):
-        block = pages_ref.at[pl.ds(first, count)]
-        pltpu.make_async_copy(block, block, sem).wait()
-
-    for part in range(parts):
-        gather(which * half + part * size, size, sems.at[part])
-    gather((1 - which) * half, half, sems.at[parts])
-    ready = [
-        functools.partial(wait, which * half + part * size, size, sems.at[part]) for part in range(parts)
-    ]
-    out_ref[...] = attention(which, length, query_ref, fresh_ref, pages_ref, ready)
-    wait((1 - which) * half, half, sems.at[parts])
-
-
-def own_kernel(info_ref, pages_ref, query_ref, fresh_ref, out_ref):
-    slots = pages_ref.shape[0]
-    which = 1 - info_ref[0, slots]
-    out_ref[...] = attention(which, info_ref[0, slots + 1], query_ref, fresh_ref, pages_ref, [lambda: None])
-
-
-def attend_cost(slots, rows, page, head):
-    return pl.CostEstimate(
-        flops=2 * rows * slots * page * head,
-        bytes_accessed=4 * slots * page * head,
-        transcendentals=rows * slots * page // 2,
-    )
-
-
-def attend_other(info, arrived, queries, fresh):
+    out_ref[...] = (mixed / total).astype(jnp.bfloat16)
+
+
+def attend(kept, info, arrived, queries, fresh, name):
     rows, head = queries.shape[1:]
-    slots = info.shape[1] - 128
+    half = (info.shape[1] - 128) // 2
     page = arrived.shape[1]
     return pl.pallas_call(
-        other_kernel,
-        out_shape=(
-            jax.ShapeDtypeStruct((rows, head), jnp.bfloat16),
-            pltpu.VMEM((slots,) + arrived.shape[1:], arrived.dtype),
-        ),
-        in_specs=[SMEM, HBM, VMEM, VMEM],
-        out_specs=(VMEM, VMEM),
-        scratch_shapes=[pltpu.SemaphoreType.DMA((3,))],
-        compiler_params=pltpu.CompilerParams(vmem_limit_bytes=LIMIT),
-        cost_estimate=attend_cost(slots, rows, page, head),
-        name="attend_other",
-    )(info, in_hbm(arrived), queries, fresh)
-
-
-def attend_own(info, pages, queries, fresh):
-    rows, head = queries.shape[1:]
-    return pl.pallas_call(
-        own_kernel,
+        functools.partial(attend_kernel, kept),
         out_shape=jax.ShapeDtypeStruct((rows, head), jnp.bfloat16),
         in_specs=[SMEM, VMEM, VMEM, VMEM],
         out_specs=VMEM,
-        compiler_params=pltpu.CompilerParams(vmem_limit_bytes=LIMIT),
-        cost_estimate=attend_cost(pages.shape[0], rows, pages.shape[1], head),
-        name="attend_own",
-    )(info, in_vmem(pages), queries, fresh)
-
-
-def store_kernel(pages_ref, _, moved_ref, sem):
-    copy = pltpu.make_async_copy(pages_ref, moved_ref, sem)
-    copy.start()
-    copy.wait()
-
-
-def store(pages, after):
+        scratch_shapes=[pltpu.VMEM((half,) + arrived.shape[1:], arrived.dtype)],
+        compiler_params=pltpu.CompilerParams(vmem_limit_bytes=LIMIT),
+        cost_estimate=pl.CostEstimate(
+            flops=4 * rows * half * page * head,
+            bytes_accessed=4 * half * page * head,
+            transcendentals=rows * half * page,
+        ),
+        name=name,
+    )(info, in_vmem(arrived), queries, fresh)
+
+
+def store_kernel(info_ref, arrived_ref, _, moved_ref, sem):
+    @pl.loop(0, moved_ref.shape[0], unroll=4)
+    def _(slot):
+        pltpu.make_async_copy(arrived_ref.at[info_ref[0, slot]], moved_ref.at[slot], sem).start()
+
+    pltpu.make_async_copy(moved_ref, moved_ref, sem).wait()
+
+
+def store(info, arrived, after):
+    shape = (info.shape[1] - 128,) + arrived.shape[1:]
     return pl.pallas_call(
         store_kernel,
-        out_shape=pltpu.HBM(pages.shape, pages.dtype),
-        in_specs=[VMEM, VMEM],
+        out_shape=pltpu.HBM(shape, arrived.dtype),
+        in_specs=[SMEM, VMEM, VMEM],
         out_specs=HBM,
         scratch_shapes=[pltpu.SemaphoreType.DMA],
         compiler_params=pltpu.CompilerParams(vmem_limit_bytes=LIMIT),
-        cost_estimate=pl.CostEstimate(flops=0, bytes_accessed=2 * pages.size, transcendentals=0),
+        cost_estimate=pl.CostEstimate(
+            flops=0, bytes_accessed=2 * shape[0] * shape[1] * shape[2], transcendentals=0
+        ),
         name="store_moved",
-    )(in_vmem(pages), in_vmem(after))
+    )(info, in_vmem(arrived), in_vmem(after))
 
 
 def project_kernel(kept_ref, partner_ref, weight_ref, sum_ref, sent_ref):
@@ -342,12 +294,12 @@
     rows = queries.reshape(steps, heads, groups, head).transpose(1, 2, 0, 3)
     rows = rows.reshape(heads, groups * steps, head)
     fresh = new_kv.reshape(steps, heads, width).transpose(1, 0, 2)
-    passed, pages = attend_other(info, arrived, rows, fresh)
+    passed = attend(False, info, arrived, rows, fresh, "attend_other")
     partner = flipped(passed, 1)
-    kept = attend_own(info, pages, rows, fresh)
+    kept = attend(True, info, arrived, rows, fresh, "attend_own")
 
     total, sent = project(kept, partner, old_weight, steps)
-    moved = store(pages, sent)
+    moved = store(info, arrived, sent)
     mine = sent[steps:]
     theirs = sent[:steps]
     own = total[:steps]

time: 151 us -> 149 us (0.987)
  no operation moved by 1% of the time
where the time goes in v9:
time: 149 us; the launch traced here: 146 us
  blocking collectives  121 us (81%)
  Pallas kernels  12.4 us (8%)
  starting transfers between devices  6.16 us (4%)
  waiting for transfers between devices  5.7 us (4%)
    all_to_all x1, blocking collectives, on_device(): arrived = exchange(taken.reshape((pairs, 4) + old_cache.shape[1:]))  102 us
    all_to_all x1, blocking collectives, on_device(): asked = exchange(wanted)  18.8 us
    ppermute x5, starting transfers between devices, flipped(): return lax.ppermute(value, 'tp', [(i, i ^ bits) for i in range(size)])  6.07 us
    ppermute x5, waiting for transfers between devices, flipped(): return lax.ppermute(value, 'tp', [(i, i ^ bits) for i in range(size)])  5.7 us
    pallas_call x2, Pallas kernels, attend(): pl.pallas_call(functools.partial(attend_kernel, kept), out_shape=jax.Shap...  3.31 us
    pallas_call x1, Pallas kernels, take(): pl.pallas_call(take_kernel, out_shape=pltpu.HBM(shape, own.dtype), in_spe...  3.12 us
  transfers between devices with their start and end apart: 6, of which 5 were waited for; matrix products, arithmetic and copies ran while one was open for 0% of the time, Pallas kernels for 4%

profile of v9, /device:TPU:24, one launch (start us, length us, event | category | flops | bytes accessed | tf_op | source)
XLA Modules:
  0.0 146.3 jit_solution(978478526253142108)
XLA Ops:
  0.6 0.1 collective-permute-start
  0.7 2.3 %make_plan.1 = (s32[64,4]{1,0:T(8,128)S(1)}, s32[1,256]{1,0:T(1,128)S(1)}, bf16[128,64,256]{2,1,0:T(8,128)(2,1)S(1)}) custom-call(s32[1,128]{1,0:T(1,128)} %src_hbm.1, s32[1,128]{1,0:T(1,128)} %page_hbm.1, s32[1,2]{1,0:T(1,128)} %bitcast.29, bf16[128,64,256]{2,1,0:T(8,128)(2,1)} %cache_ref.1), custom_call_target="tpu_custom_call" | custom-call | tf_op jit(solution)/shard_map/make_plan/pallas_call | solution.py:70
  3.0 18.8 %all_to_all.16 = s32[64,1,4]{2,1,0:T(1,128)S(1)} all-to-all(s32[64,1,4]{2,1,0:T(1,128)S(1)} %bitcast.25), channel_id=1, replica_groups={{0,1,2,3,4,5,6,7,16,17,18,19,20,21,22,23,32,33,34,35,36,37,38,39,48,49,..., dimensions={0} | all-to-all | bytes 2048 | tf_op jit(solution)/shard_map/all_to_all | solution.py:289
  21.8 0.0 collective-permute-done.other_ref
  21.8 3.1 %take_outgoing.1 = bf16[256,64,256]{2,1,0:T(8,128)(2,1)} custom-call(s32[64,4]{1,0:T(8,128)S(1)} %bitcast.22, bf16[128,64,256]{2,1,0:T(8,128)(2,1)S(1)} %get-tuple-element.9.own_ref, bf16[128,64,256]{2,1,0:T(8,128)(2,1)S(1)} %collective-permute-done.other_ref), custom_call_target="tpu_custom_call" | custom-call | bytes 8388608 | tf_op jit(solution)/shard_map/take_outgoing/pallas_call | solution.py:129
  24.9 0.0 copy-start
  24.9 0.0 copy-start.1
  24.9 101.8 %all_to_all.17 = bf16[64,4,64,256]{3,2,1,0:T(8,128)(2,1)S(1)} all-to-all(bf16[64,4,64,256]{3,2,1,0:T(8,128)(2,1)} %bitcast.28), channel_id=1, replica_groups={{0,1,2,3,4,5,6,7,16,17,18,19,20,21,22,23,32,33,34,35,36,37,38,39,48,49,..., dimensions={0} | all-to-all | bytes 16777216 | tf_op jit(solution)/shard_map/all_to_all | solution.py:291
  126.7 1.7 %attend_other.1 = bf16[32,128]{1,0:T(8,128)(2,1)S(1)} custom-call(s32[1,256]{1,0:T(1,128)S(1)} %get-tuple-element.7.info_ref, bf16[256,64,256]{2,1,0:T(8,128)(2,1)S(1)} %bitcast.17, bf16[2,32,128]{2,1,0:T(8,128)(2,1)S(1)} %bitcast.23, bf16[2,4,256]{2,1,0:T(4,128)(2,1)S(1)} %bitcast.26), custom_call_target="tpu_custom_call" | custom-call | flops 67108864 | bytes 2097152 | tf_op jit(solution)/shard_map/attend_other/pallas_call | solution.py:195
  128.4 0.0 slice-start.1
  128.4 0.1 collective-permute-start.1
  128.5 1.6 %attend_own.1.kept_ref = bf16[32,128]{1,0:T(8,128)(2,1)S(1)} custom-call(s32[1,256]{1,0:T(1,128)S(1)} %get-tuple-element.7.info_ref, bf16[256,64,256]{2,1,0:T(8,128)(2,1)S(1)} %bitcast.18, bf16[2,32,128]{2,1,0:T(8,128)(2,1)S(1)} %bitcast.24, bf16[2,4,256]{2,1,0:T(4,128)(2,1)S(1)} %bitcast.27), custom_call_target="tpu_custom_call" | custom-call | flops 67108864 | bytes 2097152 | tf_op jit(solution)/shard_map/attend_own/pallas_call | solution.py:195
  130.1 2.1 %collective-permute-done.1.partner_ref = bf16[32,128]{1,0:T(8,128)(2,1)S(1)} collective-permute-done((bf16[32,128]{1,0:T(8,128)(2,1)S(1)}, bf16[32,128]{1,0:T(8,128)(2,1)S(1)}, u32[]{:S(2)}, u32[]{:S(2)}) %collective-permute-start.1) | collective-permute-done | bytes 8224 | tf_op jit(solution)/shard_map/ppermute | solution.py:19
  132.2 1.2 project.1
  133.4 0.8 collective-permute-start.4
  134.3 1.9 %collective-permute-start.3 = (bf16[4,4096]{1,0:T(4,128)(2,1)S(1)}, bf16[4,4096]{1,0:T(4,128)(2,1)S(1)}, u32[]{:S(2)}, u32[]{:S(2)}) collective-permute-start(bf16[4,4096]{1,0:T(4,128)(2,1)S(1)} %get-tuple-element.12), channel_id=1, source_target_pairs={{0,3},{1,2},{2,1},{3,0},{4,7},{5,6},{6,5},{7,4},{8,11},{9,10},{10,... | collective-permute-start | bytes 98312 | tf_op jit(solution)/shard_map/ppermute | solution.py:19
  136.2 0.8 collective-permute-start.2
  137.0 1.9 %collective-permute-done.4 = bf16[4,4096]{1,0:T(4,128)(2,1)S(1)} collective-permute-done((bf16[4,4096]{1,0:T(4,128)(2,1)S(1)}, bf16[4,4096]{1,0:T(4,128)(2,1)S(1)}, u32[]{:S(2)}, u32[]{:S(2)}) %collective-permute-start.4) | collective-permute-done | bytes 32800 | tf_op jit(solution)/shard_map/ppermute | solution.py:19
  138.9 0.4 collective-permute-done.3
  139.4 0.7 collective-permute-done.2
  140.1 2.4 %collective-permute-start.5 = (bf16[4,4096]{1,0:T(4,128)(2,1)S(1)}, bf16[4,4096]{1,0:T(4,128)(2,1)S(1)}, u32[]{:S(2)}, u32[]{:S(2)}) collective-permute-start(bf16[4,4096]{1,0:T(4,128)(2,1)S(1)} %fusion.1), channel_id=1, source_target_pairs={{0,4},{1,5},{2,6},{3,7},{4,0},{5,1},{6,2},{7,3},{8,12},{9,13},{10,... | collective-permute-start | bytes 98312 | tf_op jit(solution)/shard_map/ppermute | solution.py:19
  142.6 2.5 %store_moved.1 = bf16[128,64,256]{2,1,0:T(8,128)(2,1)} custom-call(s32[1,256]{1,0:T(1,128)S(1)} %get-tuple-element.7.info_ref, bf16[256,64,256]{2,1,0:T(8,128)(2,1)S(1)} %bitcast.19, bf16[8,4096]{1,0:T(8,128)(2,1)S(1)} %get-tuple-element.11._), custom_call_target="tpu_custom_call" | custom-call | bytes 4194304 | tf_op jit(solution)/shard_map/store_moved/pallas_call | solution.py:221
  145.1 0.6 collective-permute-done.5
  145.6 0.7 fusion
  (8 shorter events, 0.1 us)
Async XLA Ops:
  0.6 21.1 %collective-permute-start = (bf16[128,64,256]{2,1,0:T(8,128)(2,1)}, bf16[128,64,256]{2,1,0:T(8,128)(2,1)S(1)}, u32[]{:S(2)}, u32[]{:S(2)}) collective-permute-start(bf16[128,64,256]{2,1,0:T(8,128)(2,1)} %cache_ref.1), channel_id=1, source_target_pairs={{0,8},{8,0},{16,24},{24,16},{32,40},{40,32},{48,56},{56,48},{64,72... | collective-permute-start | bytes 12582920 | tf_op jit(solution)/shard_map/ppermute | solution.py:287
  24.9 101.8 %copy-start = (bf16[1,4,2048]{2,1,0:T(4,128)(2,1)S(1)}, bf16[1,4,2048]{2,1,0:T(4,128)(2,1)}, u32[]{:S(2)}) copy-start(bf16[1,4,2048]{2,1,0:T(4,128)(2,1)} %param.12) | copy-start | bytes 49156
  24.9 101.8 %copy-start.1 = (bf16[1,4,512]{2,1,0:T(4,128)(2,1)S(1)}, bf16[1,4,512]{2,1,0:T(4,128)(2,1)}, u32[]{:S(2)}) copy-start(bf16[1,4,512]{2,1,0:T(4,128)(2,1)} %param.13) | copy-start | bytes 12292
  126.7 5.5 %slice-start = ((s8[8388608]{0:T(1024)(128)(4,1)}), s8[4194304]{0:T(1024)(128)(4,1)S(1)}, s32[]{:S(2)}) async-start(s8[8388608]{0:T(1024)(128)(4,1)} %bitcast.20), calls=%async_computation.2 | async-start | bytes 8388608
  128.4 3.8 %slice-start.1 = ((s8[8388608]{0:T(1024)(128)(4,1)}), s8[4194304]{0:T(1024)(128)(4,1)S(1)}, s32[]{:S(2)}) async-start(s8[8388608]{0:T(1024)(128)(4,1)} %bitcast.20), calls=%async_computation.3 | async-start | bytes 8388608
  128.4 3.8 %collective-permute-start.1 = (bf16[32,128]{1,0:T(8,128)(2,1)S(1)}, bf16[32,128]{1,0:T(8,128)(2,1)S(1)}, u32[]{:S(2)}, u32[]{:S(2)}) collective-permute-start(bf16[32,128]{1,0:T(8,128)(2,1)S(1)} %attend_other.1), channel_id=1, source_target_pairs={{0,1},{1,0},{2,3},{3,2},{4,5},{5,4},{6,7},{7,6},{8,9},{9,8},{10,11... | collective-permute-start | bytes 24584 | tf_op jit(solution)/shard_map/ppermute | solution.py:19
  133.4 5.5 %collective-permute-start.4 = (bf16[4,4096]{1,0:T(4,128)(2,1)S(1)}, bf16[4,4096]{1,0:T(4,128)(2,1)S(1)}, u32[]{:S(2)}, u32[]{:S(2)}) collective-permute-start(bf16[4,4096]{1,0:T(4,128)(2,1)S(1)} %get-tuple-element.13), channel_id=1, source_target_pairs={{0,2},{1,3},{2,0},{3,1},{4,6},{5,7},{6,4},{7,5},{8,10},{9,11},{10,... | collective-permute-start | bytes 98312 | tf_op jit(solution)/shard_map/ppermute | solution.py:19
  134.3 5.1 %collective-permute-start.3 = (bf16[4,4096]{1,0:T(4,128)(2,1)S(1)}, bf16[4,4096]{1,0:T(4,128)(2,1)S(1)}, u32[]{:S(2)}, u32[]{:S(2)}) collective-permute-start(bf16[4,4096]{1,0:T(4,128)(2,1)S(1)} %get-tuple-element.12), channel_id=1, source_target_pairs={{0,3},{1,2},{2,1},{3,0},{4,7},{5,6},{6,5},{7,4},{8,11},{9,10},{10,... | collective-permute-start | bytes 98312 | tf_op jit(solution)/shard_map/ppermute | solution.py:19
  136.2 3.9 %collective-permute-start.2 = (bf16[4,4096]{1,0:T(4,128)(2,1)S(1)}, bf16[4,4096]{1,0:T(4,128)(2,1)S(1)}, u32[]{:S(2)}, u32[]{:S(2)}) collective-permute-start(bf16[4,4096]{1,0:T(4,128)(2,1)S(1)} %get-tuple-element.12), channel_id=1, source_target_pairs={{0,1},{1,0},{2,3},{3,2},{4,5},{5,4},{6,7},{7,6},{8,9},{9,8},{10,11... | collective-permute-start | bytes 98312 | tf_op jit(solution)/shard_map/ppermute | solution.py:19
  140.1 5.5 %collective-permute-start.5 = (bf16[4,4096]{1,0:T(4,128)(2,1)S(1)}, bf16[4,4096]{1,0:T(4,128)(2,1)S(1)}, u32[]{:S(2)}, u32[]{:S(2)}) collective-permute-start(bf16[4,4096]{1,0:T(4,128)(2,1)S(1)} %fusion.1), channel_id=1, source_target_pairs={{0,4},{1,5},{2,6},{3,7},{4,0},{5,1},{6,2},{7,3},{8,12},{9,13},{10,... | collective-permute-start | bytes 98312 | tf_op jit(solution)/shard_map/ppermute | solution.py:19

commit v10 on v9

--- a/solution.py
+++ b/solution.py
@@ -87,7 +87,7 @@
     )(in_hbm(plan_src), in_hbm(plan_page), in_hbm(lengths), in_hbm(pages))
 
 
-def take_kernel(asked_ref, own_ref, other_ref, to_ref, turned_ref, at_ref, sem, at_sem):
+def take_kernel(asked_ref, own_ref, other_ref, to_ref, turned_ref, at_ref, at_sem):
     count, columns = asked_ref.shape
     pages = own_ref.shape[0]
     shape = (count, turned_ref.shape[1])
@@ -100,26 +100,12 @@
     scalars.start()
     scalars.wait()
 
-    @pl.loop(0, count, init_carry=jnp.int32(0), unroll=2)
-    def started(row, total):
+    @pl.loop(0, count, unroll=2)
+    def _(row):
         for column in range(columns):
             page = at_ref[column, row]
-            to = to_ref.at[row * columns + column]
-
-            @pl.when((page >= 0) & (page < pages))
-            def _():
-                pltpu.make_async_copy(own_ref.at[page], to, sem).start()
-
-            @pl.when(page >= pages)
-            def _():
-                pltpu.make_async_copy(other_ref.at[page - pages], to, sem).start()
-
-            total = total + (page >= 0).astype(jnp.int32)
-        return total
-
-    @pl.loop(0, started)
-    def _(_):
-        pltpu.make_async_copy(own_ref.at[0], to_ref.at[0], sem).wait()
+            within = jnp.maximum(page, 0) & (pages - 1)
+            to_ref[row * columns + column] = jnp.where(page >= pages, other_ref[within], own_ref[within])
 
 
 def take(own, other, at):
@@ -128,13 +114,12 @@
     turned = (at.shape[1], -(-at.shape[0] // 128) * 128)
     return pl.pallas_call(
         take_kernel,
-        out_shape=pltpu.HBM(shape, own.dtype),
+        out_shape=pltpu.VMEM(shape, own.dtype),
         in_specs=[VMEM, VMEM, VMEM],
-        out_specs=HBM,
+        out_specs=VMEM,
         scratch_shapes=[
             pltpu.VMEM(turned, jnp.int32),
             pltpu.SMEM(turned, jnp.int32),
-            pltpu.SemaphoreType.DMA,
             pltpu.SemaphoreType.DMA,
         ],
         compiler_params=pltpu.CompilerParams(vmem_limit_bytes=LIMIT),

time: 149 us -> 147 us (0.987)
  no operation moved by 1% of the time
where the time goes in v10:
time: 147 us; the launch traced here: 145 us
  blocking collectives  120 us (82%)
  Pallas kernels  11.1 us (8%)
  starting transfers between devices  6.11 us (4%)
  waiting for transfers between devices  5.76 us (4%)
    all_to_all x1, blocking collectives, on_device(): arrived = exchange(taken.reshape((pairs, 4) + old_cache.shape[1:]))  101 us
    all_to_all x1, blocking collectives, on_device(): asked = exchange(wanted)  18.8 us
    ppermute x5, starting transfers between devices, flipped(): return lax.ppermute(value, 'tp', [(i, i ^ bits) for i in range(size)])  6.03 us
    ppermute x5, waiting for transfers between devices, flipped(): return lax.ppermute(value, 'tp', [(i, i ^ bits) for i in range(size)])  5.75 us
    pallas_call x2, Pallas kernels, attend(): pl.pallas_call(functools.partial(attend_kernel, kept), out_shape=jax.Shap...  3.3 us
  transfers between devices with their start and end apart: 6, of which 5 were waited for; matrix products, arithmetic and copies ran while one was open for 0% of the time, Pallas kernels for 4%

profile of v10, /device:TPU:24, one launch (start us, length us, event | category | flops | bytes accessed | tf_op | source)
XLA Modules:
  0.0 144.5 jit_solution(16552487503366813376)
XLA Ops:
  0.6 0.1 collective-permute-start
  0.7 2.3 %make_plan.1 = (s32[64,4]{1,0:T(8,128)S(1)}, s32[1,256]{1,0:T(1,128)S(1)}, bf16[128,64,256]{2,1,0:T(8,128)(2,1)S(1)}) custom-call(s32[1,128]{1,0:T(1,128)} %src_hbm.1, s32[1,128]{1,0:T(1,128)} %page_hbm.1, s32[1,2]{1,0:T(1,128)} %bitcast.29, bf16[128,64,256]{2,1,0:T(8,128)(2,1)} %cache_ref.1), custom_call_target="tpu_custom_call" | custom-call | tf_op jit(solution)/shard_map/make_plan/pallas_call | solution.py:70
  3.0 18.8 %all_to_all.16 = s32[64,1,4]{2,1,0:T(1,128)S(1)} all-to-all(s32[64,1,4]{2,1,0:T(1,128)S(1)} %bitcast.26), channel_id=1, replica_groups={{0,1,2,3,4,5,6,7,16,17,18,19,20,21,22,23,32,33,34,35,36,37,38,39,48,49,..., dimensions={0} | all-to-all | bytes 2048 | tf_op jit(solution)/shard_map/all_to_all | solution.py:274
  21.8 0.0 collective-permute-done.other_ref
  21.8 1.8 %take_outgoing.1 = bf16[256,64,256]{2,1,0:T(8,128)(2,1)S(1)} custom-call(s32[64,4]{1,0:T(8,128)S(1)} %bitcast.23, bf16[128,64,256]{2,1,0:T(8,128)(2,1)S(1)} %get-tuple-element.9.own_ref, bf16[128,64,256]{2,1,0:T(8,128)(2,1)S(1)} %collective-permute-done.other_ref), custom_call_target="tpu_custom_call" | custom-call | bytes 8388608 | tf_op jit(solution)/shard_map/take_outgoing/pallas_call | solution.py:115
  23.6 0.0 copy-start
  23.6 0.0 copy-start.1
  23.6 101.3 %all_to_all.17 = bf16[64,4,64,256]{3,2,1,0:T(8,128)(2,1)S(1)} all-to-all(bf16[64,4,64,256]{3,2,1,0:T(8,128)(2,1)S(1)} %bitcast.20), channel_id=1, replica_groups={{0,1,2,3,4,5,6,7,16,17,18,19,20,21,22,23,32,33,34,35,36,37,38,39,48,49,..., dimensions={0} | all-to-all | bytes 16777216 | tf_op jit(solution)/shard_map/all_to_all | solution.py:276
  124.9 1.7 %attend_other.1 = bf16[32,128]{1,0:T(8,128)(2,1)S(1)} custom-call(s32[1,256]{1,0:T(1,128)S(1)} %get-tuple-element.7.info_ref, bf16[256,64,256]{2,1,0:T(8,128)(2,1)S(1)} %bitcast.17, bf16[2,32,128]{2,1,0:T(8,128)(2,1)S(1)} %bitcast.24, bf16[2,4,256]{2,1,0:T(4,128)(2,1)S(1)} %bitcast.27), custom_call_target="tpu_custom_call" | custom-call | flops 67108864 | bytes 2097152 | tf_op jit(solution)/shard_map/attend_other/pallas_call | solution.py:180
  126.6 0.0 slice-start.1
  126.6 0.1 collective-permute-start.1
  126.7 1.6 %attend_own.1.kept_ref = bf16[32,128]{1,0:T(8,128)(2,1)S(1)} custom-call(s32[1,256]{1,0:T(1,128)S(1)} %get-tuple-element.7.info_ref, bf16[256,64,256]{2,1,0:T(8,128)(2,1)S(1)} %bitcast.18, bf16[2,32,128]{2,1,0:T(8,128)(2,1)S(1)} %bitcast.25, bf16[2,4,256]{2,1,0:T(4,128)(2,1)S(1)} %bitcast.28), custom_call_target="tpu_custom_call" | custom-call | flops 67108864 | bytes 2097152 | tf_op jit(solution)/shard_map/attend_own/pallas_call | solution.py:180
  128.4 2.0 %collective-permute-done.1.partner_ref = bf16[32,128]{1,0:T(8,128)(2,1)S(1)} collective-permute-done((bf16[32,128]{1,0:T(8,128)(2,1)S(1)}, bf16[32,128]{1,0:T(8,128)(2,1)S(1)}, u32[]{:S(2)}, u32[]{:S(2)}) %collective-permute-start.1) | collective-permute-done | bytes 8224 | tf_op jit(solution)/shard_map/ppermute | solution.py:19
  130.4 1.2 project.1
  131.7 0.9 collective-permute-start.4
  132.6 1.8 %collective-permute-start.3 = (bf16[4,4096]{1,0:T(4,128)(2,1)S(1)}, bf16[4,4096]{1,0:T(4,128)(2,1)S(1)}, u32[]{:S(2)}, u32[]{:S(2)}) collective-permute-start(bf16[4,4096]{1,0:T(4,128)(2,1)S(1)} %get-tuple-element.12), channel_id=1, source_target_pairs={{0,3},{1,2},{2,1},{3,0},{4,7},{5,6},{6,5},{7,4},{8,11},{9,10},{10,... | collective-permute-start | bytes 98312 | tf_op jit(solution)/shard_map/ppermute | solution.py:19
  134.4 0.8 collective-permute-start.2
  135.3 1.9 %collective-permute-done.4 = bf16[4,4096]{1,0:T(4,128)(2,1)S(1)} collective-permute-done((bf16[4,4096]{1,0:T(4,128)(2,1)S(1)}, bf16[4,4096]{1,0:T(4,128)(2,1)S(1)}, u32[]{:S(2)}, u32[]{:S(2)}) %collective-permute-start.4) | collective-permute-done | bytes 32800 | tf_op jit(solution)/shard_map/ppermute | solution.py:19
  137.2 0.5 collective-permute-done.3
  137.7 0.6 collective-permute-done.2
  138.4 2.3 %collective-permute-start.5 = (bf16[4,4096]{1,0:T(4,128)(2,1)S(1)}, bf16[4,4096]{1,0:T(4,128)(2,1)S(1)}, u32[]{:S(2)}, u32[]{:S(2)}) collective-permute-start(bf16[4,4096]{1,0:T(4,128)(2,1)S(1)} %fusion.1), channel_id=1, source_target_pairs={{0,4},{1,5},{2,6},{3,7},{4,0},{5,1},{6,2},{7,3},{8,12},{9,13},{10,... | collective-permute-start | bytes 98312 | tf_op jit(solution)/shard_map/ppermute | solution.py:19
  140.7 2.5 %store_moved.1 = bf16[128,64,256]{2,1,0:T(8,128)(2,1)} custom-call(s32[1,256]{1,0:T(1,128)S(1)} %get-tuple-element.7.info_ref, bf16[256,64,256]{2,1,0:T(8,128)(2,1)S(1)} %bitcast.19, bf16[8,4096]{1,0:T(8,128)(2,1)S(1)} %get-tuple-element.11._), custom_call_target="tpu_custom_call" | custom-call | bytes 4194304 | tf_op jit(solution)/shard_map/store_moved/pallas_call | solution.py:206
  143.2 0.6 collective-permute-done.5
  143.9 0.7 fusion
  (8 shorter events, 0.1 us)
Async XLA Ops:
  0.6 21.1 %collective-permute-start = (bf16[128,64,256]{2,1,0:T(8,128)(2,1)}, bf16[128,64,256]{2,1,0:T(8,128)(2,1)S(1)}, u32[]{:S(2)}, u32[]{:S(2)}) collective-permute-start(bf16[128,64,256]{2,1,0:T(8,128)(2,1)} %cache_ref.1), channel_id=1, source_target_pairs={{0,8},{8,0},{16,24},{24,16},{32,40},{40,32},{48,56},{56,48},{64,72... | collective-permute-start | bytes 12582920 | tf_op jit(solution)/shard_map/ppermute | solution.py:272
  23.6 101.3 %copy-start = (bf16[1,4,2048]{2,1,0:T(4,128)(2,1)S(1)}, bf16[1,4,2048]{2,1,0:T(4,128)(2,1)}, u32[]{:S(2)}) copy-start(bf16[1,4,2048]{2,1,0:T(4,128)(2,1)} %param.12) | copy-start | bytes 49156
  23.6 101.3 %copy-start.1 = (bf16[1,4,512]{2,1,0:T(4,128)(2,1)S(1)}, bf16[1,4,512]{2,1,0:T(4,128)(2,1)}, u32[]{:S(2)}) copy-start(bf16[1,4,512]{2,1,0:T(4,128)(2,1)} %param.13) | copy-start | bytes 12292
  124.9 5.5 %slice-start = ((s8[8388608]{0:T(1024)(128)(4,1)}), s8[4194304]{0:T(1024)(128)(4,1)S(1)}, s32[]{:S(2)}) async-start(s8[8388608]{0:T(1024)(128)(4,1)} %bitcast.21), calls=%async_computation.2 | async-start | bytes 8388608
  126.6 3.8 %slice-start.1 = ((s8[8388608]{0:T(1024)(128)(4,1)}), s8[4194304]{0:T(1024)(128)(4,1)S(1)}, s32[]{:S(2)}) async-start(s8[8388608]{0:T(1024)(128)(4,1)} %bitcast.21), calls=%async_computation.3 | async-start | bytes 8388608
  126.6 3.8 %collective-permute-start.1 = (bf16[32,128]{1,0:T(8,128)(2,1)S(1)}, bf16[32,128]{1,0:T(8,128)(2,1)S(1)}, u32[]{:S(2)}, u32[]{:S(2)}) collective-permute-start(bf16[32,128]{1,0:T(8,128)(2,1)S(1)} %attend_other.1), channel_id=1, source_target_pairs={{0,1},{1,0},{2,3},{3,2},{4,5},{5,4},{6,7},{7,6},{8,9},{9,8},{10,11... | collective-permute-start | bytes 24584 | tf_op jit(solution)/shard_map/ppermute | solution.py:19
  131.7 5.5 %collective-permute-start.4 = (bf16[4,4096]{1,0:T(4,128)(2,1)S(1)}, bf16[4,4096]{1,0:T(4,128)(2,1)S(1)}, u32[]{:S(2)}, u32[]{:S(2)}) collective-permute-start(bf16[4,4096]{1,0:T(4,128)(2,1)S(1)} %get-tuple-element.13), channel_id=1, source_target_pairs={{0,2},{1,3},{2,0},{3,1},{4,6},{5,7},{6,4},{7,5},{8,10},{9,11},{10,... | collective-permute-start | bytes 98312 | tf_op jit(solution)/shard_map/ppermute | solution.py:19
  132.6 5.1 %collective-permute-start.3 = (bf16[4,4096]{1,0:T(4,128)(2,1)S(1)}, bf16[4,4096]{1,0:T(4,128)(2,1)S(1)}, u32[]{:S(2)}, u32[]{:S(2)}) collective-permute-start(bf16[4,4096]{1,0:T(4,128)(2,1)S(1)} %get-tuple-element.12), channel_id=1, source_target_pairs={{0,3},{1,2},{2,1},{3,0},{4,7},{5,6},{6,5},{7,4},{8,11},{9,10},{10,... | collective-permute-start | bytes 98312 | tf_op jit(solution)/shard_map/ppermute | solution.py:19
  134.4 3.9 %collective-permute-start.2 = (bf16[4,4096]{1,0:T(4,128)(2,1)S(1)}, bf16[4,4096]{1,0:T(4,128)(2,1)S(1)}, u32[]{:S(2)}, u32[]{:S(2)}) collective-permute-start(bf16[4,4096]{1,0:T(4,128)(2,1)S(1)} %get-tuple-element.12), channel_id=1, source_target_pairs={{0,1},{1,0},{2,3},{3,2},{4,5},{5,4},{6,7},{7,6},{8,9},{9,8},{10,11... | collective-permute-start | bytes 98312 | tf_op jit(solution)/shard_map/ppermute | solution.py:19
  138.4 5.5 %collective-permute-start.5 = (bf16[4,4096]{1,0:T(4,128)(2,1)S(1)}, bf16[4,4096]{1,0:T(4,128)(2,1)S(1)}, u32[]{:S(2)}, u32[]{:S(2)}) collective-permute-start(bf16[4,4096]{1,0:T(4,128)(2,1)S(1)} %fusion.1), channel_id=1, source_target_pairs={{0,4},{1,5},{2,6},{3,7},{4,0},{5,1},{6,2},{7,3},{8,12},{9,13},{10,... | collective-permute-start | bytes 98312 | tf_op jit(solution)/shard_map/ppermute | solution.py:19
